TPU v7x, 32 devices: a whole 2x2x4 slice. The times are simulated.
32 devices in a mesh: dp: 4 (over y, x), fsdp: 4 (over z), tensor: 2 (over core).
Axes of the slice: x: 2, y: 2, z: 4, core: 2. Of those that a mesh axis runs over, the one named last changes fastest.
Arguments:
- momentum: bfloat16 [4, 8192, 8192], P('dp', 'fsdp', 'tensor'), may hold values from -24 to 24
- gradient: bfloat16 [4, 8192, 8192], P('dp', 'fsdp', 'tensor'), may hold values from -4 to 4
- factor: float32 [8192, 256], P('tensor'), may hold values from -6 to 6
Outputs:
- new_momentum: float32 [4, 8192, 8192], P('dp', 'fsdp', 'tensor')
- step_direction: bfloat16 [8192, 8192], P('fsdp', 'tensor')
- new_factor: float32 [8192, 256], P('tensor')
All inputs are finite; a program needn't handle non-finite values.
Results may differ from a plain program's by a relative error of at most 0.0065.
Values may be sent and summed in bfloat16 or wider, within the bound.
No kernel may reach another device: no remote copies, remote signals or barrier semaphores. Data moves between devices by JAX's collectives and lax.ppermute only.
A program may use at most 192 MiB of HBM per device.

v0:
```python
import jax
import jax.numpy as jnp
from jax import lax
from jax.sharding import PartitionSpec as P

ROWS = 8192
COLS = 8192
RANK = 256


def orthonormal(rows_part, gram):
    lower = jnp.linalg.cholesky(gram)
    return jax.scipy.linalg.solve_triangular(lower, rows_part.T, lower=True).T


def transposed_product(block, ortho_low):
    return lax.dot_general(
        block, ortho_low, (((0,), (0,)), ((), ())), preferred_element_type=jnp.float32
    )


def local(momentum, gradient, factor):
    highest = lax.Precision.HIGHEST
    replicas = lax.axis_size("dp")
    moment = momentum[0]
    change = gradient[0]
    factor_low = factor.astype(jnp.bfloat16)
    partial_left = jnp.dot(moment, factor_low, preferred_element_type=jnp.float32)
    partial_left = partial_left + jnp.dot(change, factor_low, preferred_element_type=jnp.float32)
    left = lax.psum(partial_left, ("dp", "tensor")) / replicas
    gram = lax.psum(jnp.dot(left.T, left, precision=highest), "fsdp")
    ortho_low = orthonormal(left, gram).astype(jnp.bfloat16)
    partial_right = transposed_product(moment, ortho_low) + transposed_product(change, ortho_low)
    right = lax.psum(partial_right, ("dp", "fsdp")) / replicas
    square_sums = lax.psum(jnp.sum(right * right, axis=0), "tensor")
    new_factor = right / jnp.sqrt(square_sums / COLS + 1e-06)
    right_low = right.astype(jnp.bfloat16)
    feedback = jnp.dot(ortho_low, right_low.T, preferred_element_type=jnp.float32)
    new_momentum = (moment.astype(jnp.float32) + change.astype(jnp.float32) - 0.05 * feedback)[None]
    step_scale = jnp.sqrt(jnp.float32(ROWS / RANK))
    factor_next_low = new_factor.astype(jnp.bfloat16)
    step_direction = (
        step_scale * jnp.dot(ortho_low, factor_next_low.T, preferred_element_type=jnp.float32)
    ).astype(jnp.bfloat16)
    return (new_momentum, step_direction, new_factor)


def solution(mesh):
    in_specs = (P("dp", "fsdp", "tensor"), P("dp", "fsdp", "tensor"), P("tensor", None))
    out_specs = (P("dp", "fsdp", "tensor"), P("fsdp", "tensor"), P("tensor", None))
    return jax.shard_map(local, mesh=mesh, in_specs=in_specs, out_specs=out_specs, check_vma=False)
```

profile of v0, /device:TPU:1, one launch (start us, length us, event | category | flops | bytes accessed | tf_op | source)
XLA Modules:
  0.0 440.9 jit_solution(3974662505523653435)
XLA Ops:
  7.2 9.5 %fusion.2 = f32[2048,256]{1,0:T(8,128)S(1)} fusion(bf16[1,2048,4096]{2,1,0:T(8,128)(2,1)} %param.4, f32[4096,256]{1,0:T(8,128)} %param.5), kind=kOutput, calls=%fused_computation.6 | convolution fusion | flops 4296015872 | bytes 23068672 | tf_op jit(solution)/shard_map/dot_general | solution.py:29
  16.7 2.2 copy-done
  20.1 6.2 %fusion.14 = f32[2048,256]{1,0:T(8,128)} fusion(f32[2048,256]{1,0:T(8,128)S(1)} %fusion.2, bf16[1,2048,4096]{2,1,0:T(8,128)(2,1)S(1)} %copy-done, f32[4096,256]{1,0:T(8,128)S(1)} %copy-done.1), kind=kOutput, calls=%fused_computation.17 | convolution fusion | flops 4296540160 | bytes 25165824 | tf_op jit(solution)/shard_map/dot_general | solution.py:28
  26.4 62.6 %all-reduce.5.cloned.1.call-done = f32[2048,256]{1,0:T(8,128)} async-done(((f32[2048,256]{1,0:T(8,128)}), f32[2048,256]{1,0:T(8,128)}) %all-reduce.5.cloned.1.call-update) | async-done | bytes 2097168 | tf_op jit(solution)/shard_map/psum | solution.py:30
  89.0 6.4 %fusion.19 = f32[256,256]{0,1:T(8,128)} fusion(f32[2048,256]{1,0:T(8,128)} %all-reduce.5.cloned.1.call-done), kind=kOutput, calls=%fused_computation.23 | convolution fusion | flops 1611137024 | bytes 2359296 | tf_op jit(solution)/shard_map/dot_general | solution.py:31
  95.6 1.7 multiply_bitcast_fusion
  97.3 32.3 %all-reduce.7.cloned.1.call-done = f32[256,256]{0,1:T(8,128)} async-done(((f32[256,256]{0,1:T(8,128)}), f32[256,256]{0,1:T(8,128)}) %all-reduce.7.cloned.1.call-update) | async-done | bytes 262160 | tf_op jit(solution)/shard_map/psum | solution.py:31
  131.8 11.7 %cholesky.50 = f32[128,128]{1,0:T(8,128)S(1)} custom-call(f32[128,128]{1,0:T(8,128)S(1)} %cholesky.118), custom_call_target="Cholesky" | custom-call | tf_op jit(solution)/shard_map/jit(cholesky)/cholesky | solution.py:12
  143.6 9.8 %custom-call.15 = f32[1,128,128]{1,2,0:T(8,128)S(1)} custom-call(f32[1,128,128]{2,1,0:T(8,128)S(1)} %get-tuple-element.27), custom_call_target="InvertDiagBlocksLowerTriangular" | custom-call | tf_op jit(solution)/shard_map/jit(cholesky)/cholesky | solution.py:12
  153.8 11.7 %cholesky.105 = f32[128,128]{1,0:T(8,128)S(1)} custom-call(f32[128,128]{1,0:T(8,128)S(1)} %convolution_subtract_fusion.1), custom_call_target="Cholesky" | custom-call | tf_op jit(solution)/shard_map/jit(cholesky)/cholesky | solution.py:12
  167.6 4.2 while.1
  168.4 1.4 bitcast_dynamic-update-slice_fusion.2
  170.4 1.4 bitcast_dynamic-update-slice_fusion.2
  171.8 19.7 %custom-call.16 = f32[2,128,128]{1,2,0:T(8,128)S(1)} custom-call(f32[2,128,128]{2,1,0:T(8,128)S(1)} %get-tuple-element.10), custom_call_target="InvertDiagBlocksLowerTriangular" | custom-call | tf_op jit(solution)/shard_map/jit(_solve_triangular)/triangular_solve | solution.py:13
  192.6 1.8 convolution_subtract_fusion
  195.6 10.3 %fusion = f32[256,4096]{1,0:T(8,128)} fusion(bf16[1,2048,4096]{2,1,0:T(8,128)(2,1)} %param.4, bf16[128,2048]{1,0:T(8,128)(2,1)S(1)} %convolution_convert_fusion, bf16[128,2048]{1,0:T(8,128)(2,1)S(1)} %get-tuple-element.30), kind=kOutput, calls=%fused_computation.4 | convolution fusion | flops 4297064448 | bytes 22020096 | tf_op jit(solution)/shard_map/dot_general | solution.py:17
  205.9 7.9 %fusion.11 = f32[4096,256]{0,1:T(8,128)} fusion(f32[256,4096]{1,0:T(8,128)} %fusion, bf16[1,2048,4096]{2,1,0:T(8,128)(2,1)S(1)} %bitcast.58, bf16[128,2048]{1,0:T(8,128)(2,1)S(1)} %convolution_convert_fusion, bf16[128,2048]{1,0:T(8,128)(2,1)S(1)} %get-tuple-element.30), kind=kOutput, calls=%fused_computation.13 | convolution fusion | flops 4298113024 | bytes 26214400 | tf_op jit(solution)/shard_map/dot_general | solution.py:17
  213.8 169.5 %all-reduce.9.cloned.1.call-done = f32[4096,256]{0,1:T(8,128)} async-done(((f32[4096,256]{0,1:T(8,128)}), f32[4096,256]{0,1:T(8,128)}) %all-reduce.9.cloned.1.call-update) | async-done | bytes 4194320 | tf_op jit(solution)/shard_map/psum | solution.py:34
  383.3 2.7 multiply_reduce_fusion
  386.0 2.8 psum.31
  388.8 4.8 %multiply_divide_fusion = f32[4096,256]{0,1:T(8,128)} fusion(f32[4096,256]{0,1:T(8,128)} %all-reduce.9.cloned.1.call-done, f32[256]{0:T(256)S(1)} %add_sqrt_fusion), kind=kLoop, calls=%fused_computation.15 | loop fusion | flops 2097152 | bytes 8389632 | tf_op jit(solution)/shard_map/div | solution.py:36
  393.6 11.0 %multiply_convert_fusion = bf16[2048,4096]{1,0:T(8,128)(2,1)} fusion(f32[4096,256]{0,1:T(8,128)} %multiply_divide_fusion, bf16[128,2048]{1,0:T(8,128)(2,1)S(1)} %convolution_convert_fusion, bf16[128,2048]{1,0:T(8,128)(2,1)S(1)} %get-tuple-element.30), kind=kOutput, calls=%fused_computation.2 | convolution fusion | flops 4314890240 | bytes 22020096 | tf_op jit(solution)/shard_map/dot_general | solution.py:43
  404.6 5.6 %copy.8 = f32[4096,256]{1,0:T(8,128)} copy(f32[4096,256]{0,1:T(8,128)} %multiply_divide_fusion) | data formatting | bytes 8388608
  410.2 23.8 %subtract_bitcast_fusion = f32[1,2048,4096]{2,1,0:T(8,128)} fusion(bf16[1,2048,4096]{2,1,0:T(8,128)(2,1)} %param.4, bf16[1,2048,4096]{2,1,0:T(8,128)(2,1)} %param.3, f32[4096,256]{0,1:T(8,128)} %all-reduce.9.cloned.1.call-done, bf16[128,2048]{1,0:T(8,128)(2,1)S(1)} %convolution_convert_fusion, bf16[128,2048]{1,0:T(8,128)(2,1)S(1)} %get-tuple-element.30), kind=kOutput, calls=%fused_computation.3 | convolution fusion | flops 4341104640 | bytes 72351744 | tf_op jit(solution)/shard_map/dot_general | solution.py:38
  (38 shorter events, 8.3 us)
Async XLA Ops:
  7.2 81.8 %all-reduce.5.cloned.1.call-start = ((), (), s32[]{:S(2)}) async-start(), calls=%async_computation | async-start | bytes 4194304 | tf_op jit(solution)/shard_map/psum | solution.py:30
  7.2 11.7 %copy-start = (bf16[1,2048,4096]{2,1,0:T(8,128)(2,1)S(1)}, bf16[1,2048,4096]{2,1,0:T(8,128)(2,1)}, u32[]{:S(2)}) copy-start(bf16[1,2048,4096]{2,1,0:T(8,128)(2,1)} %param.3) | copy-start | bytes 50331652
  7.2 12.9 %copy-start.1 = (f32[4096,256]{1,0:T(8,128)S(1)}, f32[4096,256]{1,0:T(8,128)}, u32[]{:S(2)}) copy-start(f32[4096,256]{1,0:T(8,128)} %param.5) | copy-start | bytes 12582916
  26.3 103.4 %all-reduce.7.cloned.1.call-start = ((), (), s32[]{:S(2)}) async-start(), calls=%async_computation.1 | async-start | bytes 524288 | tf_op jit(solution)/shard_map/psum | solution.py:31
  95.4 287.9 %all-reduce.9.cloned.1.call-start = ((), (), s32[]{:S(2)}) async-start(), calls=%async_computation.2 | async-start | bytes 8388608 | tf_op jit(solution)/shard_map/psum | solution.py:34
  194.4 11.5 %slice-start = ((s8[16777216]{0:T(1024)(128)(4,1)}), s8[4194304]{0:T(1024)(128)(4,1)S(1)}, s32[]{:S(2)}) async-start(s8[16777216]{0:T(1024)(128)(4,1)} %bitcast.57), calls=%async_computation.3 | async-start | bytes 8388608
  195.5 10.4 %slice-start.1 = ((s8[16777216]{0:T(1024)(128)(4,1)}), s8[4194304]{0:T(1024)(128)(4,1)S(1)}, s32[]{:S(2)}) async-start(s8[16777216]{0:T(1024)(128)(4,1)} %bitcast.57), calls=%async_computation.4 | async-start | bytes 8388608
  195.5 10.4 %slice-start.2 = ((s8[16777216]{0:T(1024)(128)(4,1)}), s8[4194304]{0:T(1024)(128)(4,1)S(1)}, s32[]{:S(2)}) async-start(s8[16777216]{0:T(1024)(128)(4,1)} %bitcast.57), calls=%async_computation.5 | async-start | bytes 8388608
  195.6 10.4 %slice-start.3 = ((s8[16777216]{0:T(1024)(128)(4,1)}), s8[4194304]{0:T(1024)(128)(4,1)S(1)}, s32[]{:S(2)}) async-start(s8[16777216]{0:T(1024)(128)(4,1)} %bitcast.57), calls=%async_computation.6 | async-start | bytes 8388608
Sparse Core Ops, SparseCore 0:
  26.4 62.4 all-reduce.4
  95.5 34.1 all-reduce.6
  213.9 169.3 all-reduce.8
where the time goes:
time: 449 us; the launch traced here: 441 us
  waiting for transfers between devices  264 us (59%)
  matrix products  79.4 us (18%)
  other arithmetic  63.9 us (14%)
  between operations  15.7 us (3%)
  local copies, waits for them, and re-layouts  14.2 us (3%)
    psum x1, waiting for transfers between devices, local(): right = lax.psum(partial_right, ('dp', 'fsdp')) / replicas  169 us
    psum x1, waiting for transfers between devices, local(): left = lax.psum(partial_left, ('dp', 'tensor')) / replicas  62.6 us
    another operation x6, other arithmetic, orthonormal(): lower = jnp.linalg.cholesky(gram)  33.9 us
    psum x1, waiting for transfers between devices, local(): gram = lax.psum(jnp.dot(left.T, left, precision=highest), 'fsdp')  32.3 us
    dot_general x1, matrix products, local(): jnp.dot(ortho_low, right_low.T, preferred_element_type=jnp.float32)  23.8 us
    another operation x3, other arithmetic, orthonormal(): return jax.scipy.linalg.solve_triangular(lower, rows_part.T, lower=True).T  19.7 us
    dot_general x2, matrix products, transposed_product(): lax.dot_general(block, ortho_low, (((0,), (0,)), ((), ())), preferred_ele...  18.2 us
    dot_general x1, matrix products, local(): jnp.dot(ortho_low, factor_next_low.T, preferred_element_type=jnp.float32)  11 us
  transfers between devices with their start and end apart: 3, of which 3 were waited for; matrix products, arithmetic and copies ran while one was open for 0% of the time, Pallas kernels for 0%

commit v1 on v0

v1 whole, which is shorter than its diff:
```python
import functools

import jax
import jax.numpy as jnp
from jax import lax
from jax.experimental import pallas as pl
from jax.experimental.pallas import tpu as pltpu
from jax.sharding import PartitionSpec as P

F32 = jnp.float32
LOW = jnp.bfloat16
LANES = 128
COLS_OVER = (((0,), (0,)), ((), ()))


def inverse_factor_kernel(panel, group, gram_ref, out_ref, work_ref):
    n = gram_ref.shape[0]
    work_ref[...] = jnp.zeros_like(work_ref)
    out_ref[...] = jnp.zeros_like(out_ref)
    rows = lax.broadcasted_iota(jnp.int32, (panel, LANES), 0)
    lanes = lax.broadcasted_iota(jnp.int32, (panel, LANES), 1)
    product = functools.partial(
        lax.dot_general,
        dimension_numbers=COLS_OVER,
        precision=lax.Precision.HIGHEST,
        preferred_element_type=F32,
    )
    for start in range(0, n, panel):
        base = start // LANES * LANES
        wide = base + LANES
        upper = gram_ref[start : start + panel, base:n]
        if start:
            before = work_ref[0:start, start : start + panel]
            upper = upper - product(before, work_ref[0:start, base:n])
            inverse = -product(before, work_ref[0:start, n : n + wide])
            inverse = [inverse[:, c : c + LANES] for c in range(0, wide, LANES)]
        else:
            inverse = [jnp.zeros((panel, LANES), F32)]
        inverse[-1] = inverse[-1] + (lanes == rows + (start - base)).astype(F32)
        upper = [upper[:, c : c + LANES] for c in range(0, n - base, LANES)]
        pivots = jnp.ones((panel, LANES), F32)
        for first in range(0, panel, group):
            lane = start - base + first
            columns = [
                jnp.broadcast_to(upper[0][:, lane + q : lane + q + 1], (panel, LANES))
                for q in range(group)
            ]
            factors = []
            for j in range(group):
                r = first + j
                pivot = columns[j][r : r + 1, :]
                pivots = jnp.where(rows == r, jnp.broadcast_to(pivot, rows.shape), pivots)
                factors.append(jnp.where(rows > r, columns[j] * (1.0 / pivot), 0.0))
                for q in range(j + 1, group):
                    columns[q] = columns[q] - factors[j] * columns[q][r : r + 1, :]
            for j in range(group):
                r = first + j
                upper = [x - factors[j] * x[r : r + 1, :] for x in upper]
                inverse = [x - factors[j] * x[r : r + 1, :] for x in inverse]
        scale = lax.rsqrt(pivots)
        for t, x in enumerate(upper):
            at = base + t * LANES
            work_ref[start : start + panel, at : at + LANES] = x * scale
        for t, x in enumerate(inverse):
            at = t * LANES
            work_ref[start : start + panel, n + at : n + at + LANES] = x * scale
            out_ref[start : start + panel, at : at + LANES] = x * scale


def inverse_factor(gram):
    n = gram.shape[0]
    return pl.pallas_call(
        functools.partial(inverse_factor_kernel, 32, 16),
        out_shape=jax.ShapeDtypeStruct((n, n), F32),
        scratch_shapes=[pltpu.VMEM((n, 2 * n), F32)],
        cost_estimate=pl.CostEstimate(flops=2 * n**3, bytes_accessed=8 * n * n, transcendentals=n),
    )(gram)


def bits_of(axis):
    return range(lax.axis_size(axis).bit_length() - 1)


def swap(x, axis, mask):
    size = lax.axis_size(axis)
    return lax.ppermute(x, axis, [(i, i ^ mask) for i in range(size)])


def halve(x, axis, bit, dtype):
    mine = (lax.axis_index(axis) >> bit) & 1
    halves = x.reshape(2, x.shape[0] // 2, x.shape[1])
    kept = lax.dynamic_index_in_dim(halves, mine, 0, False)
    sent = lax.dynamic_index_in_dim(halves, 1 - mine, 0, False)
    return kept + swap(sent.astype(dtype), axis, 1 << bit).astype(F32)


def unhalve(x, axis, bit):
    mine = (lax.axis_index(axis) >> bit) & 1
    other = swap(x, axis, 1 << bit)
    return jnp.where(mine == 0, jnp.concatenate([x, other]), jnp.concatenate([other, x]))


def add_both(x, axis, bit):
    low = x.astype(LOW)
    return low.astype(F32) + swap(low, axis, 1 << bit).astype(F32)


def tree_sum(terms):
    while len(terms) > 1:
        terms = [terms[i] + terms[i + 1] for i in range(0, len(terms), 2)]
    return terms[0]


def sum_left(partial):
    for bit in bits_of("tensor"):
        partial = halve(partial, "tensor", bit, F32)
    half = partial.shape[0] // 2
    parts = [partial[:half], partial[half:]]
    bits = list(bits_of("dp"))
    for k in range(len(bits)):
        parts = [
            add_both(part, "dp", bits[(k + turn) % len(bits)]) for turn, part in enumerate(parts)
        ]
    low = (jnp.concatenate(parts) / lax.axis_size("dp")).astype(LOW)
    for bit in reversed(bits_of("tensor")):
        low = unhalve(low, "tensor", bit)
    return low


def sum_gram(gram):
    shards = lax.axis_size("tensor")
    count = gram.shape[0] // shards
    part = lax.dynamic_slice_in_dim(gram, lax.axis_index("tensor") * count, count, 0)
    part = tree_sum([part] + [swap(part, "fsdp", k) for k in range(1, lax.axis_size("fsdp"))])
    for bit in bits_of("tensor"):
        part = unhalve(part, "tensor", bit)
    return part


def scatter_right(partial):
    half = partial.shape[0] // 2
    parts = [partial[:half], partial[half:]]
    bits = list(bits_of("dp"))
    for k in range(len(bits)):
        parts = [
            halve(part, "dp", bits[(k + turn) % len(bits)], LOW) for turn, part in enumerate(parts)
        ]
    size = lax.axis_size("fsdp")
    index = lax.axis_index("fsdp")
    rank = partial.shape[1]
    split = jnp.stack([part.reshape(size, -1, rank) for part in parts], axis=1)
    own = lax.dynamic_index_in_dim(split, index, 0, False)
    terms = [own]
    for k in range(1, size):
        sent = lax.dynamic_index_in_dim(split, index ^ k, 0, False).astype(LOW)
        terms.append(swap(sent, "fsdp", k).astype(F32))
    return tree_sum(terms)


def gather_right(low):
    size = lax.axis_size("fsdp")
    index = lax.axis_index("fsdp")
    rank = low.shape[-1]
    blocks = jnp.stack([low] + [swap(low, "fsdp", k) for k in range(1, size)])
    for bit in bits_of("fsdp"):
        turned = blocks.reshape((-1, 2, 1 << bit) + low.shape)[:, ::-1].reshape(blocks.shape)
        blocks = jnp.where((index >> bit) & 1, turned, blocks)
    parts = [blocks[:, 0].reshape(-1, rank), blocks[:, 1].reshape(-1, rank)]
    bits = list(bits_of("dp"))
    for k in reversed(range(len(bits))):
        parts = [
            unhalve(part, "dp", bits[(k + turn) % len(bits)]) for turn, part in enumerate(parts)
        ]
    return jnp.concatenate(parts)


def transposed_product(block, low):
    return lax.dot_general(block, low, COLS_OVER, preferred_element_type=F32)


def local(momentum, gradient, factor):
    high = lax.Precision.HIGH
    replicas = lax.axis_size("dp")
    moment = momentum[0]
    change = gradient[0]
    all_rows = moment.shape[0] * lax.axis_size("fsdp")
    all_cols = moment.shape[1] * lax.axis_size("tensor")
    factor_low = factor.astype(LOW)
    left_low = sum_left(
        jnp.dot(moment, factor_low, preferred_element_type=F32)
        + jnp.dot(change, factor_low, preferred_element_type=F32)
    )
    gram = sum_gram(transposed_product(left_low, left_low))
    mixed = transposed_product(moment, left_low) + transposed_product(change, left_low)
    inverse = inverse_factor(gram)
    ortho_low = jnp.dot(left_low.astype(F32), inverse.T, precision=high).astype(LOW)
    right = scatter_right(jnp.dot(mixed, inverse.T, precision=high)) / replicas
    right_low = gather_right(right.astype(LOW))
    right = right_low.astype(F32)
    square_sums = jnp.sum(right * right, axis=0)
    for bit in bits_of("tensor"):
        square_sums = square_sums + swap(square_sums, "tensor", 1 << bit)
    new_factor = right / jnp.sqrt(square_sums / all_cols + 1e-06)
    feedback = jnp.dot(ortho_low, right_low.T, preferred_element_type=F32)
    new_momentum = (moment.astype(F32) + change.astype(F32) - 0.05 * feedback)[None]
    step_scale = jnp.sqrt(F32(all_rows / factor.shape[1]))
    step_direction = (
        step_scale
        * jnp.dot(ortho_low, new_factor.astype(LOW).T, preferred_element_type=F32)
    ).astype(LOW)
    return (new_momentum, step_direction, new_factor)


def solution(mesh):
    in_specs = (P("dp", "fsdp", "tensor"), P("dp", "fsdp", "tensor"), P("tensor", None))
    out_specs = (P("dp", "fsdp", "tensor"), P("fsdp", "tensor"), P("tensor", None))
    return jax.shard_map(local, mesh=mesh, in_specs=in_specs, out_specs=out_specs, check_vma=False)
```

time: 449 us -> 199 us (0.44); the launches traced: 441 us -> 199 us
  waiting for transfers between devices: 264 us -> 65.5 us
  other arithmetic: 63.9 us -> 11.9 us
  starting transfers between devices: 0.29 us -> 31.6 us
  between operations: 15.7 us -> 1.01 us
  local copies, waits for them, and re-layouts: 14.2 us -> 4.53 us
  Pallas kernels: 0 us -> 9.05 us
    psum x3 -> x0, waiting for transfers between devices: 264 us -> none  [the longest x1 169 us: local(): right = lax.psum(partial_right, ('dp', 'fsdp')) / replicas]
    ppermute x0 -> x25, waiting for transfers between devices: none -> 65.5 us  [swap(): return lax.ppermute(x, axis, [(i, i ^ mask) for i in range(size)])]
    another operation x9 -> x2, other arithmetic: 53.7 us -> 1.39 us  [the longest x6 33.9 us: orthonormal(): lower = jnp.linalg.cholesky(gram)]
    ppermute x0 -> x25, starting transfers between devices: none -> 31.6 us  [swap(): return lax.ppermute(x, axis, [(i, i ^ mask) for i in range(size)])]
    pallas_call x0 -> x1, Pallas kernels: none -> 9.05 us  [inverse_factor(): pl.pallas_call(functools.partial(inverse_factor_kernel, 32, 16), out_shap...]
    unnamed x13 -> x26, local copies, waits for them, and re-layouts: 9.04 us -> 2.34 us
    dot_general x7 -> x9, matrix products: 75 us -> 75.3 us  [the longest x1 23 us: local(): feedback = jnp.dot(ortho_low, right_low.T, preferred_element_type=F32)]
  transfers between devices with their start and end apart: 3 -> 25, of which waited for: 3 -> 16; matrix products, arithmetic and copies ran while one was open for 0% -> 23% of each run, Pallas kernels for 0% -> 0%
where the time goes in v1:
time: 199 us
  matrix products  75.3 us (38%)
  waiting for transfers between devices  65.5 us (33%)
  starting transfers between devices  31.6 us (16%)
  other arithmetic  11.9 us (6%)
  Pallas kernels  9.05 us (5%)
  local copies, waits for them, and re-layouts  4.53 us (2%)
    ppermute x25, waiting for transfers between devices, swap(): return lax.ppermute(x, axis, [(i, i ^ mask) for i in range(size)])  65.5 us
    ppermute x25, starting transfers between devices, swap(): return lax.ppermute(x, axis, [(i, i ^ mask) for i in range(size)])  31.6 us
    dot_general x1, matrix products, local(): feedback = jnp.dot(ortho_low, right_low.T, preferred_element_type=F32)  23 us
    dot_general x3, matrix products, transposed_product(): return lax.dot_general(block, low, COLS_OVER, preferred_element_type=F32)  15.5 us
    dot_general x1, matrix products, local(): jnp.dot(change, factor_low, preferred_element_type=F32)  13.2 us
    dot_general x1, matrix products, local(): jnp.dot(ortho_low, new_factor.astype(LOW).T, preferred_element_type=F32)  10.7 us
    pallas_call x1, Pallas kernels, inverse_factor(): pl.pallas_call(functools.partial(inverse_factor_kernel, 32, 16), out_shap...  9.05 us
    dot_general x1, matrix products, local(): jnp.dot(moment, factor_low, preferred_element_type=F32)  6.45 us
  transfers between devices with their start and end apart: 25, of which 16 were waited for; matrix products, arithmetic and copies ran while one was open for 23% of the time, Pallas kernels for 0%

profile of v1, /device:TPU:1, one launch (start us, length us, event | category | flops | bytes accessed | tf_op | source)
XLA Modules:
  0.0 198.9 jit_solution(8317936597568719880)
XLA Ops:
  0.7 13.2 %fusion.2 = f32[2048,256]{1,0:T(8,128)} fusion(bf16[1,2048,4096]{2,1,0:T(8,128)(2,1)} %param.4, f32[4096,256]{1,0:T(8,128)} %param.5), kind=kOutput, calls=%fused_computation.4 | convolution fusion | flops 4296015872 | bytes 23068672 | tf_op jit(solution)/shard_map/dot_general | solution.py:191
  13.9 6.4 %fusion.12 = f32[2048,256]{1,0:T(8,128)S(1)} fusion(f32[2048,256]{1,0:T(8,128)} %fusion.2, bf16[1,2048,4096]{2,1,0:T(8,128)(2,1)S(1)} %copy-done, f32[4096,256]{1,0:T(8,128)S(1)} %copy-done.8), kind=kOutput, calls=%fused_computation.15 | convolution fusion | flops 4296540160 | bytes 25165824 | tf_op jit(solution)/shard_map/dot_general | solution.py:190
  20.5 2.7 %collective-permute-done = f32[1024,256]{1,0:T(8,128)} collective-permute-done((f32[1024,256]{1,0:T(8,128)S(1)}, f32[1024,256]{1,0:T(8,128)}, u32[]{:S(2)}, u32[]{:S(2)}) %collective-permute-start) | collective-permute-done | bytes 1048608 | tf_op jit(solution)/shard_map/ppermute | solution.py:86
  24.6 2.4 %collective-permute-start.1 = (bf16[512,256]{1,0:T(8,128)(2,1)S(1)}, bf16[512,256]{1,0:T(8,128)(2,1)S(1)}, u32[]{:S(2)}, u32[]{:S(2)}) collective-permute-start(bf16[512,256]{1,0:T(8,128)(2,1)S(1)} %get-tuple-element.12), channel_id=1, source_target_pairs={{0,8},{8,0},{16,24},{24,16},{1,9},{9,1},{17,25},{25,17},{2,10},{10... | collective-permute-start | bytes 786440 | tf_op jit(solution)/shard_map/ppermute | solution.py:86
  28.3 5.1 %collective-permute-done.1 = bf16[512,256]{1,0:T(8,128)(2,1)S(1)} collective-permute-done((bf16[512,256]{1,0:T(8,128)(2,1)S(1)}, bf16[512,256]{1,0:T(8,128)(2,1)S(1)}, u32[]{:S(2)}, u32[]{:S(2)}) %collective-permute-start.1) | collective-permute-done | bytes 262176 | tf_op jit(solution)/shard_map/ppermute | solution.py:86
  36.0 4.7 %collective-permute-done.4 = bf16[512,256]{1,0:T(8,128)(2,1)S(1)} collective-permute-done((bf16[512,256]{1,0:T(8,128)(2,1)S(1)}, bf16[512,256]{1,0:T(8,128)(2,1)S(1)}, u32[]{:S(2)}, u32[]{:S(2)}) %collective-permute-start.4) | collective-permute-done | bytes 262176 | tf_op jit(solution)/shard_map/ppermute | solution.py:86
  41.3 2.5 %collective-permute-start.5 = (bf16[1024,256]{1,0:T(8,128)(2,1)S(1)}, bf16[1024,256]{1,0:T(8,128)(2,1)S(1)}, u32[]{:S(2)}, u32[]{:S(2)}) collective-permute-start(bf16[1024,256]{1,0:T(8,128)(2,1)S(1)} %fusion.16), channel_id=1, source_target_pairs={{0,1},{1,0},{2,3},{3,2},{4,5},{5,4},{6,7},{7,6},{8,9},{9,8},{10,11... | collective-permute-start | bytes 1572872 | tf_op jit(solution)/shard_map/ppermute | solution.py:86
  45.9 2.3 %collective-permute-start.7 = (f32[128,256]{1,0:T(8,128)S(1)}, f32[128,256]{1,0:T(8,128)S(1)}, u32[]{:S(2)}, u32[]{:S(2)}) collective-permute-start(f32[128,256]{1,0:T(8,128)S(1)} %constant_dynamic-slice_fusion), channel_id=1, source_target_pairs={{0,4},{2,6},{4,0},{6,2},{1,5},{3,7},{5,1},{7,3},{8,12},{10,14},{12... | collective-permute-start | bytes 393224 | tf_op jit(solution)/shard_map/ppermute | solution.py:86
  49.5 8.9 %fusion = f32[256,4096]{1,0:T(8,128)S(1)} fusion(bf16[1,2048,4096]{2,1,0:T(8,128)(2,1)} %param.4, bf16[1024,256]{1,0:T(8,128)(2,1)S(1)} %collective-permute-done.5, bf16[1024,256]{1,0:T(8,128)(2,1)S(1)} %fusion.16, pred[]{:T(512)S(6)} %eq.12), kind=kOutput, calls=%fused_computation.2 | convolution fusion | flops 4299685888 | bytes 22020096 | tf_op jit(solution)/shard_map/dot_general | solution.py:178
  60.0 6.1 %fusion.8 = f32[256,4096]{1,0:T(8,128)} fusion(f32[256,4096]{1,0:T(8,128)S(1)} %fusion, bf16[1,2048,4096]{2,1,0:T(8,128)(2,1)S(1)} %bitcast.87, bf16[1024,256]{1,0:T(8,128)(2,1)S(1)} %collective-permute-done.5, bf16[1024,256]{1,0:T(8,128)(2,1)S(1)} %fusion.16, pred[]{:T(512)S(6)} %eq.12), kind=kOutput, calls=%fused_computation.12 | convolution fusion | flops 4300734464 | bytes 26214400 | tf_op jit(solution)/shard_map/dot_general | solution.py:178
  66.7 9.1 %shard_map.58 = f32[256,256]{1,0:T(8,128)} custom-call(f32[256,256]{1,0:T(8,128)} %maximum_select_fusion.5.gram_ref), custom_call_target="tpu_custom_call" | custom-call | flops 33554432 | bytes 524288 | tf_op jit(solution)/shard_map/pallas_call | solution.py:72
  75.8 5.6 %fusion.44 = f32[4096,256]{1,0:T(8,128)S(1)} fusion(f32[256,4096]{1,0:T(8,128)} %fusion.8, f32[256,256]{1,0:T(8,128)} %shard_map.58), kind=kOutput, calls=%fused_computation.81 | convolution fusion | flops 1610612736 | bytes 8650752 | tf_op jit(solution)/shard_map/dot_general | solution.py:197
  86.3 10.5 %collective-permute-done.10 = bf16[1024,256]{1,0:T(8,128)(2,1)} collective-permute-done((bf16[1024,256]{1,0:T(8,128)(2,1)S(1)}, bf16[1024,256]{1,0:T(8,128)(2,1)}, u32[]{:S(2)}, u32[]{:S(2)}) %collective-permute-start.10) | collective-permute-done | bytes 524320 | tf_op jit(solution)/shard_map/ppermute | solution.py:86
  103.6 2.7 %collective-permute-done.11 = bf16[512,256]{1,0:T(8,128)(2,1)S(1)} collective-permute-done((bf16[512,256]{1,0:T(8,128)(2,1)}, bf16[512,256]{1,0:T(8,128)(2,1)S(1)}, u32[]{:S(2)}, u32[]{:S(2)}) %collective-permute-start.11) | collective-permute-done | bytes 262176 | tf_op jit(solution)/shard_map/ppermute | solution.py:86
  106.3 2.8 %collective-permute-done.13 = bf16[512,256]{1,0:T(8,128)(2,1)S(1)} collective-permute-done((bf16[512,256]{1,0:T(8,128)(2,1)S(1)}, bf16[512,256]{1,0:T(8,128)(2,1)S(1)}, u32[]{:S(2)}, u32[]{:S(2)}) %collective-permute-start.13) | collective-permute-done | bytes 262176 | tf_op jit(solution)/shard_map/ppermute | solution.py:86
  110.3 3.2 %collective-permute-start.16 = (bf16[2,128,256]{2,1,0:T(8,128)(2,1)S(1)}, bf16[2,128,256]{2,1,0:T(8,128)(2,1)S(1)}, u32[]{:S(2)}, u32[]{:S(2)}) collective-permute-start(bf16[2,128,256]{2,1,0:T(8,128)(2,1)S(1)} %get-tuple-element.7), channel_id=1, source_target_pairs={{0,6},{2,4},{4,2},{6,0},{1,7},{3,5},{5,3},{7,1},{8,14},{10,12},{12... | collective-permute-start | bytes 393224 | tf_op jit(solution)/shard_map/ppermute | solution.py:86
  116.1 8.8 %collective-permute-done.15 = bf16[2,128,256]{2,1,0:T(8,128)(2,1)S(1)} collective-permute-done((bf16[2,128,256]{2,1,0:T(8,128)(2,1)S(1)}, bf16[2,128,256]{2,1,0:T(8,128)(2,1)S(1)}, u32[]{:S(2)}, u32[]{:S(2)}) %collective-permute-start.15) | collective-permute-done | bytes 131104 | tf_op jit(solution)/shard_map/ppermute | solution.py:86
  124.9 3.7 %collective-permute-start.19 = (bf16[2,128,256]{2,1,0:T(8,128)(2,1)S(1)}, bf16[2,128,256]{2,1,0:T(8,128)(2,1)S(1)}, u32[]{:S(2)}, u32[]{:S(2)}) collective-permute-start(bf16[2,128,256]{2,1,0:T(8,128)(2,1)S(1)} %fusion.31), channel_id=1, source_target_pairs={{0,6},{2,4},{4,2},{6,0},{1,7},{3,5},{5,3},{7,1},{8,14},{10,12},{12... | collective-permute-start | bytes 393224 | tf_op jit(solution)/shard_map/ppermute | solution.py:86
  131.1 7.3 %collective-permute-done.18 = bf16[2,128,256]{2,1,0:T(8,128)(2,1)S(1)} collective-permute-done((bf16[2,128,256]{2,1,0:T(8,128)(2,1)S(1)}, bf16[2,128,256]{2,1,0:T(8,128)(2,1)S(1)}, u32[]{:S(2)}, u32[]{:S(2)}) %collective-permute-start.18) | collective-permute-done | bytes 131104 | tf_op jit(solution)/shard_map/ppermute | solution.py:86
  140.3 5.0 %collective-permute-done.22 = bf16[512,256]{1,0:T(8,128)(2,1)S(1)} collective-permute-done((bf16[512,256]{1,0:T(8,128)(2,1)S(1)}, bf16[512,256]{1,0:T(8,128)(2,1)S(1)}, u32[]{:S(2)}, u32[]{:S(2)}) %collective-permute-start.22) | collective-permute-done | bytes 262176 | tf_op jit(solution)/shard_map/ppermute | solution.py:86
  148.0 9.0 %collective-permute-done.23 = bf16[1024,256]{1,0:T(8,128)(2,1)} collective-permute-done((bf16[1024,256]{1,0:T(8,128)(2,1)S(1)}, bf16[1024,256]{1,0:T(8,128)(2,1)}, u32[]{:S(2)}, u32[]{:S(2)}) %collective-permute-start.23) | collective-permute-done | bytes 524320 | tf_op jit(solution)/shard_map/ppermute | solution.py:86
  159.6 3.2 %collective-permute-start.24 = (f32[256]{0:T(256)S(1)}, f32[256]{0:T(256)S(1)}, u32[]{:S(2)}, u32[]{:S(2)}) collective-permute-start(f32[256]{0:T(256)S(1)} %fusion.11), channel_id=1, source_target_pairs={{0,1},{1,0},{2,3},{3,2},{4,5},{5,4},{6,7},{7,6},{8,9},{9,8},{10,11... | collective-permute-start | bytes 3080 | tf_op jit(solution)/shard_map/ppermute | solution.py:86
  162.8 23.0 %subtract_bitcast_fusion = f32[1,2048,4096]{2,1,0:T(8,128)} fusion(bf16[1,2048,4096]{2,1,0:T(8,128)(2,1)} %param.4, bf16[1,2048,4096]{2,1,0:T(8,128)(2,1)} %param.3, bf16[2048,256]{1,0:T(8,128)(2,1)S(1)} %convolution_convert_fusion, bf16[2048,256]{1,0:T(8,128)(2,1)S(1)} %maximum_select_fusion.2, bf16[2048,256]{1,0:T(8,128)(2,1)S(1)} %maximum_select_fusion.1), kind=kOutput, calls=%fused_computation.1 | convolution fusion | flops 4341104640 | bytes 70254592 | tf_op jit(solution)/shard_map/dot_general | solution.py:204
  188.2 10.7 %multiply_convert_fusion = bf16[2048,4096]{1,0:T(8,128)(2,1)} fusion(bf16[2048,256]{1,0:T(8,128)(2,1)S(1)} %convolution_convert_fusion, f32[4096,256]{1,0:T(8,128)} %convert_divide_fusion), kind=kOutput, calls=%fused_computation | convolution fusion | flops 4312793088 | bytes 22020096 | tf_op jit(solution)/shard_map/dot_general | solution.py:209
  (97 shorter events, 38.9 us)
Async XLA Ops:
  24.6 8.8 %collective-permute-start.1 = (bf16[512,256]{1,0:T(8,128)(2,1)S(1)}, bf16[512,256]{1,0:T(8,128)(2,1)S(1)}, u32[]{:S(2)}, u32[]{:S(2)}) collective-permute-start(bf16[512,256]{1,0:T(8,128)(2,1)S(1)} %get-tuple-element.12), channel_id=1, source_target_pairs={{0,8},{8,0},{16,24},{24,16},{1,9},{9,1},{17,25},{25,17},{2,10},{10... | collective-permute-start | bytes 786440 | tf_op jit(solution)/shard_map/ppermute | solution.py:86
  27.0 7.2 %collective-permute-start.3 = (bf16[512,256]{1,0:T(8,128)(2,1)S(1)}, bf16[512,256]{1,0:T(8,128)(2,1)S(1)}, u32[]{:S(2)}, u32[]{:S(2)}) collective-permute-start(bf16[512,256]{1,0:T(8,128)(2,1)S(1)} %get-tuple-element.13), channel_id=1, source_target_pairs={{0,16},{8,24},{16,0},{24,8},{1,17},{9,25},{17,1},{25,9},{2,18},{10... | collective-permute-start | bytes 786440 | tf_op jit(solution)/shard_map/ppermute | solution.py:86
  34.4 6.3 %collective-permute-start.4 = (bf16[512,256]{1,0:T(8,128)(2,1)S(1)}, bf16[512,256]{1,0:T(8,128)(2,1)S(1)}, u32[]{:S(2)}, u32[]{:S(2)}) collective-permute-start(bf16[512,256]{1,0:T(8,128)(2,1)S(1)} %get-tuple-element.11), channel_id=1, source_target_pairs={{0,8},{8,0},{16,24},{24,16},{1,9},{9,1},{17,25},{25,17},{2,10},{10... | collective-permute-start | bytes 786440 | tf_op jit(solution)/shard_map/ppermute | solution.py:86
  34.8 6.3 %collective-permute-start.2 = (bf16[512,256]{1,0:T(8,128)(2,1)S(1)}, bf16[512,256]{1,0:T(8,128)(2,1)S(1)}, u32[]{:S(2)}, u32[]{:S(2)}) collective-permute-start(bf16[512,256]{1,0:T(8,128)(2,1)S(1)} %get-tuple-element.10), channel_id=1, source_target_pairs={{0,16},{8,24},{16,0},{24,8},{1,17},{9,25},{17,1},{25,9},{2,18},{10... | collective-permute-start | bytes 786440 | tf_op jit(solution)/shard_map/ppermute | solution.py:86
  41.3 4.0 %collective-permute-start.5 = (bf16[1024,256]{1,0:T(8,128)(2,1)S(1)}, bf16[1024,256]{1,0:T(8,128)(2,1)S(1)}, u32[]{:S(2)}, u32[]{:S(2)}) collective-permute-start(bf16[1024,256]{1,0:T(8,128)(2,1)S(1)} %fusion.16), channel_id=1, source_target_pairs={{0,1},{1,0},{2,3},{3,2},{4,5},{5,4},{6,7},{7,6},{8,9},{9,8},{10,11... | collective-permute-start | bytes 1572872 | tf_op jit(solution)/shard_map/ppermute | solution.py:86
  45.9 12.5 %collective-permute-start.7 = (f32[128,256]{1,0:T(8,128)S(1)}, f32[128,256]{1,0:T(8,128)S(1)}, u32[]{:S(2)}, u32[]{:S(2)}) collective-permute-start(f32[128,256]{1,0:T(8,128)S(1)} %constant_dynamic-slice_fusion), channel_id=1, source_target_pairs={{0,4},{2,6},{4,0},{6,2},{1,5},{3,7},{5,1},{7,3},{8,12},{10,14},{12... | collective-permute-start | bytes 393224 | tf_op jit(solution)/shard_map/ppermute | solution.py:86
  48.2 10.2 %collective-permute-start.8 = (f32[128,256]{1,0:T(8,128)S(1)}, f32[128,256]{1,0:T(8,128)S(1)}, u32[]{:S(2)}, u32[]{:S(2)}) collective-permute-start(f32[128,256]{1,0:T(8,128)S(1)} %constant_dynamic-slice_fusion), channel_id=1, source_target_pairs={{0,6},{2,4},{4,2},{6,0},{1,7},{3,5},{5,3},{7,1},{8,14},{10,12},{12... | collective-permute-start | bytes 393224 | tf_op jit(solution)/shard_map/ppermute | solution.py:86
  49.3 9.2 %collective-permute-start.6 = (f32[128,256]{1,0:T(8,128)S(1)}, f32[128,256]{1,0:T(8,128)S(1)}, u32[]{:S(2)}, u32[]{:S(2)}) collective-permute-start(f32[128,256]{1,0:T(8,128)S(1)} %constant_dynamic-slice_fusion), channel_id=1, source_target_pairs={{0,2},{2,0},{4,6},{6,4},{1,3},{3,1},{5,7},{7,5},{8,10},{10,8},{12,... | collective-permute-start | bytes 393224 | tf_op jit(solution)/shard_map/ppermute | solution.py:86
  58.5 7.5 %collective-permute-start.9 = (f32[128,256]{1,0:T(8,128)S(1)}, f32[128,256]{1,0:T(8,128)S(1)}, u32[]{:S(2)}, u32[]{:S(2)}) collective-permute-start(f32[128,256]{1,0:T(8,128)S(1)} %add_add_fusion), channel_id=1, source_target_pairs={{0,1},{1,0},{2,3},{3,2},{4,5},{5,4},{6,7},{7,6},{8,9},{9,8},{10,11... | collective-permute-start | bytes 393224 | tf_op jit(solution)/shard_map/ppermute | solution.py:86
  83.1 13.7 %collective-permute-start.10 = (bf16[1024,256]{1,0:T(8,128)(2,1)S(1)}, bf16[1024,256]{1,0:T(8,128)(2,1)}, u32[]{:S(2)}, u32[]{:S(2)}) collective-permute-start(bf16[1024,256]{1,0:T(8,128)(2,1)S(1)} %fusion.20), channel_id=1, source_target_pairs={{0,8},{8,0},{16,24},{24,16},{1,9},{9,1},{17,25},{25,17},{2,10},{10... | collective-permute-start | bytes 1572872 | tf_op jit(solution)/shard_map/ppermute | solution.py:86
  85.1 15.1 %collective-permute-start.12 = (bf16[1024,256]{1,0:T(8,128)(2,1)}, bf16[1024,256]{1,0:T(8,128)(2,1)}, u32[]{:S(2)}, u32[]{:S(2)}) collective-permute-start(bf16[1024,256]{1,0:T(8,128)(2,1)} %fusion.21), channel_id=1, source_target_pairs={{0,16},{8,24},{16,0},{24,8},{1,17},{9,25},{17,1},{25,9},{2,18},{10... | collective-permute-start | bytes 1572872 | tf_op jit(solution)/shard_map/ppermute | solution.py:86
  99.0 7.2 %collective-permute-start.11 = (bf16[512,256]{1,0:T(8,128)(2,1)}, bf16[512,256]{1,0:T(8,128)(2,1)S(1)}, u32[]{:S(2)}, u32[]{:S(2)}) collective-permute-start(bf16[512,256]{1,0:T(8,128)(2,1)} %fusion.22), channel_id=1, source_target_pairs={{0,16},{8,24},{16,0},{24,8},{1,17},{9,25},{17,1},{25,9},{2,18},{10... | collective-permute-start | bytes 786440 | tf_op jit(solution)/shard_map/ppermute | solution.py:86
  102.4 6.8 %collective-permute-start.13 = (bf16[512,256]{1,0:T(8,128)(2,1)S(1)}, bf16[512,256]{1,0:T(8,128)(2,1)S(1)}, u32[]{:S(2)}, u32[]{:S(2)}) collective-permute-start(bf16[512,256]{1,0:T(8,128)(2,1)S(1)} %fusion.23), channel_id=1, source_target_pairs={{0,8},{8,0},{16,24},{24,16},{1,9},{9,1},{17,25},{25,17},{2,10},{10... | collective-permute-start | bytes 786440 | tf_op jit(solution)/shard_map/ppermute | solution.py:86
  110.3 5.8 %collective-permute-start.16 = (bf16[2,128,256]{2,1,0:T(8,128)(2,1)S(1)}, bf16[2,128,256]{2,1,0:T(8,128)(2,1)S(1)}, u32[]{:S(2)}, u32[]{:S(2)}) collective-permute-start(bf16[2,128,256]{2,1,0:T(8,128)(2,1)S(1)} %get-tuple-element.7), channel_id=1, source_target_pairs={{0,6},{2,4},{4,2},{6,0},{1,7},{3,5},{5,3},{7,1},{8,14},{10,12},{12... | collective-permute-start | bytes 393224 | tf_op jit(solution)/shard_map/ppermute | solution.py:86
  113.5 11.3 %collective-permute-start.15 = (bf16[2,128,256]{2,1,0:T(8,128)(2,1)S(1)}, bf16[2,128,256]{2,1,0:T(8,128)(2,1)S(1)}, u32[]{:S(2)}, u32[]{:S(2)}) collective-permute-start(bf16[2,128,256]{2,1,0:T(8,128)(2,1)S(1)} %get-tuple-element.6), channel_id=1, source_target_pairs={{0,4},{2,6},{4,0},{6,2},{1,5},{3,7},{5,1},{7,3},{8,12},{10,14},{12... | collective-permute-start | bytes 393224 | tf_op jit(solution)/shard_map/ppermute | solution.py:86
  114.2 10.7 %collective-permute-start.14 = (bf16[2,128,256]{2,1,0:T(8,128)(2,1)S(1)}, bf16[2,128,256]{2,1,0:T(8,128)(2,1)S(1)}, u32[]{:S(2)}, u32[]{:S(2)}) collective-permute-start(bf16[2,128,256]{2,1,0:T(8,128)(2,1)S(1)} %get-tuple-element.5), channel_id=1, source_target_pairs={{0,2},{2,0},{4,6},{6,4},{1,3},{3,1},{5,7},{7,5},{8,10},{10,8},{12,... | collective-permute-start | bytes 393224 | tf_op jit(solution)/shard_map/ppermute | solution.py:86
  124.9 6.2 %collective-permute-start.19 = (bf16[2,128,256]{2,1,0:T(8,128)(2,1)S(1)}, bf16[2,128,256]{2,1,0:T(8,128)(2,1)S(1)}, u32[]{:S(2)}, u32[]{:S(2)}) collective-permute-start(bf16[2,128,256]{2,1,0:T(8,128)(2,1)S(1)} %fusion.31), channel_id=1, source_target_pairs={{0,6},{2,4},{4,2},{6,0},{1,7},{3,5},{5,3},{7,1},{8,14},{10,12},{12... | collective-permute-start | bytes 393224 | tf_op jit(solution)/shard_map/ppermute | solution.py:86
  128.6 9.8 %collective-permute-start.18 = (bf16[2,128,256]{2,1,0:T(8,128)(2,1)S(1)}, bf16[2,128,256]{2,1,0:T(8,128)(2,1)S(1)}, u32[]{:S(2)}, u32[]{:S(2)}) collective-permute-start(bf16[2,128,256]{2,1,0:T(8,128)(2,1)S(1)} %fusion.31), channel_id=1, source_target_pairs={{0,4},{2,6},{4,0},{6,2},{1,5},{3,7},{5,1},{7,3},{8,12},{10,14},{12... | collective-permute-start | bytes 393224 | tf_op jit(solution)/shard_map/ppermute | solution.py:86
  128.6 9.8 %collective-permute-start.17 = (bf16[2,128,256]{2,1,0:T(8,128)(2,1)S(1)}, bf16[2,128,256]{2,1,0:T(8,128)(2,1)S(1)}, u32[]{:S(2)}, u32[]{:S(2)}) collective-permute-start(bf16[2,128,256]{2,1,0:T(8,128)(2,1)S(1)} %fusion.31), channel_id=1, source_target_pairs={{0,2},{2,0},{4,6},{6,4},{1,3},{3,1},{5,7},{7,5},{8,10},{10,8},{12,... | collective-permute-start | bytes 393224 | tf_op jit(solution)/shard_map/ppermute | solution.py:86
  138.9 6.4 %collective-permute-start.22 = (bf16[512,256]{1,0:T(8,128)(2,1)S(1)}, bf16[512,256]{1,0:T(8,128)(2,1)S(1)}, u32[]{:S(2)}, u32[]{:S(2)}) collective-permute-start(bf16[512,256]{1,0:T(8,128)(2,1)S(1)} %bitcast.111), channel_id=1, source_target_pairs={{0,8},{8,0},{16,24},{24,16},{1,9},{9,1},{17,25},{25,17},{2,10},{10... | collective-permute-start | bytes 786440 | tf_op jit(solution)/shard_map/ppermute | solution.py:86
  140.1 6.0 %collective-permute-start.20 = (bf16[512,256]{1,0:T(8,128)(2,1)S(1)}, bf16[512,256]{1,0:T(8,128)(2,1)S(1)}, u32[]{:S(2)}, u32[]{:S(2)}) collective-permute-start(bf16[512,256]{1,0:T(8,128)(2,1)S(1)} %bitcast.109), channel_id=1, source_target_pairs={{0,16},{8,24},{16,0},{24,8},{1,17},{9,25},{17,1},{25,9},{2,18},{10... | collective-permute-start | bytes 786440 | tf_op jit(solution)/shard_map/ppermute | solution.py:86
  145.5 11.5 %collective-permute-start.23 = (bf16[1024,256]{1,0:T(8,128)(2,1)S(1)}, bf16[1024,256]{1,0:T(8,128)(2,1)}, u32[]{:S(2)}, u32[]{:S(2)}) collective-permute-start(bf16[1024,256]{1,0:T(8,128)(2,1)S(1)} %maximum_select_fusion.4), channel_id=1, source_target_pairs={{0,16},{8,24},{16,0},{24,8},{1,17},{9,25},{17,1},{25,9},{2,18},{10... | collective-permute-start | bytes 1572872 | tf_op jit(solution)/shard_map/ppermute | solution.py:86
  146.4 12.3 %collective-permute-start.21 = (bf16[1024,256]{1,0:T(8,128)(2,1)S(1)}, bf16[1024,256]{1,0:T(8,128)(2,1)S(1)}, u32[]{:S(2)}, u32[]{:S(2)}) collective-permute-start(bf16[1024,256]{1,0:T(8,128)(2,1)S(1)} %maximum_select_fusion.3), channel_id=1, source_target_pairs={{0,8},{8,0},{16,24},{24,16},{1,9},{9,1},{17,25},{25,17},{2,10},{10... | collective-permute-start | bytes 1572872 | tf_op jit(solution)/shard_map/ppermute | solution.py:86
  159.6 26.3 %collective-permute-start.24 = (f32[256]{0:T(256)S(1)}, f32[256]{0:T(256)S(1)}, u32[]{:S(2)}, u32[]{:S(2)}) collective-permute-start(f32[256]{0:T(256)S(1)} %fusion.11), channel_id=1, source_target_pairs={{0,1},{1,0},{2,3},{3,2},{4,5},{5,4},{6,7},{7,6},{8,9},{9,8},{10,11... | collective-permute-start | bytes 3080 | tf_op jit(solution)/shard_map/ppermute | solution.py:86
  (14 other events, 146.7 us)

commit v2 on v1

--- a/solution.py
+++ b/solution.py
@@ -67,14 +67,183 @@
             out_ref[start : start + panel, at : at + LANES] = x * scale
 
 
-def inverse_factor(gram):
-    n = gram.shape[0]
+def apply_kernel(panel, group, gram_ref, high_ref, low_ref, inverse_ref, right_ref, work_ref):
+    inverse_factor_kernel(panel, group, gram_ref, inverse_ref, work_ref)
+    inverse = inverse_ref[...]
+    inverse_high = inverse.astype(LOW)
+    inverse_low = (inverse - inverse_high.astype(F32)).astype(LOW)
+    width = tile_of(high_ref.shape[1])
+    for at in range(0, high_ref.shape[1], width):
+        high = high_ref[:, at : at + width]
+        low = low_ref[:, at : at + width]
+        right_ref[:, at : at + width] = (
+            jnp.dot(inverse_high, low, preferred_element_type=F32)
+            + jnp.dot(inverse_low, high, preferred_element_type=F32)
+        ) + jnp.dot(inverse_high, high, preferred_element_type=F32)
+
+
+def apply_inverse(gram, high, low):
+    n, columns = high.shape
     return pl.pallas_call(
-        functools.partial(inverse_factor_kernel, 32, 16),
-        out_shape=jax.ShapeDtypeStruct((n, n), F32),
+        functools.partial(apply_kernel, 32, 16),
+        out_shape=(
+            jax.ShapeDtypeStruct((n, n), F32),
+            jax.ShapeDtypeStruct((n, columns), F32),
+        ),
         scratch_shapes=[pltpu.VMEM((n, 2 * n), F32)],
-        cost_estimate=pl.CostEstimate(flops=2 * n**3, bytes_accessed=8 * n * n, transcendentals=n),
-    )(gram)
+        compiler_params=pltpu.CompilerParams(vmem_limit_bytes=24 << 20),
+        cost_estimate=pl.CostEstimate(
+            flops=40 * n * n * columns, bytes_accessed=8 * n * columns, transcendentals=n
+        ),
+    )(gram, high, low)
+
+
+def tile_of(size):
+    return 256 if size % 256 == 0 else LANES
+
+
+def left_kernel(moment_ref, change_ref, factor_ref, out_ref):
+    factor = factor_ref[...]
+    out_ref[...] = jnp.dot(moment_ref[...], factor, preferred_element_type=F32) + jnp.dot(
+        change_ref[...], factor, preferred_element_type=F32
+    )
+
+
+def left_product(moment, change, factor_low):
+    rows, columns = moment.shape
+    rank = factor_low.shape[1]
+    tile = LANES
+    return pl.pallas_call(
+        left_kernel,
+        grid=(rows // tile,),
+        in_specs=[
+            pl.BlockSpec((tile, columns), lambda i: (i, 0)),
+            pl.BlockSpec((tile, columns), lambda i: (i, 0)),
+            pl.BlockSpec((columns, rank), lambda i: (0, 0)),
+        ],
+        out_specs=pl.BlockSpec((tile, rank), lambda i: (i, 0)),
+        out_shape=jax.ShapeDtypeStruct((rows, rank), F32),
+        compiler_params=pltpu.CompilerParams(vmem_limit_bytes=24 << 20),
+        cost_estimate=pl.CostEstimate(
+            flops=4 * rows * columns * rank,
+            bytes_accessed=4 * rows * columns,
+            transcendentals=0,
+        ),
+    )(moment, change, factor_low)
+
+
+def mixed_kernel(left_ref, moment_ref, change_ref, high_ref, low_ref):
+    left = left_ref[...]
+    mixed = jnp.dot(left, moment_ref[...], preferred_element_type=F32) + jnp.dot(
+        left, change_ref[...], preferred_element_type=F32
+    )
+    high = mixed.astype(LOW)
+    high_ref[...] = high
+    low_ref[...] = (mixed - high.astype(F32)).astype(LOW)
+
+
+def mixed_product(left_turned, moment, change):
+    rows, columns = moment.shape
+    rank = left_turned.shape[0]
+    tile = tile_of(columns)
+    return pl.pallas_call(
+        mixed_kernel,
+        grid=(columns // tile,),
+        in_specs=[
+            pl.BlockSpec((rank, rows), lambda j: (0, 0)),
+            pl.BlockSpec((rows, tile), lambda j: (0, j)),
+            pl.BlockSpec((rows, tile), lambda j: (0, j)),
+        ],
+        out_specs=[pl.BlockSpec((rank, tile), lambda j: (0, j))] * 2,
+        out_shape=[jax.ShapeDtypeStruct((rank, columns), LOW)] * 2,
+        compiler_params=pltpu.CompilerParams(vmem_limit_bytes=24 << 20),
+        cost_estimate=pl.CostEstimate(
+            flops=4 * rows * columns * rank,
+            bytes_accessed=4 * rows * columns,
+            transcendentals=0,
+        ),
+    )(left_turned, moment, change)
+
+
+def feedback_kernel(place_ref, ortho_ref, right_ref, moment_ref, change_ref, *refs):
+    feedback = jnp.dot(ortho_ref[...], right_ref[0], preferred_element_type=F32)
+    refs[-1][0] = moment_ref[0].astype(F32) + change_ref[0].astype(F32) - 0.05 * feedback
+
+
+def feedback_columns(places, ortho_low, pieces, momentum, gradient, written):
+    count, rank, width = pieces.shape
+    _, rows, columns = momentum.shape
+    tile = tile_of(width)
+    steps = width // tile
+
+    def column(j, place):
+        return (0, 0, place[j // steps] * steps + j % steps)
+
+    block = pl.BlockSpec((1, rows, tile), column)
+    specs = [
+        pl.BlockSpec((rows, rank), lambda j, place: (0, 0)),
+        pl.BlockSpec((1, rank, tile), lambda j, place: (j // steps, 0, j % steps)),
+        block,
+        block,
+    ]
+    operands = [places, ortho_low, pieces, momentum, gradient]
+    aliases = {}
+    if written is not None:
+        specs.append(pl.BlockSpec(memory_space=pl.ANY))
+        aliases = {len(operands): 0}
+        operands.append(written)
+    size = count * width
+    return pl.pallas_call(
+        feedback_kernel,
+        grid_spec=pltpu.PrefetchScalarGridSpec(
+            num_scalar_prefetch=1, grid=(count * steps,), in_specs=specs, out_specs=block
+        ),
+        out_shape=jax.ShapeDtypeStruct(momentum.shape, F32),
+        input_output_aliases=aliases,
+        compiler_params=pltpu.CompilerParams(vmem_limit_bytes=24 << 20),
+        cost_estimate=pl.CostEstimate(
+            flops=2 * rows * rank * size, bytes_accessed=8 * rows * size, transcendentals=0
+        ),
+    )(*operands)
+
+
+def step_kernel(scale, place_ref, ortho_ref, right_ref, norm_ref, step_ref, factor_ref):
+    factor = right_ref[0].astype(F32) / norm_ref[...]
+    product = jnp.dot(ortho_ref[...], factor.astype(LOW), preferred_element_type=F32)
+    step_ref[...] = (scale * product).astype(LOW)
+    factor_ref[...] = factor.T
+
+
+def step_outputs(places, ortho_low, pieces, norms, scale):
+    count, rank, width = pieces.shape
+    rows = ortho_low.shape[0]
+    tile = tile_of(width)
+    steps = width // tile
+    columns = count * width
+    return pl.pallas_call(
+        functools.partial(step_kernel, scale),
+        grid_spec=pltpu.PrefetchScalarGridSpec(
+            num_scalar_prefetch=1,
+            grid=(count * steps,),
+            in_specs=[
+                pl.BlockSpec((rows, rank), lambda j, place: (0, 0)),
+                pl.BlockSpec((1, rank, tile), lambda j, place: (j // steps, 0, j % steps)),
+                pl.BlockSpec((rank, 1), lambda j, place: (0, 0)),
+            ],
+            out_specs=[
+                pl.BlockSpec((rows, tile), lambda j, place: (0, place[j // steps] * steps + j % steps)),
+                pl.BlockSpec((tile, rank), lambda j, place: (place[j // steps] * steps + j % steps, 0)),
+            ],
+        ),
+        out_shape=[
+            jax.ShapeDtypeStruct((rows, columns), LOW),
+            jax.ShapeDtypeStruct((columns, rank), F32),
+        ],
+        compiler_params=pltpu.CompilerParams(vmem_limit_bytes=24 << 20),
+        cost_estimate=pl.CostEstimate(
+            flops=2 * rows * rank * columns, bytes_accessed=2 * rows * columns, transcendentals=0
+        ),
+    )(places, ortho_low, pieces, norms)
 
 
 def bits_of(axis):
@@ -86,11 +255,11 @@
     return lax.ppermute(x, axis, [(i, i ^ mask) for i in range(size)])
 
 
-def halve(x, axis, bit, dtype):
+def halve(x, axis, bit, dtype, dim):
     mine = (lax.axis_index(axis) >> bit) & 1
-    halves = x.reshape(2, x.shape[0] // 2, x.shape[1])
-    kept = lax.dynamic_index_in_dim(halves, mine, 0, False)
-    sent = lax.dynamic_index_in_dim(halves, 1 - mine, 0, False)
+    size = x.shape[dim] // 2
+    kept = lax.dynamic_slice_in_dim(x, mine * size, size, dim)
+    sent = lax.dynamic_slice_in_dim(x, (1 - mine) * size, size, dim)
     return kept + swap(sent.astype(dtype), axis, 1 << bit).astype(F32)
 
 
@@ -113,7 +282,7 @@
 
 def sum_left(partial):
     for bit in bits_of("tensor"):
-        partial = halve(partial, "tensor", bit, F32)
+        partial = halve(partial, "tensor", bit, F32, 0)
     half = partial.shape[0] // 2
     parts = [partial[:half], partial[half:]]
     bits = list(bits_of("dp"))
@@ -137,77 +306,110 @@
     return part
 
 
+def orders_of():
+    bits = list(bits_of("dp"))
+    return [bits[turn % len(bits) :] + bits[: turn % len(bits)] for turn in range(2)]
+
+
 def scatter_right(partial):
-    half = partial.shape[0] // 2
-    parts = [partial[:half], partial[half:]]
-    bits = list(bits_of("dp"))
-    for k in range(len(bits)):
+    half = partial.shape[1] // 2
+    parts = [partial[:, :half], partial[:, half:]]
+    orders = orders_of()
+    for k in range(len(orders[0])):
         parts = [
-            halve(part, "dp", bits[(k + turn) % len(bits)], LOW) for turn, part in enumerate(parts)
+            halve(part, "dp", order[k], LOW, 1) for part, order in zip(parts, orders)
         ]
     size = lax.axis_size("fsdp")
     index = lax.axis_index("fsdp")
-    rank = partial.shape[1]
-    split = jnp.stack([part.reshape(size, -1, rank) for part in parts], axis=1)
-    own = lax.dynamic_index_in_dim(split, index, 0, False)
-    terms = [own]
+    width = parts[0].shape[1] // size
+
+    def share(at):
+        return jnp.concatenate(
+            [lax.dynamic_slice_in_dim(part, at * width, width, 1) for part in parts], axis=1
+        )
+
+    terms = [share(index)]
     for k in range(1, size):
-        sent = lax.dynamic_index_in_dim(split, index ^ k, 0, False).astype(LOW)
-        terms.append(swap(sent, "fsdp", k).astype(F32))
+        terms.append(swap(share(index ^ k).astype(LOW), "fsdp", k).astype(F32))
     return tree_sum(terms)
 
 
-def gather_right(low):
+def gather_fsdp(low):
     size = lax.axis_size("fsdp")
     index = lax.axis_index("fsdp")
-    rank = low.shape[-1]
-    blocks = jnp.stack([low] + [swap(low, "fsdp", k) for k in range(1, size)])
+    width = low.shape[1] // 2
+    blocks = [low] + [swap(low, "fsdp", k) for k in range(1, size)]
     for bit in bits_of("fsdp"):
-        turned = blocks.reshape((-1, 2, 1 << bit) + low.shape)[:, ::-1].reshape(blocks.shape)
-        blocks = jnp.where((index >> bit) & 1, turned, blocks)
-    parts = [blocks[:, 0].reshape(-1, rank), blocks[:, 1].reshape(-1, rank)]
-    bits = list(bits_of("dp"))
-    for k in reversed(range(len(bits))):
-        parts = [
-            unhalve(part, "dp", bits[(k + turn) % len(bits)]) for turn, part in enumerate(parts)
-        ]
-    return jnp.concatenate(parts)
-
-
-def transposed_product(block, low):
-    return lax.dot_general(block, low, COLS_OVER, preferred_element_type=F32)
+        high = ((index >> bit) & 1) == 1
+        blocks = [jnp.where(high, blocks[i ^ (1 << bit)], blocks[i]) for i in range(size)]
+    return [
+        jnp.concatenate([b[:, :width] for b in blocks], axis=1),
+        jnp.concatenate([b[:, width:] for b in blocks], axis=1),
+    ]
+
+
+def gather_rounds(pieces):
+    index = lax.axis_index("dp")
+    orders = orders_of()
+    depth = len(orders[0])
+    known = [{0: piece} for piece in pieces]
+    rounds = []
+    for r in range(depth + 1):
+        new = []
+        for turn, order in enumerate(orders):
+            for mask in range(1 << depth):
+                if mask.bit_count() != r:
+                    continue
+                if r:
+                    bit = next(b for b in order if (mask >> b) & 1)
+                    known[turn][mask] = swap(known[turn][mask ^ (1 << bit)], "dp", 1 << bit)
+                place = turn << depth
+                for k, b in enumerate(order):
+                    place = place + ((((index ^ mask) >> b) & 1) << (depth - 1 - k))
+                new.append((place, turn, mask, known[turn][mask]))
+        rounds.append(new)
+    return rounds
 
 
 def local(momentum, gradient, factor):
-    high = lax.Precision.HIGH
     replicas = lax.axis_size("dp")
     moment = momentum[0]
     change = gradient[0]
     all_rows = moment.shape[0] * lax.axis_size("fsdp")
     all_cols = moment.shape[1] * lax.axis_size("tensor")
-    factor_low = factor.astype(LOW)
-    left_low = sum_left(
-        jnp.dot(moment, factor_low, preferred_element_type=F32)
-        + jnp.dot(change, factor_low, preferred_element_type=F32)
-    )
-    gram = sum_gram(transposed_product(left_low, left_low))
-    mixed = transposed_product(moment, left_low) + transposed_product(change, left_low)
-    inverse = inverse_factor(gram)
-    ortho_low = jnp.dot(left_low.astype(F32), inverse.T, precision=high).astype(LOW)
-    right = scatter_right(jnp.dot(mixed, inverse.T, precision=high)) / replicas
-    right_low = gather_right(right.astype(LOW))
-    right = right_low.astype(F32)
-    square_sums = jnp.sum(right * right, axis=0)
+    left_low = sum_left(left_product(moment, change, factor.astype(LOW)))
+    left_turned = left_low.T
+    gram = sum_gram(jnp.dot(left_turned, left_low, preferred_element_type=F32))
+    mixed_high, mixed_low = mixed_product(left_turned, moment, change)
+    inverse, right = apply_inverse(gram, mixed_high, mixed_low)
+    ortho_low = jnp.dot(
+        left_low.astype(F32), inverse.T, precision=lax.Precision.HIGH
+    ).astype(LOW)
+    right = scatter_right(right) / replicas
+    rounds = gather_rounds(gather_fsdp(right.astype(LOW)))
+    new_momentum = None
+    all_places = []
+    all_pieces = []
+    sums = {}
+    for new in rounds:
+        places = jnp.stack([jnp.asarray(place, jnp.int32) for place, _, _, _ in new])
+        pieces = jnp.stack([piece for _, _, _, piece in new])
+        for _, turn, mask, piece in new:
+            wide = piece.astype(F32)
+            sums[turn, mask] = jnp.sum(wide * wide, axis=1, keepdims=True)
+        new_momentum = feedback_columns(
+            places, ortho_low, pieces, momentum, gradient, new_momentum
+        )
+        all_places.append(places)
+        all_pieces.append(pieces)
+    square_sums = tree_sum([sums[key] for key in sorted(sums)])
     for bit in bits_of("tensor"):
         square_sums = square_sums + swap(square_sums, "tensor", 1 << bit)
-    new_factor = right / jnp.sqrt(square_sums / all_cols + 1e-06)
-    feedback = jnp.dot(ortho_low, right_low.T, preferred_element_type=F32)
-    new_momentum = (moment.astype(F32) + change.astype(F32) - 0.05 * feedback)[None]
-    step_scale = jnp.sqrt(F32(all_rows / factor.shape[1]))
-    step_direction = (
-        step_scale
-        * jnp.dot(ortho_low, new_factor.astype(LOW).T, preferred_element_type=F32)
-    ).astype(LOW)
+    norms = jnp.sqrt(square_sums / all_cols + 1e-06)
+    scale = (all_rows / factor.shape[1]) ** 0.5
+    step_direction, new_factor = step_outputs(
+        jnp.concatenate(all_places), ortho_low, jnp.concatenate(all_pieces), norms, scale
+    )
     return (new_momentum, step_direction, new_factor)
 
 

time: 199 us -> 220 us (1.11)
  Pallas kernels: 9.05 us -> 86.3 us
  matrix products: 75.3 us -> 1.54 us
  local copies, waits for them, and re-layouts: 4.53 us -> 23.6 us
  waiting for transfers between devices: 65.5 us -> 61.5 us
  starting transfers between devices: 31.6 us -> 34.9 us
  other arithmetic: 11.9 us -> 9.15 us
    pallas_call x1 -> x7, Pallas kernels: 9.05 us -> 86.3 us  [the longest x3 27.8 us: feedback_columns(): pl.pallas_call(feedback_kernel, grid_spec=pltpu.PrefetchScalarGridSpec(nu...]
    dot_general x9 -> x2, matrix products: 75.3 us -> 1.54 us  [the longest x1 1.01 us: local(): jnp.dot(left_low.astype(F32), inverse.T, precision=lax.Precision.HIGH)]
    unnamed x26 -> x15, local copies, waits for them, and re-layouts: 2.34 us -> 18.1 us
    ppermute x25 -> x27, waiting for transfers between devices: 65.5 us -> 61.5 us  [swap(): return lax.ppermute(x, axis, [(i, i ^ mask) for i in range(size)])]
    ppermute x25 -> x27, starting transfers between devices: 31.6 us -> 34.9 us  [swap(): return lax.ppermute(x, axis, [(i, i ^ mask) for i in range(size)])]
    select_n x5 -> x1, other arithmetic: 3.16 us -> 0.02 us  [unhalve(): jnp.where(mine == 0, jnp.concatenate([x, other]), jnp.concatenate([other,...]
    convert_element_type x2, other arithmetic: 0.12 us -> 2.47 us  [the longest x1 2.39 us: local(): left_low = sum_left(left_product(moment, change, factor.astype(LOW)))]
    div x1 -> x0, other arithmetic: 2.3 us -> none  [local(): new_factor = right / jnp.sqrt(square_sums / all_cols + 1e-06)]
  transfers between devices with their start and end apart: 25 -> 27, of which waited for: 16 -> 17; matrix products, arithmetic and copies ran while one was open for 23% -> 3% of each run, Pallas kernels for 0% -> 15%
where the time goes in v2:
time: 220 us; the launch traced here: 218 us
  Pallas kernels  86.3 us (39%)
  waiting for transfers between devices  61.5 us (28%)
  starting transfers between devices  34.9 us (16%)
  local copies, waits for them, and re-layouts  23.6 us (11%)
  other arithmetic  9.15 us (4%)
    ppermute x27, waiting for transfers between devices, swap(): return lax.ppermute(x, axis, [(i, i ^ mask) for i in range(size)])  61.5 us
    ppermute x27, starting transfers between devices, swap(): return lax.ppermute(x, axis, [(i, i ^ mask) for i in range(size)])  34.9 us
    pallas_call x3, Pallas kernels, feedback_columns(): pl.pallas_call(feedback_kernel, grid_spec=pltpu.PrefetchScalarGridSpec(nu...  27.8 us
    pallas_call x1, Pallas kernels, mixed_product(): pl.pallas_call(mixed_kernel, grid=(columns // tile,), in_specs=[pl.BlockS...  18.5 us
    unnamed x15, local copies, waits for them, and re-layouts  18.1 us
    pallas_call x1, Pallas kernels, left_product(): pl.pallas_call(left_kernel, grid=(rows // tile,), in_specs=[pl.BlockSpec(...  17.2 us
    pallas_call x1, Pallas kernels, step_outputs(): pl.pallas_call(functools.partial(step_kernel, scale), grid_spec=pltpu.Pre...  13.7 us
    pallas_call x1, Pallas kernels, apply_inverse(): pl.pallas_call(functools.partial(apply_kernel, 32, 16), out_shape=(jax.Sh...  9.12 us
  transfers between devices with their start and end apart: 27, of which 17 were waited for; matrix products, arithmetic and copies ran while one was open for 3% of the time, Pallas kernels for 15%

profile of v2, /device:TPU:1, one launch (start us, length us, event | category | flops | bytes accessed | tf_op | source)
XLA Modules:
  0.0 218.1 jit_solution(5243095761543524207)
XLA Ops:
  3.0 5.8 %copy-done = bf16[1,2048,4096]{2,1,0:T(8,128)(2,1)S(1)} copy-done((bf16[1,2048,4096]{2,1,0:T(8,128)(2,1)S(1)}, bf16[1,2048,4096]{2,1,0:T(8,128)(2,1)}, u32[]{:S(2)}) %copy-start) | copy-done | bytes 16777240
  8.8 17.2 %shard_map.58 = f32[2048,256]{1,0:T(8,128)S(1)} custom-call(bf16[2048,4096]{1,0:T(8,128)(2,1)S(1)} %bitcast.30, bf16[2048,4096]{1,0:T(8,128)(2,1)} %bitcast.32, bf16[4096,256]{1,0:T(8,128)(2,1)S(1)} %convert_element_type.105.factor_ref), custom_call_target="tpu_custom_call" | custom-call | flops 8589934592 | bytes 33554432 | tf_op jit(solution)/shard_map/pallas_call | solution.py:116
  26.9 2.4 %collective-permute-done = f32[1024,256]{0,1:T(8,128)} collective-permute-done((f32[1024,256]{0,1:T(8,128)S(1)}, f32[1024,256]{0,1:T(8,128)}, u32[]{:S(2)}, u32[]{:S(2)}) %collective-permute-start) | collective-permute-done | bytes 1048608 | tf_op jit(solution)/shard_map/ppermute | solution.py:255
  30.8 2.4 %collective-permute-start.1 = (bf16[512,256]{0,1:T(8,128)(2,1)S(1)}, bf16[512,256]{0,1:T(8,128)(2,1)S(1)}, u32[]{:S(2)}, u32[]{:S(2)}) collective-permute-start(bf16[512,256]{0,1:T(8,128)(2,1)S(1)} %get-tuple-element.35), channel_id=1, source_target_pairs={{0,8},{8,0},{16,24},{24,16},{1,9},{9,1},{17,25},{25,17},{2,10},{10... | collective-permute-start | bytes 786440 | tf_op jit(solution)/shard_map/ppermute | solution.py:255
  34.4 5.2 %collective-permute-done.1 = bf16[512,256]{0,1:T(8,128)(2,1)S(1)} collective-permute-done((bf16[512,256]{0,1:T(8,128)(2,1)S(1)}, bf16[512,256]{0,1:T(8,128)(2,1)S(1)}, u32[]{:S(2)}, u32[]{:S(2)}) %collective-permute-start.1) | collective-permute-done | bytes 262176 | tf_op jit(solution)/shard_map/ppermute | solution.py:255
  42.2 4.7 %collective-permute-done.4 = bf16[512,256]{0,1:T(8,128)(2,1)S(1)} collective-permute-done((bf16[512,256]{0,1:T(8,128)(2,1)S(1)}, bf16[512,256]{0,1:T(8,128)(2,1)S(1)}, u32[]{:S(2)}, u32[]{:S(2)}) %collective-permute-start.4) | collective-permute-done | bytes 262176 | tf_op jit(solution)/shard_map/ppermute | solution.py:255
  47.5 2.5 %collective-permute-start.5 = (bf16[1024,256]{0,1:T(8,128)(2,1)S(1)}, bf16[1024,256]{0,1:T(8,128)(2,1)S(1)}, u32[]{:S(2)}, u32[]{:S(2)}) collective-permute-start(bf16[1024,256]{0,1:T(8,128)(2,1)S(1)} %fusion), channel_id=1, source_target_pairs={{0,1},{1,0},{2,3},{3,2},{4,5},{5,4},{6,7},{7,6},{8,9},{9,8},{10,11... | collective-permute-start | bytes 1572872 | tf_op jit(solution)/shard_map/ppermute | solution.py:255
  56.0 7.4 %collective-permute-done.7 = f32[128,256]{1,0:T(8,128)S(1)} collective-permute-done((f32[128,256]{1,0:T(8,128)S(1)}, f32[128,256]{1,0:T(8,128)S(1)}, u32[]{:S(2)}, u32[]{:S(2)}) %collective-permute-start.7) | collective-permute-done | bytes 131104 | tf_op jit(solution)/shard_map/ppermute | solution.py:255
  66.0 5.8 %copy-done.1 = bf16[1,2048,4096]{2,1,0:T(8,128)(2,1)S(1)} copy-done((bf16[1,2048,4096]{2,1,0:T(8,128)(2,1)S(1)}, bf16[1,2048,4096]{2,1,0:T(8,128)(2,1)}, u32[]{:S(2)}) %copy-start.1) | copy-done | bytes 16777240
  71.8 18.5 %shard_map.59 = (bf16[256,4096]{1,0:T(8,128)(2,1)S(1)}, bf16[256,4096]{1,0:T(8,128)(2,1)S(1)}) custom-call(bf16[256,2048]{1,0:T(8,128)(2,1)S(1)} %fusion.4.left_ref, bf16[2048,4096]{1,0:T(8,128)(2,1)S(1)} %bitcast.31, bf16[2048,4096]{1,0:T(8,128)(2,1)} %bitcast.33), custom_call_target="tpu_custom_call" | custom-call | flops 8589934592 | bytes 33554432 | tf_op jit(solution)/shard_map/pallas_call | solution.py:149
  90.3 9.1 %shard_map.60 = (f32[256,256]{1,0:T(8,128)S(1)}, f32[256,4096]{1,0:T(8,128)S(1)}) custom-call(f32[256,256]{1,0:T(8,128)S(1)} %maximum_select_fusion.1.gram_ref, bf16[256,4096]{1,0:T(8,128)(2,1)S(1)} %get-tuple-element.9.high_ref, bf16[256,4096]{1,0:T(8,128)(2,1)S(1)} %get-tuple-element.10.low_ref), custom_call_target="tpu_custom_call" | custom-call | flops 10737418240 | bytes 8388608 | tf_op jit(solution)/shard_map/pallas_call | solution.py:87
  106.7 10.4 %collective-permute-done.12 = bf16[256,1024]{1,0:T(8,128)(2,1)} collective-permute-done((bf16[256,1024]{1,0:T(8,128)(2,1)}, bf16[256,1024]{1,0:T(8,128)(2,1)}, u32[]{:S(2)}, u32[]{:S(2)}) %collective-permute-start.12) | collective-permute-done | bytes 524320 | tf_op jit(solution)/shard_map/ppermute | solution.py:255
  122.4 3.4 %collective-permute-done.13 = bf16[256,512]{1,0:T(8,128)(2,1)S(1)} collective-permute-done((bf16[256,512]{1,0:T(8,128)(2,1)S(1)}, bf16[256,512]{1,0:T(8,128)(2,1)S(1)}, u32[]{:S(2)}, u32[]{:S(2)}) %collective-permute-start.13) | collective-permute-done | bytes 262176 | tf_op jit(solution)/shard_map/ppermute | solution.py:255
  128.0 3.3 %collective-permute-start.16 = (bf16[256,256]{1,0:T(8,128)(2,1)S(1)}, bf16[256,256]{1,0:T(8,128)(2,1)S(1)}, u32[]{:S(2)}, u32[]{:S(2)}) collective-permute-start(bf16[256,256]{1,0:T(8,128)(2,1)S(1)} %pad_maximum_fusion.7), channel_id=1, source_target_pairs={{0,6},{2,4},{4,2},{6,0},{1,7},{3,5},{5,3},{7,1},{8,14},{10,12},{12... | collective-permute-start | bytes 393224 | tf_op jit(solution)/shard_map/ppermute | solution.py:255
  133.8 8.8 %collective-permute-done.15 = bf16[256,256]{1,0:T(8,128)(2,1)S(1)} collective-permute-done((bf16[256,256]{1,0:T(8,128)(2,1)S(1)}, bf16[256,256]{1,0:T(8,128)(2,1)S(1)}, u32[]{:S(2)}, u32[]{:S(2)}) %collective-permute-start.15) | collective-permute-done | bytes 131104 | tf_op jit(solution)/shard_map/ppermute | solution.py:255
  142.7 3.6 %collective-permute-start.17 = (bf16[256,256]{1,0:T(8,128)(2,1)S(1)}, bf16[256,256]{1,0:T(8,128)(2,1)S(1)}, u32[]{:S(2)}, u32[]{:S(2)}) collective-permute-start(bf16[256,256]{1,0:T(8,128)(2,1)S(1)} %fusion.3), channel_id=1, source_target_pairs={{0,6},{2,4},{4,2},{6,0},{1,7},{3,5},{5,3},{7,1},{8,14},{10,12},{12... | collective-permute-start | bytes 393224 | tf_op jit(solution)/shard_map/ppermute | solution.py:255
  148.8 7.3 %collective-permute-done.18 = bf16[256,256]{1,0:T(8,128)(2,1)S(1)} collective-permute-done((bf16[256,256]{1,0:T(8,128)(2,1)S(1)}, bf16[256,256]{1,0:T(8,128)(2,1)S(1)}, u32[]{:S(2)}, u32[]{:S(2)}) %collective-permute-start.18) | collective-permute-done | bytes 131104 | tf_op jit(solution)/shard_map/ppermute | solution.py:255
  159.7 5.8 %copy-done.2 = bf16[1,2048,4096]{2,1,0:T(8,128)(2,1)S(1)} copy-done((bf16[1,2048,4096]{2,1,0:T(8,128)(2,1)S(1)}, bf16[1,2048,4096]{2,1,0:T(8,128)(2,1)}, u32[]{:S(2)}) %copy-start.2) | copy-done | bytes 16777240
  165.4 7.4 %shard_map.61.refs_0_ = f32[1,2048,4096]{2,1,0:T(8,128)} custom-call(s32[2]{0:T(128)S(1)} %pad_add_fusion.2.place_ref, bf16[2048,256]{1,0:T(8,128)(2,1)S(1)} %convolution_convert_fusion.ortho_ref, bf16[2,256,512]{2,1,0:T(8,128)(2,1)S(1)} %pad_maximum_fusion.2.right_ref, bf16[1,2048,4096]{2,1,0:T(8,128)(2,1)S(1)} %copy-done.2, bf16[1,2048,4096]{2,1,0:T(8,128)(2,1)} %change_ref.5), custom_call_target="tpu_custom_call" | custom-call | flops 1073741824 | bytes 16777216 | tf_op jit(solution)/shard_map/pallas_call | solution.py:196
  173.1 13.0 %shard_map.62.refs_0_ = f32[1,2048,4096]{2,1,0:T(8,128)} custom-call(s32[4]{0:T(128)S(1)} %pad_add_fusion.1.place_ref, bf16[2048,256]{1,0:T(8,128)(2,1)S(1)} %convolution_convert_fusion.ortho_ref, bf16[4,256,512]{2,1,0:T(8,128)(2,1)S(1)} %pad_maximum_fusion.right_ref, bf16[1,2048,4096]{2,1,0:T(8,128)(2,1)S(1)} %copy-done.2, ...), custom_call_target="tpu_custom_call", output_to_operand_aliasing={{}: (5, {})} | custom-call | flops 2147483648 | bytes 33554432 | tf_op jit(solution)/shard_map/pallas_call | solution.py:196
  188.2 3.0 %collective-permute-done.23 = bf16[256,512]{1,0:T(8,128)(2,1)S(1)} collective-permute-done((bf16[256,512]{1,0:T(8,128)(2,1)S(1)}, bf16[256,512]{1,0:T(8,128)(2,1)S(1)}, u32[]{:S(2)}, u32[]{:S(2)}) %collective-permute-start.23) | collective-permute-done | bytes 262176 | tf_op jit(solution)/shard_map/ppermute | solution.py:255
  192.9 3.8 %collective-permute-start.26 = (f32[256,1]{0,1:T(1,128)S(1)}, f32[256,1]{0,1:T(1,128)S(1)}, u32[]{:S(2)}, u32[]{:S(2)}) collective-permute-start(f32[256,1]{0,1:T(1,128)S(1)} %bitcast.42), channel_id=1, source_target_pairs={{0,1},{1,0},{2,3},{3,2},{4,5},{5,4},{6,7},{7,6},{8,9},{9,8},{10,11... | collective-permute-start | bytes 3080 | tf_op jit(solution)/shard_map/ppermute | solution.py:255
  196.8 7.4 %shard_map.63 = f32[1,2048,4096]{2,1,0:T(8,128)} custom-call(s32[2]{0:T(128)S(1)} %pad_add_fusion.place_ref, bf16[2048,256]{1,0:T(8,128)(2,1)S(1)} %convolution_convert_fusion.ortho_ref, bf16[2,256,512]{2,1,0:T(8,128)(2,1)S(1)} %pad_maximum_fusion.1.right_ref, bf16[1,2048,4096]{2,1,0:T(8,128)(2,1)S(1)} %copy-done.2, ...), custom_call_target="tpu_custom_call", output_to_operand_aliasing={{}: (5, {})} | custom-call | flops 1073741824 | bytes 16777216 | tf_op jit(solution)/shard_map/pallas_call | solution.py:196
  204.4 13.7 %shard_map.64 = (bf16[2048,4096]{1,0:T(8,128)(2,1)}, f32[4096,256]{1,0:T(8,128)}) custom-call(s32[8]{0:T(128)S(1)} %concatenate.55.place_ref, bf16[2048,256]{1,0:T(8,128)(2,1)S(1)} %convolution_convert_fusion.ortho_ref, bf16[8,256,512]{2,1,0:T(8,128)(2,1)S(1)} %constant_dynamic-update-slice_fusion.right_ref, f32[256,1]{1,0:T(8,128)S(1)} %sqrt.3.norm_ref), custom_call_target="tpu_custom_call" | custom-call | flops 4294967296 | bytes 16777216 | tf_op jit(solution)/shard_map/pallas_call | solution.py:223
  (106 shorter events, 45.2 us)
Async XLA Ops:
  30.8 8.8 %collective-permute-start.1 = (bf16[512,256]{0,1:T(8,128)(2,1)S(1)}, bf16[512,256]{0,1:T(8,128)(2,1)S(1)}, u32[]{:S(2)}, u32[]{:S(2)}) collective-permute-start(bf16[512,256]{0,1:T(8,128)(2,1)S(1)} %get-tuple-element.35), channel_id=1, source_target_pairs={{0,8},{8,0},{16,24},{24,16},{1,9},{9,1},{17,25},{25,17},{2,10},{10... | collective-permute-start | bytes 786440 | tf_op jit(solution)/shard_map/ppermute | solution.py:255
  33.2 7.2 %collective-permute-start.3 = (bf16[512,256]{0,1:T(8,128)(2,1)S(1)}, bf16[512,256]{0,1:T(8,128)(2,1)S(1)}, u32[]{:S(2)}, u32[]{:S(2)}) collective-permute-start(bf16[512,256]{0,1:T(8,128)(2,1)S(1)} %get-tuple-element.36), channel_id=1, source_target_pairs={{0,16},{8,24},{16,0},{24,8},{1,17},{9,25},{17,1},{25,9},{2,18},{10... | collective-permute-start | bytes 786440 | tf_op jit(solution)/shard_map/ppermute | solution.py:255
  40.5 6.3 %collective-permute-start.4 = (bf16[512,256]{0,1:T(8,128)(2,1)S(1)}, bf16[512,256]{0,1:T(8,128)(2,1)S(1)}, u32[]{:S(2)}, u32[]{:S(2)}) collective-permute-start(bf16[512,256]{0,1:T(8,128)(2,1)S(1)} %get-tuple-element.34), channel_id=1, source_target_pairs={{0,8},{8,0},{16,24},{24,16},{1,9},{9,1},{17,25},{25,17},{2,10},{10... | collective-permute-start | bytes 786440 | tf_op jit(solution)/shard_map/ppermute | solution.py:255
  41.0 6.3 %collective-permute-start.2 = (bf16[512,256]{0,1:T(8,128)(2,1)S(1)}, bf16[512,256]{0,1:T(8,128)(2,1)S(1)}, u32[]{:S(2)}, u32[]{:S(2)}) collective-permute-start(bf16[512,256]{0,1:T(8,128)(2,1)S(1)} %get-tuple-element.33), channel_id=1, source_target_pairs={{0,16},{8,24},{16,0},{24,8},{1,17},{9,25},{17,1},{25,9},{2,18},{10... | collective-permute-start | bytes 786440 | tf_op jit(solution)/shard_map/ppermute | solution.py:255
  52.0 11.3 %collective-permute-start.7 = (f32[128,256]{1,0:T(8,128)S(1)}, f32[128,256]{1,0:T(8,128)S(1)}, u32[]{:S(2)}, u32[]{:S(2)}) collective-permute-start(f32[128,256]{1,0:T(8,128)S(1)} %constant_dynamic-slice_fusion.2), channel_id=1, source_target_pairs={{0,4},{2,6},{4,0},{6,2},{1,5},{3,7},{5,1},{7,3},{8,12},{10,14},{12... | collective-permute-start | bytes 393224 | tf_op jit(solution)/shard_map/ppermute | solution.py:255
  54.3 9.0 %collective-permute-start.8 = (f32[128,256]{1,0:T(8,128)S(1)}, f32[128,256]{1,0:T(8,128)S(1)}, u32[]{:S(2)}, u32[]{:S(2)}) collective-permute-start(f32[128,256]{1,0:T(8,128)S(1)} %constant_dynamic-slice_fusion.2), channel_id=1, source_target_pairs={{0,6},{2,4},{4,2},{6,0},{1,7},{3,5},{5,3},{7,1},{8,14},{10,12},{12... | collective-permute-start | bytes 393224 | tf_op jit(solution)/shard_map/ppermute | solution.py:255
  55.4 8.3 %collective-permute-start.6 = (f32[128,256]{1,0:T(8,128)S(1)}, f32[128,256]{1,0:T(8,128)S(1)}, u32[]{:S(2)}, u32[]{:S(2)}) collective-permute-start(f32[128,256]{1,0:T(8,128)S(1)} %constant_dynamic-slice_fusion.2), channel_id=1, source_target_pairs={{0,2},{2,0},{4,6},{6,4},{1,3},{3,1},{5,7},{7,5},{8,10},{10,8},{12,... | collective-permute-start | bytes 393224 | tf_op jit(solution)/shard_map/ppermute | solution.py:255
  63.8 26.5 %collective-permute-start.9 = (f32[128,256]{1,0:T(8,128)S(1)}, f32[128,256]{1,0:T(8,128)S(1)}, u32[]{:S(2)}, u32[]{:S(2)}) collective-permute-start(f32[128,256]{1,0:T(8,128)S(1)} %add_add_fusion), channel_id=1, source_target_pairs={{0,1},{1,0},{2,3},{3,2},{4,5},{5,4},{6,7},{7,6},{8,9},{9,8},{10,11... | collective-permute-start | bytes 393224 | tf_op jit(solution)/shard_map/ppermute | solution.py:255
  103.3 13.9 %collective-permute-start.12 = (bf16[256,1024]{1,0:T(8,128)(2,1)}, bf16[256,1024]{1,0:T(8,128)(2,1)}, u32[]{:S(2)}, u32[]{:S(2)}) collective-permute-start(bf16[256,1024]{1,0:T(8,128)(2,1)} %dynamic-slice_convert_fusion), channel_id=1, source_target_pairs={{0,16},{8,24},{16,0},{24,8},{1,17},{9,25},{17,1},{25,9},{2,18},{10... | collective-permute-start | bytes 1572872 | tf_op jit(solution)/shard_map/ppermute | solution.py:255
  105.3 14.5 %collective-permute-start.10 = (bf16[256,1024]{1,0:T(8,128)(2,1)}, bf16[256,1024]{1,0:T(8,128)(2,1)}, u32[]{:S(2)}, u32[]{:S(2)}) collective-permute-start(bf16[256,1024]{1,0:T(8,128)(2,1)} %dynamic-slice_convert_fusion.1), channel_id=1, source_target_pairs={{0,8},{8,0},{16,24},{24,16},{1,9},{9,1},{17,25},{25,17},{2,10},{10... | collective-permute-start | bytes 1572872 | tf_op jit(solution)/shard_map/ppermute | solution.py:255
  118.7 7.1 %collective-permute-start.13 = (bf16[256,512]{1,0:T(8,128)(2,1)S(1)}, bf16[256,512]{1,0:T(8,128)(2,1)S(1)}, u32[]{:S(2)}, u32[]{:S(2)}) collective-permute-start(bf16[256,512]{1,0:T(8,128)(2,1)S(1)} %dynamic-slice_convert_fusion.2), channel_id=1, source_target_pairs={{0,8},{8,0},{16,24},{24,16},{1,9},{9,1},{17,25},{25,17},{2,10},{10... | collective-permute-start | bytes 786440 | tf_op jit(solution)/shard_map/ppermute | solution.py:255
  121.1 6.8 %collective-permute-start.11 = (bf16[256,512]{1,0:T(8,128)(2,1)S(1)}, bf16[256,512]{1,0:T(8,128)(2,1)S(1)}, u32[]{:S(2)}, u32[]{:S(2)}) collective-permute-start(bf16[256,512]{1,0:T(8,128)(2,1)S(1)} %dynamic-slice_convert_fusion.3), channel_id=1, source_target_pairs={{0,16},{8,24},{16,0},{24,8},{1,17},{9,25},{17,1},{25,9},{2,18},{10... | collective-permute-start | bytes 786440 | tf_op jit(solution)/shard_map/ppermute | solution.py:255
  128.0 5.8 %collective-permute-start.16 = (bf16[256,256]{1,0:T(8,128)(2,1)S(1)}, bf16[256,256]{1,0:T(8,128)(2,1)S(1)}, u32[]{:S(2)}, u32[]{:S(2)}) collective-permute-start(bf16[256,256]{1,0:T(8,128)(2,1)S(1)} %pad_maximum_fusion.7), channel_id=1, source_target_pairs={{0,6},{2,4},{4,2},{6,0},{1,7},{3,5},{5,3},{7,1},{8,14},{10,12},{12... | collective-permute-start | bytes 393224 | tf_op jit(solution)/shard_map/ppermute | solution.py:255
  131.3 11.3 %collective-permute-start.15 = (bf16[256,256]{1,0:T(8,128)(2,1)S(1)}, bf16[256,256]{1,0:T(8,128)(2,1)S(1)}, u32[]{:S(2)}, u32[]{:S(2)}) collective-permute-start(bf16[256,256]{1,0:T(8,128)(2,1)S(1)} %pad_maximum_fusion.6), channel_id=1, source_target_pairs={{0,4},{2,6},{4,0},{6,2},{1,5},{3,7},{5,1},{7,3},{8,12},{10,14},{12... | collective-permute-start | bytes 393224 | tf_op jit(solution)/shard_map/ppermute | solution.py:255
  132.0 10.7 %collective-permute-start.14 = (bf16[256,256]{1,0:T(8,128)(2,1)S(1)}, bf16[256,256]{1,0:T(8,128)(2,1)S(1)}, u32[]{:S(2)}, u32[]{:S(2)}) collective-permute-start(bf16[256,256]{1,0:T(8,128)(2,1)S(1)} %pad_maximum_fusion.5), channel_id=1, source_target_pairs={{0,2},{2,0},{4,6},{6,4},{1,3},{3,1},{5,7},{7,5},{8,10},{10,8},{12,... | collective-permute-start | bytes 393224 | tf_op jit(solution)/shard_map/ppermute | solution.py:255
  142.7 6.1 %collective-permute-start.17 = (bf16[256,256]{1,0:T(8,128)(2,1)S(1)}, bf16[256,256]{1,0:T(8,128)(2,1)S(1)}, u32[]{:S(2)}, u32[]{:S(2)}) collective-permute-start(bf16[256,256]{1,0:T(8,128)(2,1)S(1)} %fusion.3), channel_id=1, source_target_pairs={{0,6},{2,4},{4,2},{6,0},{1,7},{3,5},{5,3},{7,1},{8,14},{10,12},{12... | collective-permute-start | bytes 393224 | tf_op jit(solution)/shard_map/ppermute | solution.py:255
  146.3 9.8 %collective-permute-start.18 = (bf16[256,256]{1,0:T(8,128)(2,1)S(1)}, bf16[256,256]{1,0:T(8,128)(2,1)S(1)}, u32[]{:S(2)}, u32[]{:S(2)}) collective-permute-start(bf16[256,256]{1,0:T(8,128)(2,1)S(1)} %fusion.3), channel_id=1, source_target_pairs={{0,4},{2,6},{4,0},{6,2},{1,5},{3,7},{5,1},{7,3},{8,12},{10,14},{12... | collective-permute-start | bytes 393224 | tf_op jit(solution)/shard_map/ppermute | solution.py:255
  146.3 9.8 %collective-permute-start.19 = (bf16[256,256]{1,0:T(8,128)(2,1)S(1)}, bf16[256,256]{1,0:T(8,128)(2,1)S(1)}, u32[]{:S(2)}, u32[]{:S(2)}) collective-permute-start(bf16[256,256]{1,0:T(8,128)(2,1)S(1)} %fusion.3), channel_id=1, source_target_pairs={{0,2},{2,0},{4,6},{6,4},{1,3},{3,1},{5,7},{7,5},{8,10},{10,8},{12,... | collective-permute-start | bytes 393224 | tf_op jit(solution)/shard_map/ppermute | solution.py:255
  156.4 16.5 %collective-permute-start.22 = (bf16[256,512]{1,0:T(8,128)(2,1)S(1)}, bf16[256,512]{1,0:T(8,128)(2,1)S(1)}, u32[]{:S(2)}, u32[]{:S(2)}) collective-permute-start(bf16[256,512]{1,0:T(8,128)(2,1)S(1)} %get-tuple-element.18), channel_id=1, source_target_pairs={{0,8},{8,0},{16,24},{24,16},{1,9},{9,1},{17,25},{25,17},{2,10},{10... | collective-permute-start | bytes 786440 | tf_op jit(solution)/shard_map/ppermute | solution.py:255
  156.8 16.1 %collective-permute-start.25 = (bf16[256,512]{1,0:T(8,128)(2,1)S(1)}, bf16[256,512]{1,0:T(8,128)(2,1)S(1)}, u32[]{:S(2)}, u32[]{:S(2)}) collective-permute-start(bf16[256,512]{1,0:T(8,128)(2,1)S(1)} %get-tuple-element.18), channel_id=1, source_target_pairs={{0,16},{8,24},{16,0},{24,8},{1,17},{9,25},{17,1},{25,9},{2,18},{10... | collective-permute-start | bytes 786440 | tf_op jit(solution)/shard_map/ppermute | solution.py:255
  158.2 14.8 %collective-permute-start.20 = (bf16[256,512]{1,0:T(8,128)(2,1)S(1)}, bf16[256,512]{1,0:T(8,128)(2,1)S(1)}, u32[]{:S(2)}, u32[]{:S(2)}) collective-permute-start(bf16[256,512]{1,0:T(8,128)(2,1)S(1)} %get-tuple-element.16), channel_id=1, source_target_pairs={{0,16},{8,24},{16,0},{24,8},{1,17},{9,25},{17,1},{25,9},{2,18},{10... | collective-permute-start | bytes 786440 | tf_op jit(solution)/shard_map/ppermute | solution.py:255
  158.4 14.5 %collective-permute-start.24 = (bf16[256,512]{1,0:T(8,128)(2,1)S(1)}, bf16[256,512]{1,0:T(8,128)(2,1)S(1)}, u32[]{:S(2)}, u32[]{:S(2)}) collective-permute-start(bf16[256,512]{1,0:T(8,128)(2,1)S(1)} %get-tuple-element.16), channel_id=1, source_target_pairs={{0,8},{8,0},{16,24},{24,16},{1,9},{9,1},{17,25},{25,17},{2,10},{10... | collective-permute-start | bytes 786440 | tf_op jit(solution)/shard_map/ppermute | solution.py:255
  187.2 5.5 %collective-permute-start.21 = (bf16[256,512]{1,0:T(8,128)(2,1)S(1)}, bf16[256,512]{1,0:T(8,128)(2,1)S(1)}, u32[]{:S(2)}, u32[]{:S(2)}) collective-permute-start(bf16[256,512]{1,0:T(8,128)(2,1)S(1)} %collective-permute-done.20), channel_id=1, source_target_pairs={{0,8},{8,0},{16,24},{24,16},{1,9},{9,1},{17,25},{25,17},{2,10},{10... | collective-permute-start | bytes 786440 | tf_op jit(solution)/shard_map/ppermute | solution.py:255
  192.9 11.3 %collective-permute-start.26 = (f32[256,1]{0,1:T(1,128)S(1)}, f32[256,1]{0,1:T(1,128)S(1)}, u32[]{:S(2)}, u32[]{:S(2)}) collective-permute-start(f32[256,1]{0,1:T(1,128)S(1)} %bitcast.42), channel_id=1, source_target_pairs={{0,1},{1,0},{2,3},{3,2},{4,5},{5,4},{6,7},{7,6},{8,9},{9,8},{10,11... | collective-permute-start | bytes 3080 | tf_op jit(solution)/shard_map/ppermute | solution.py:255
  (6 other events, 29.4 us)

commit v3 on v2

--- a/solution.py
+++ b/solution.py
@@ -10,6 +10,7 @@
 F32 = jnp.float32
 LOW = jnp.bfloat16
 LANES = 128
+ROOM = 50 << 20
 COLS_OVER = (((0,), (0,)), ((), ()))
 
 
@@ -67,143 +68,182 @@
             out_ref[start : start + panel, at : at + LANES] = x * scale
 
 
-def apply_kernel(panel, group, gram_ref, high_ref, low_ref, inverse_ref, right_ref, work_ref):
-    inverse_factor_kernel(panel, group, gram_ref, inverse_ref, work_ref)
-    inverse = inverse_ref[...]
-    inverse_high = inverse.astype(LOW)
-    inverse_low = (inverse - inverse_high.astype(F32)).astype(LOW)
-    width = tile_of(high_ref.shape[1])
-    for at in range(0, high_ref.shape[1], width):
-        high = high_ref[:, at : at + width]
-        low = low_ref[:, at : at + width]
-        right_ref[:, at : at + width] = (
-            jnp.dot(inverse_high, low, preferred_element_type=F32)
-            + jnp.dot(inverse_low, high, preferred_element_type=F32)
-        ) + jnp.dot(inverse_high, high, preferred_element_type=F32)
-
-
-def apply_inverse(gram, high, low):
+def split_low(x):
+    high = x.astype(LOW)
+    return high, (x - high.astype(F32)).astype(LOW)
+
+
+def apply_halves(upper, side_ref, inverse, high_ref, low_ref, out_refs):
+    inverse_high, inverse_low = split_low(inverse)
+    half = high_ref.shape[1] // 2
+    size = half // 2
+    width = tile_of(size)
+    for turn, out_ref in enumerate(out_refs):
+        side = side_ref[turn] if upper else 1 - side_ref[turn]
+        for at in range(0, size, width):
+            start = pl.multiple_of(side * size + (turn * half + at), LANES)
+            high = high_ref[:, pl.ds(start, width)]
+            low = low_ref[:, pl.ds(start, width)]
+            product = (
+                jnp.dot(inverse_high, low, preferred_element_type=F32)
+                + jnp.dot(inverse_low, high, preferred_element_type=F32)
+            ) + jnp.dot(inverse_high, high, preferred_element_type=F32)
+            out_ref[:, at : at + width] = product.astype(out_ref.dtype)
+
+
+def sent_kernel(side_ref, gram_ref, high_ref, low_ref, inverse_ref, first_ref, second_ref, work_ref):
+    inverse_factor_kernel(32, 16, gram_ref, inverse_ref, work_ref)
+    apply_halves(False, side_ref, inverse_ref[...], high_ref, low_ref, (first_ref, second_ref))
+
+
+def kept_kernel(side_ref, inverse_ref, high_ref, low_ref, first_ref, second_ref):
+    apply_halves(True, side_ref, inverse_ref[...], high_ref, low_ref, (first_ref, second_ref))
+
+
+WHOLE = pl.BlockSpec(memory_space=pltpu.VMEM)
+SCALARS = pl.BlockSpec(memory_space=pltpu.SMEM)
+
+
+def inverse_and_sent(side, gram, high, low):
     n, columns = high.shape
-    return pl.pallas_call(
-        functools.partial(apply_kernel, 32, 16),
-        out_shape=(
-            jax.ShapeDtypeStruct((n, n), F32),
-            jax.ShapeDtypeStruct((n, columns), F32),
-        ),
+    quarter = jax.ShapeDtypeStruct((n, columns // 4), LOW)
+    return pl.pallas_call(
+        sent_kernel,
+        in_specs=[SCALARS, WHOLE, WHOLE, WHOLE],
+        out_shape=(jax.ShapeDtypeStruct((n, n), F32), quarter, quarter),
         scratch_shapes=[pltpu.VMEM((n, 2 * n), F32)],
-        compiler_params=pltpu.CompilerParams(vmem_limit_bytes=24 << 20),
-        cost_estimate=pl.CostEstimate(
-            flops=40 * n * n * columns, bytes_accessed=8 * n * columns, transcendentals=n
-        ),
-    )(gram, high, low)
+        compiler_params=pltpu.CompilerParams(vmem_limit_bytes=16 << 20),
+    )(side, gram, high, low)
+
+
+def kept_quarters(side, inverse, high, low):
+    n, columns = high.shape
+    quarter = jax.ShapeDtypeStruct((n, columns // 4), F32)
+    return pl.pallas_call(
+        kept_kernel,
+        in_specs=[SCALARS, WHOLE, WHOLE, WHOLE],
+        out_shape=(quarter, quarter),
+        compiler_params=pltpu.CompilerParams(vmem_limit_bytes=16 << 20),
+    )(side, inverse, high, low)
 
 
 def tile_of(size):
     return 256 if size % 256 == 0 else LANES
 
 
-def left_kernel(moment_ref, change_ref, factor_ref, out_ref):
-    factor = factor_ref[...]
+def left_kernel(moment_ref, change_ref, factor_ref, out_ref, low_ref):
+    @pl.when(pl.program_id(0) == 0)
+    def _():
+        low_ref[...] = factor_ref[...].astype(LOW)
+
+    factor = low_ref[...]
     out_ref[...] = jnp.dot(moment_ref[...], factor, preferred_element_type=F32) + jnp.dot(
         change_ref[...], factor, preferred_element_type=F32
     )
 
 
-def left_product(moment, change, factor_low):
+def left_product(moment, change, factor):
     rows, columns = moment.shape
-    rank = factor_low.shape[1]
-    tile = LANES
+    rank = factor.shape[1]
+    tile = min(rows, 256)
     return pl.pallas_call(
         left_kernel,
         grid=(rows // tile,),
         in_specs=[
             pl.BlockSpec((tile, columns), lambda i: (i, 0)),
             pl.BlockSpec((tile, columns), lambda i: (i, 0)),
-            pl.BlockSpec((columns, rank), lambda i: (0, 0)),
+            pl.BlockSpec((columns, rank), lambda i: (0, 0), pipeline_mode=pl.Buffered(1)),
         ],
         out_specs=pl.BlockSpec((tile, rank), lambda i: (i, 0)),
         out_shape=jax.ShapeDtypeStruct((rows, rank), F32),
-        compiler_params=pltpu.CompilerParams(vmem_limit_bytes=24 << 20),
+        scratch_shapes=[pltpu.VMEM((columns, rank), LOW)],
+        compiler_params=pltpu.CompilerParams(vmem_limit_bytes=ROOM),
         cost_estimate=pl.CostEstimate(
             flops=4 * rows * columns * rank,
             bytes_accessed=4 * rows * columns,
             transcendentals=0,
         ),
-    )(moment, change, factor_low)
-
-
-def mixed_kernel(left_ref, moment_ref, change_ref, high_ref, low_ref):
-    left = left_ref[...]
-    mixed = jnp.dot(left, moment_ref[...], preferred_element_type=F32) + jnp.dot(
-        left, change_ref[...], preferred_element_type=F32
-    )
-    high = mixed.astype(LOW)
-    high_ref[...] = high
-    low_ref[...] = (mixed - high.astype(F32)).astype(LOW)
-
-
-def mixed_product(left_turned, moment, change):
+    )(moment, change, factor)
+
+
+def mixed_product(left_low, moment, change):
+    mixed = lax.dot_general(
+        left_low, moment, COLS_OVER, preferred_element_type=F32
+    ) + lax.dot_general(left_low, change, COLS_OVER, preferred_element_type=F32)
+    return split_low(mixed)
+
+
+def total_kernel(moment_ref, change_ref, first_ref, second_ref):
+    rows, columns = moment_ref.shape
+    at = pl.multiple_of(pl.program_id(0) * rows, rows)
+    total = moment_ref[...].astype(F32) + change_ref[...].astype(F32)
+    first_ref[pl.ds(at, rows), :] = total[:, : columns // 2]
+    second_ref[pl.ds(at, rows), :] = total[:, columns // 2 :]
+
+
+def total_of(moment, change):
     rows, columns = moment.shape
-    rank = left_turned.shape[0]
-    tile = tile_of(columns)
-    return pl.pallas_call(
-        mixed_kernel,
-        grid=(columns // tile,),
-        in_specs=[
-            pl.BlockSpec((rank, rows), lambda j: (0, 0)),
-            pl.BlockSpec((rows, tile), lambda j: (0, j)),
-            pl.BlockSpec((rows, tile), lambda j: (0, j)),
-        ],
-        out_specs=[pl.BlockSpec((rank, tile), lambda j: (0, j))] * 2,
-        out_shape=[jax.ShapeDtypeStruct((rank, columns), LOW)] * 2,
-        compiler_params=pltpu.CompilerParams(vmem_limit_bytes=24 << 20),
-        cost_estimate=pl.CostEstimate(
-            flops=4 * rows * columns * rank,
-            bytes_accessed=4 * rows * columns,
-            transcendentals=0,
-        ),
-    )(left_turned, moment, change)
-
-
-def feedback_kernel(place_ref, ortho_ref, right_ref, moment_ref, change_ref, *refs):
+    tile = min(rows, 256)
+    block = pl.BlockSpec((tile, columns), lambda i: (i, 0))
+    return pl.pallas_call(
+        total_kernel,
+        grid=(rows // tile,),
+        in_specs=[block, block],
+        out_specs=[WHOLE, WHOLE],
+        out_shape=[pltpu.VMEM((rows, columns // 2), F32)] * 2,
+        compiler_params=pltpu.CompilerParams(vmem_limit_bytes=12 << 20),
+    )(moment, change)
+
+
+def feedback_kernel(steps, place_ref, ortho_ref, right_ref, first_ref, second_ref, *refs):
+    out_ref = refs[-1]
+    tile = out_ref.shape[2]
+    half = first_ref.shape[1]
+    j = pl.program_id(0)
+    at = pl.multiple_of((place_ref[j // steps] * steps + j % steps) * tile, tile)
     feedback = jnp.dot(ortho_ref[...], right_ref[0], preferred_element_type=F32)
-    refs[-1][0] = moment_ref[0].astype(F32) + change_ref[0].astype(F32) - 0.05 * feedback
-
-
-def feedback_columns(places, ortho_low, pieces, momentum, gradient, written):
+
+    @pl.when(at < half)
+    def _():
+        out_ref[0] = first_ref[:, pl.ds(pl.multiple_of(jnp.minimum(at, half - tile), tile), tile)] - 0.05 * feedback
+
+    @pl.when(at >= half)
+    def _():
+        out_ref[0] = second_ref[:, pl.ds(pl.multiple_of(jnp.maximum(at - half, 0), tile), tile)] - 0.05 * feedback
+
+
+def feedback_columns(places, ortho_low, pieces, total, written):
     count, rank, width = pieces.shape
-    _, rows, columns = momentum.shape
+    rows, columns = total[0].shape[0], 2 * total[0].shape[1]
     tile = tile_of(width)
     steps = width // tile
 
     def column(j, place):
         return (0, 0, place[j // steps] * steps + j % steps)
 
-    block = pl.BlockSpec((1, rows, tile), column)
     specs = [
         pl.BlockSpec((rows, rank), lambda j, place: (0, 0)),
         pl.BlockSpec((1, rank, tile), lambda j, place: (j // steps, 0, j % steps)),
-        block,
-        block,
+        WHOLE,
+        WHOLE,
     ]
-    operands = [places, ortho_low, pieces, momentum, gradient]
+    operands = [places, ortho_low, pieces, *total]
     aliases = {}
     if written is not None:
         specs.append(pl.BlockSpec(memory_space=pl.ANY))
         aliases = {len(operands): 0}
         operands.append(written)
-    size = count * width
-    return pl.pallas_call(
-        feedback_kernel,
+    return pl.pallas_call(
+        functools.partial(feedback_kernel, steps),
         grid_spec=pltpu.PrefetchScalarGridSpec(
-            num_scalar_prefetch=1, grid=(count * steps,), in_specs=specs, out_specs=block
+            num_scalar_prefetch=1,
+            grid=(count * steps,),
+            in_specs=specs,
+            out_specs=pl.BlockSpec((1, rows, tile), column),
         ),
-        out_shape=jax.ShapeDtypeStruct(momentum.shape, F32),
+        out_shape=jax.ShapeDtypeStruct((1, rows, columns), F32),
         input_output_aliases=aliases,
-        compiler_params=pltpu.CompilerParams(vmem_limit_bytes=24 << 20),
-        cost_estimate=pl.CostEstimate(
-            flops=2 * rows * rank * size, bytes_accessed=8 * rows * size, transcendentals=0
-        ),
+        compiler_params=pltpu.CompilerParams(vmem_limit_bytes=12 << 20),
     )(*operands)
 
 
@@ -217,7 +257,7 @@
 def step_outputs(places, ortho_low, pieces, norms, scale):
     count, rank, width = pieces.shape
     rows = ortho_low.shape[0]
-    tile = tile_of(width)
+    tile = width
     steps = width // tile
     columns = count * width
     return pl.pallas_call(
@@ -239,7 +279,7 @@
             jax.ShapeDtypeStruct((rows, columns), LOW),
             jax.ShapeDtypeStruct((columns, rank), F32),
         ],
-        compiler_params=pltpu.CompilerParams(vmem_limit_bytes=24 << 20),
+        compiler_params=pltpu.CompilerParams(vmem_limit_bytes=16 << 20),
         cost_estimate=pl.CostEstimate(
             flops=2 * rows * rank * columns, bytes_accessed=2 * rows * columns, transcendentals=0
         ),
@@ -311,11 +351,15 @@
     return [bits[turn % len(bits) :] + bits[: turn % len(bits)] for turn in range(2)]
 
 
-def scatter_right(partial):
-    half = partial.shape[1] // 2
-    parts = [partial[:, :half], partial[:, half:]]
+def scatter_right(gram, high, low):
     orders = orders_of()
-    for k in range(len(orders[0])):
+    index = lax.axis_index("dp")
+    side = jnp.stack([(index >> order[0]) & 1 for order in orders])
+    inverse, *sent = inverse_and_sent(side, gram, high, low)
+    come = [swap(x, "dp", 1 << order[0]) for x, order in zip(sent, orders)]
+    kept = kept_quarters(side, inverse, high, low)
+    parts = [a + b.astype(F32) for a, b in zip(kept, come)]
+    for k in range(1, len(orders[0])):
         parts = [
             halve(part, "dp", order[k], LOW, 1) for part, order in zip(parts, orders)
         ]
@@ -331,7 +375,7 @@
     terms = [share(index)]
     for k in range(1, size):
         terms.append(swap(share(index ^ k).astype(LOW), "fsdp", k).astype(F32))
-    return tree_sum(terms)
+    return inverse, tree_sum(terms)
 
 
 def gather_fsdp(low):
@@ -377,16 +421,18 @@
     change = gradient[0]
     all_rows = moment.shape[0] * lax.axis_size("fsdp")
     all_cols = moment.shape[1] * lax.axis_size("tensor")
-    left_low = sum_left(left_product(moment, change, factor.astype(LOW)))
-    left_turned = left_low.T
-    gram = sum_gram(jnp.dot(left_turned, left_low, preferred_element_type=F32))
-    mixed_high, mixed_low = mixed_product(left_turned, moment, change)
-    inverse, right = apply_inverse(gram, mixed_high, mixed_low)
+    left_low = sum_left(left_product(moment, change, factor))
+    gram = sum_gram(
+        lax.dot_general(left_low, left_low, COLS_OVER, preferred_element_type=F32)
+    )
+    mixed_high, mixed_low = mixed_product(left_low, moment, change)
+    inverse, right = scatter_right(gram, mixed_high, mixed_low)
     ortho_low = jnp.dot(
         left_low.astype(F32), inverse.T, precision=lax.Precision.HIGH
     ).astype(LOW)
-    right = scatter_right(right) / replicas
-    rounds = gather_rounds(gather_fsdp(right.astype(LOW)))
+    moment, change, _ = lax.optimization_barrier((moment, change, inverse))
+    total = total_of(moment, change)
+    rounds = gather_rounds(gather_fsdp((right / replicas).astype(LOW)))
     new_momentum = None
     all_places = []
     all_pieces = []
@@ -398,7 +444,7 @@
             wide = piece.astype(F32)
             sums[turn, mask] = jnp.sum(wide * wide, axis=1, keepdims=True)
         new_momentum = feedback_columns(
-            places, ortho_low, pieces, momentum, gradient, new_momentum
+            places, ortho_low, pieces, total, new_momentum
         )
         all_places.append(places)
         all_pieces.append(pieces)

time: 220 us -> 181 us (0.82)
  local copies, waits for them, and re-layouts: 23.6 us -> 4.09 us
  matrix products: 1.54 us -> 20.5 us
  waiting for transfers between devices: 61.5 us -> 44.9 us
  Pallas kernels: 86.3 us -> 72.1 us
  starting transfers between devices: 34.9 us -> 31.8 us
  other arithmetic: 9.15 us -> 6.14 us
    dot_general x1 -> x3, matrix products: 0.52 us -> 19.8 us  [the longest x1 11.1 us: mixed_product(): lax.dot_general(left_low, moment, COLS_OVER, preferred_element_type=F32)]
    ppermute x27, waiting for transfers between devices: 61.5 us -> 44.9 us  [swap(): return lax.ppermute(x, axis, [(i, i ^ mask) for i in range(size)])]
    unnamed x15 -> x19, local copies, waits for them, and re-layouts: 18.1 us -> 3.33 us
    pallas_call x5 -> x6, Pallas kernels: 55.5 us -> 44.3 us  [the longest x3 20.7 us: feedback_columns(): pl.pallas_call(functools.partial(feedback_kernel, steps), grid_spec=pltpu...]
    ppermute x27, starting transfers between devices: 34.9 us -> 31.8 us  [swap(): return lax.ppermute(x, axis, [(i, i ^ mask) for i in range(size)])]
    pallas_call x1, Pallas kernels: 13.7 us -> 10.6 us  [step_outputs(): pl.pallas_call(functools.partial(step_kernel, scale), grid_spec=pltpu.Pre...]
    convert_element_type x4 -> x2, local copies, waits for them, and re-layouts: 3.04 us -> 0.08 us  [halve(): return kept + swap(sent.astype(dtype), axis, 1 << bit).astype(F32)]
    add x4 -> x2, other arithmetic: 2.84 us -> 0.17 us  [halve(): return kept + swap(sent.astype(dtype), axis, 1 << bit).astype(F32)]
  transfers between devices with their start and end apart: 27 -> 27, of which waited for: 17 -> 13; matrix products, arithmetic and copies ran while one was open for 3% -> 13% of each run, Pallas kernels for 15% -> 19%
where the time goes in v3:
time: 181 us
  Pallas kernels  72.1 us (40%)
  waiting for transfers between devices  44.9 us (25%)
  starting transfers between devices  31.8 us (18%)
  matrix products  20.5 us (11%)
  other arithmetic  6.14 us (3%)
  local copies, waits for them, and re-layouts  4.09 us (2%)
    ppermute x27, waiting for transfers between devices, swap(): return lax.ppermute(x, axis, [(i, i ^ mask) for i in range(size)])  44.9 us
    ppermute x27, starting transfers between devices, swap(): return lax.ppermute(x, axis, [(i, i ^ mask) for i in range(size)])  31.8 us
    pallas_call x3, Pallas kernels, feedback_columns(): pl.pallas_call(functools.partial(feedback_kernel, steps), grid_spec=pltpu...  20.7 us
    pallas_call x1, Pallas kernels, left_product(): pl.pallas_call(left_kernel, grid=(rows // tile,), in_specs=[pl.BlockSpec(...  17.2 us
    pallas_call x1, Pallas kernels, total_of(): pl.pallas_call(total_kernel, grid=(rows // tile,), in_specs=[block, block...  12.5 us
    dot_general x1, matrix products, mixed_product(): lax.dot_general(left_low, moment, COLS_OVER, preferred_element_type=F32)  11.1 us
    pallas_call x1, Pallas kernels, step_outputs(): pl.pallas_call(functools.partial(step_kernel, scale), grid_spec=pltpu.Pre...  10.6 us
    pallas_call x1, Pallas kernels, inverse_and_sent(): pl.pallas_call(sent_kernel, in_specs=[SCALARS, WHOLE, WHOLE, WHOLE], out_...  9.61 us
  transfers between devices with their start and end apart: 27, of which 13 were waited for; matrix products, arithmetic and copies ran while one was open for 13% of the time, Pallas kernels for 19%

profile of v3, /device:TPU:1, one launch (start us, length us, event | category | flops | bytes accessed | tf_op | source)
XLA Modules:
  0.0 180.6 jit_solution(14939884242309104126)
XLA Ops:
  0.6 17.2 %shard_map.58 = f32[2048,256]{1,0:T(8,128)S(1)} custom-call(bf16[2048,4096]{1,0:T(8,128)(2,1)} %bitcast.36, bf16[2048,4096]{1,0:T(8,128)(2,1)} %bitcast.38, f32[4096,256]{1,0:T(8,128)} %factor_ref.1), custom_call_target="tpu_custom_call" | custom-call | flops 8589934592 | bytes 33554432 | tf_op jit(solution)/shard_map/pallas_call | solution.py:149
  18.0 2.7 %collective-permute-done = f32[1024,256]{1,0:T(8,128)} collective-permute-done((f32[1024,256]{1,0:T(8,128)S(1)}, f32[1024,256]{1,0:T(8,128)}, u32[]{:S(2)}, u32[]{:S(2)}) %collective-permute-start) | collective-permute-done | bytes 1048608 | tf_op jit(solution)/shard_map/ppermute | solution.py:295
  22.2 2.4 %collective-permute-start.1 = (bf16[512,256]{1,0:T(8,128)(2,1)S(1)}, bf16[512,256]{1,0:T(8,128)(2,1)S(1)}, u32[]{:S(2)}, u32[]{:S(2)}) collective-permute-start(bf16[512,256]{1,0:T(8,128)(2,1)S(1)} %get-tuple-element.43), channel_id=1, source_target_pairs={{0,8},{8,0},{16,24},{24,16},{1,9},{9,1},{17,25},{25,17},{2,10},{10... | collective-permute-start | bytes 786440 | tf_op jit(solution)/shard_map/ppermute | solution.py:295
  25.9 5.1 %collective-permute-done.1 = bf16[512,256]{1,0:T(8,128)(2,1)S(1)} collective-permute-done((bf16[512,256]{1,0:T(8,128)(2,1)S(1)}, bf16[512,256]{1,0:T(8,128)(2,1)S(1)}, u32[]{:S(2)}, u32[]{:S(2)}) %collective-permute-start.1) | collective-permute-done | bytes 262176 | tf_op jit(solution)/shard_map/ppermute | solution.py:295
  33.6 4.7 %collective-permute-done.4 = bf16[512,256]{1,0:T(8,128)(2,1)S(1)} collective-permute-done((bf16[512,256]{1,0:T(8,128)(2,1)S(1)}, bf16[512,256]{1,0:T(8,128)(2,1)S(1)}, u32[]{:S(2)}, u32[]{:S(2)}) %collective-permute-start.4) | collective-permute-done | bytes 262176 | tf_op jit(solution)/shard_map/ppermute | solution.py:295
  38.9 2.5 %collective-permute-start.5 = (bf16[1024,256]{1,0:T(8,128)(2,1)S(1)}, bf16[1024,256]{1,0:T(8,128)(2,1)S(1)}, u32[]{:S(2)}, u32[]{:S(2)}) collective-permute-start(bf16[1024,256]{1,0:T(8,128)(2,1)S(1)} %fusion), channel_id=1, source_target_pairs={{0,1},{1,0},{2,3},{3,2},{4,5},{5,4},{6,7},{7,6},{8,9},{9,8},{10,11... | collective-permute-start | bytes 1572872 | tf_op jit(solution)/shard_map/ppermute | solution.py:295
  43.5 2.3 %collective-permute-start.7 = (f32[128,256]{1,0:T(8,128)S(1)}, f32[128,256]{1,0:T(8,128)S(1)}, u32[]{:S(2)}, u32[]{:S(2)}) collective-permute-start(f32[128,256]{1,0:T(8,128)S(1)} %constant_dynamic-slice_fusion.2), channel_id=1, source_target_pairs={{0,4},{2,6},{4,0},{6,2},{1,5},{3,7},{5,1},{7,3},{8,12},{10,14},{12... | collective-permute-start | bytes 393224 | tf_op jit(solution)/shard_map/ppermute | solution.py:295
  47.1 8.2 %fusion.4 = f32[256,4096]{1,0:T(8,128)S(1)} fusion(bf16[1,2048,4096]{2,1,0:T(8,128)(2,1)} %param.4, bf16[1024,256]{1,0:T(8,128)(2,1)S(1)} %collective-permute-done.5, bf16[1024,256]{1,0:T(8,128)(2,1)S(1)} %fusion, pred[]{:T(512)S(6)} %eq.10), kind=kOutput, calls=%fused_computation.71 | convolution fusion | flops 4299685888 | bytes 22020096 | tf_op jit(solution)/shard_map/dot_general | solution.py:172
  55.3 2.1 %collective-permute-start.9 = (f32[128,256]{1,0:T(8,128)S(1)}, f32[128,256]{1,0:T(8,128)S(1)}, u32[]{:S(2)}, u32[]{:S(2)}) collective-permute-start(f32[128,256]{1,0:T(8,128)S(1)} %add_add_fusion), channel_id=1, source_target_pairs={{0,1},{1,0},{2,3},{3,2},{4,5},{5,4},{6,7},{7,6},{8,9},{9,8},{10,11... | collective-permute-start | bytes 393224 | tf_op jit(solution)/shard_map/ppermute | solution.py:295
  57.5 11.1 %subtract_convert_fusion = (bf16[256,4096]{1,0:T(8,128)(2,1)S(1)}, bf16[256,4096]{1,0:T(8,128)(2,1)S(1)}) fusion(f32[256,4096]{1,0:T(8,128)S(1)} %fusion.4, bf16[1,2048,4096]{2,1,0:T(8,128)(2,1)} %param.3, bf16[1024,256]{1,0:T(8,128)(2,1)S(1)} %collective-permute-done.5, bf16[1024,256]{1,0:T(8,128)(2,1)S(1)} %fusion, pred[]{:T(512)S(6)} %eq.10), kind=kOutput, calls=%fused_computation.1 | convolution fusion | flops 4304928768 | bytes 26214400 | tf_op jit(solution)/shard_map/dot_general | solution.py:170
  68.6 9.6 %shard_map.59 = (f32[256,256]{1,0:T(8,128)S(1)}, bf16[256,1024]{1,0:T(8,128)(2,1)S(1)}, bf16[256,1024]{1,0:T(8,128)(2,1)}) custom-call(s32[2]{0:T(128)S(1)} %pad_add_fusion.1.side_ref, f32[256,256]{1,0:T(8,128)S(1)} %maximum_select_fusion.1.gram_ref, bf16[256,4096]{1,0:T(8,128)(2,1)S(1)} %get-tuple-element.30.high_ref, ...), custom_call_target="tpu_custom_call" | custom-call | tf_op jit(solution)/shard_map/pallas_call | solution.py:110
  80.9 1.6 copy-done.1
  84.0 12.5 %shard_map.61 = (f32[2048,2048]{1,0:T(8,128)S(1)}, f32[2048,2048]{1,0:T(8,128)S(1)}) custom-call(bf16[2048,4096]{1,0:T(8,128)(2,1)} %bitcast.37, bf16[2048,4096]{1,0:T(8,128)(2,1)} %bitcast.39), custom_call_target="tpu_custom_call" | custom-call | tf_op jit(solution)/shard_map/pallas_call | solution.py:188
  99.7 5.3 %collective-permute-done.13 = bf16[256,512]{1,0:T(8,128)(2,1)S(1)} collective-permute-done((bf16[256,512]{1,0:T(8,128)(2,1)S(1)}, bf16[256,512]{1,0:T(8,128)(2,1)S(1)}, u32[]{:S(2)}, u32[]{:S(2)}) %collective-permute-start.13) | collective-permute-done | bytes 262176 | tf_op jit(solution)/shard_map/ppermute | solution.py:295
  106.6 3.2 %collective-permute-start.16 = (bf16[256,256]{1,0:T(8,128)(2,1)S(1)}, bf16[256,256]{1,0:T(8,128)(2,1)S(1)}, u32[]{:S(2)}, u32[]{:S(2)}) collective-permute-start(bf16[256,256]{1,0:T(8,128)(2,1)S(1)} %pad_maximum_fusion.7), channel_id=1, source_target_pairs={{0,6},{2,4},{4,2},{6,0},{1,7},{3,5},{5,3},{7,1},{8,14},{10,12},{12... | collective-permute-start | bytes 393224 | tf_op jit(solution)/shard_map/ppermute | solution.py:295
  112.4 9.0 %collective-permute-done.15 = bf16[256,256]{1,0:T(8,128)(2,1)S(1)} collective-permute-done((bf16[256,256]{1,0:T(8,128)(2,1)S(1)}, bf16[256,256]{1,0:T(8,128)(2,1)S(1)}, u32[]{:S(2)}, u32[]{:S(2)}) %collective-permute-start.15) | collective-permute-done | bytes 131104 | tf_op jit(solution)/shard_map/ppermute | solution.py:295
  121.5 3.5 %collective-permute-start.17 = (bf16[256,256]{1,0:T(8,128)(2,1)S(1)}, bf16[256,256]{1,0:T(8,128)(2,1)S(1)}, u32[]{:S(2)}, u32[]{:S(2)}) collective-permute-start(bf16[256,256]{1,0:T(8,128)(2,1)S(1)} %fusion.3), channel_id=1, source_target_pairs={{0,6},{2,4},{4,2},{6,0},{1,7},{3,5},{5,3},{7,1},{8,14},{10,12},{12... | collective-permute-start | bytes 393224 | tf_op jit(solution)/shard_map/ppermute | solution.py:295
  127.4 7.3 %collective-permute-done.18 = bf16[256,256]{1,0:T(8,128)(2,1)S(1)} collective-permute-done((bf16[256,256]{1,0:T(8,128)(2,1)S(1)}, bf16[256,256]{1,0:T(8,128)(2,1)S(1)}, u32[]{:S(2)}, u32[]{:S(2)}) %collective-permute-start.18) | collective-permute-done | bytes 131104 | tf_op jit(solution)/shard_map/ppermute | solution.py:295
  138.3 5.5 %shard_map.62.refs_0_ = f32[1,2048,4096]{2,1,0:T(8,128)} custom-call(s32[2]{0:T(128)S(1)} %pad_add_fusion.3.place_ref, bf16[2048,256]{1,0:T(8,128)(2,1)S(1)} %convolution_convert_fusion.ortho_ref, bf16[2,256,512]{2,1,0:T(8,128)(2,1)S(1)} %pad_maximum_fusion.2.right_ref, f32[2048,2048]{1,0:T(8,128)S(1)} %get-tuple-element.21.first_ref, ...), custom_call_target="tpu_custom_call" | custom-call | tf_op jit(solution)/shard_map/pallas_call | solution.py:236
  143.8 4.1 %collective-permute-done.20 = bf16[256,512]{1,0:T(8,128)(2,1)S(1)} collective-permute-done((bf16[256,512]{1,0:T(8,128)(2,1)S(1)}, bf16[256,512]{1,0:T(8,128)(2,1)S(1)}, u32[]{:S(2)}, u32[]{:S(2)}) %collective-permute-start.20) | collective-permute-done | bytes 262176 | tf_op jit(solution)/shard_map/ppermute | solution.py:295
  149.1 9.8 %shard_map.63.refs_0_ = f32[1,2048,4096]{2,1,0:T(8,128)} custom-call(s32[4]{0:T(128)S(1)} %pad_add_fusion.2.place_ref, bf16[2048,256]{1,0:T(8,128)(2,1)S(1)} %convolution_convert_fusion.ortho_ref, bf16[4,256,512]{2,1,0:T(8,128)(2,1)S(1)} %pad_maximum_fusion.right_ref, f32[2048,2048]{1,0:T(8,128)S(1)} %get-tuple-element.21.first_ref, ...), custom_call_target="tpu_custom_call", output_to_operand_aliasing={{}: (5, {})} | custom-call | tf_op jit(solution)/shard_map/pallas_call | solution.py:236
  159.3 3.3 %collective-permute-start.26 = (f32[256,1]{0,1:T(1,128)S(1)}, f32[256,1]{0,1:T(1,128)S(1)}, u32[]{:S(2)}, u32[]{:S(2)}) collective-permute-start(f32[256,1]{0,1:T(1,128)S(1)} %bitcast.48), channel_id=1, source_target_pairs={{0,1},{1,0},{2,3},{3,2},{4,5},{5,4},{6,7},{7,6},{8,9},{9,8},{10,11... | collective-permute-start | bytes 3080 | tf_op jit(solution)/shard_map/ppermute | solution.py:295
  162.8 5.5 %shard_map.64 = f32[1,2048,4096]{2,1,0:T(8,128)} custom-call(s32[2]{0:T(128)S(1)} %pad_add_fusion.place_ref, bf16[2048,256]{1,0:T(8,128)(2,1)S(1)} %convolution_convert_fusion.ortho_ref, bf16[2,256,512]{2,1,0:T(8,128)(2,1)S(1)} %pad_maximum_fusion.1.right_ref, f32[2048,2048]{1,0:T(8,128)S(1)} %get-tuple-element.21.first_ref, ...), custom_call_target="tpu_custom_call", output_to_operand_aliasing={{}: (5, {})} | custom-call | tf_op jit(solution)/shard_map/pallas_call | solution.py:236
  170.0 10.6 %shard_map.65 = (bf16[2048,4096]{1,0:T(8,128)(2,1)}, f32[4096,256]{1,0:T(8,128)}) custom-call(s32[8]{0:T(128)S(1)} %concatenate.55.place_ref, bf16[2048,256]{1,0:T(8,128)(2,1)S(1)} %convolution_convert_fusion.ortho_ref, bf16[8,256,512]{2,1,0:T(8,128)(2,1)S(1)} %copy-done.3, f32[256,1]{1,0:T(8,128)S(1)} %sqrt.3.norm_ref), custom_call_target="tpu_custom_call" | custom-call | flops 4294967296 | bytes 16777216 | tf_op jit(solution)/shard_map/pallas_call | solution.py:263
  (109 shorter events, 30.5 us)
Async XLA Ops:
  22.2 8.8 %collective-permute-start.1 = (bf16[512,256]{1,0:T(8,128)(2,1)S(1)}, bf16[512,256]{1,0:T(8,128)(2,1)S(1)}, u32[]{:S(2)}, u32[]{:S(2)}) collective-permute-start(bf16[512,256]{1,0:T(8,128)(2,1)S(1)} %get-tuple-element.43), channel_id=1, source_target_pairs={{0,8},{8,0},{16,24},{24,16},{1,9},{9,1},{17,25},{25,17},{2,10},{10... | collective-permute-start | bytes 786440 | tf_op jit(solution)/shard_map/ppermute | solution.py:295
  24.6 7.2 %collective-permute-start.3 = (bf16[512,256]{1,0:T(8,128)(2,1)S(1)}, bf16[512,256]{1,0:T(8,128)(2,1)S(1)}, u32[]{:S(2)}, u32[]{:S(2)}) collective-permute-start(bf16[512,256]{1,0:T(8,128)(2,1)S(1)} %get-tuple-element.44), channel_id=1, source_target_pairs={{0,16},{8,24},{16,0},{24,8},{1,17},{9,25},{17,1},{25,9},{2,18},{10... | collective-permute-start | bytes 786440 | tf_op jit(solution)/shard_map/ppermute | solution.py:295
  32.0 6.3 %collective-permute-start.4 = (bf16[512,256]{1,0:T(8,128)(2,1)S(1)}, bf16[512,256]{1,0:T(8,128)(2,1)S(1)}, u32[]{:S(2)}, u32[]{:S(2)}) collective-permute-start(bf16[512,256]{1,0:T(8,128)(2,1)S(1)} %get-tuple-element.42), channel_id=1, source_target_pairs={{0,8},{8,0},{16,24},{24,16},{1,9},{9,1},{17,25},{25,17},{2,10},{10... | collective-permute-start | bytes 786440 | tf_op jit(solution)/shard_map/ppermute | solution.py:295
  32.4 6.3 %collective-permute-start.2 = (bf16[512,256]{1,0:T(8,128)(2,1)S(1)}, bf16[512,256]{1,0:T(8,128)(2,1)S(1)}, u32[]{:S(2)}, u32[]{:S(2)}) collective-permute-start(bf16[512,256]{1,0:T(8,128)(2,1)S(1)} %get-tuple-element.41), channel_id=1, source_target_pairs={{0,16},{8,24},{16,0},{24,8},{1,17},{9,25},{17,1},{25,9},{2,18},{10... | collective-permute-start | bytes 786440 | tf_op jit(solution)/shard_map/ppermute | solution.py:295
  43.5 11.8 %collective-permute-start.7 = (f32[128,256]{1,0:T(8,128)S(1)}, f32[128,256]{1,0:T(8,128)S(1)}, u32[]{:S(2)}, u32[]{:S(2)}) collective-permute-start(f32[128,256]{1,0:T(8,128)S(1)} %constant_dynamic-slice_fusion.2), channel_id=1, source_target_pairs={{0,4},{2,6},{4,0},{6,2},{1,5},{3,7},{5,1},{7,3},{8,12},{10,14},{12... | collective-permute-start | bytes 393224 | tf_op jit(solution)/shard_map/ppermute | solution.py:295
  45.8 9.5 %collective-permute-start.8 = (f32[128,256]{1,0:T(8,128)S(1)}, f32[128,256]{1,0:T(8,128)S(1)}, u32[]{:S(2)}, u32[]{:S(2)}) collective-permute-start(f32[128,256]{1,0:T(8,128)S(1)} %constant_dynamic-slice_fusion.2), channel_id=1, source_target_pairs={{0,6},{2,4},{4,2},{6,0},{1,7},{3,5},{5,3},{7,1},{8,14},{10,12},{12... | collective-permute-start | bytes 393224 | tf_op jit(solution)/shard_map/ppermute | solution.py:295
  46.9 8.4 %collective-permute-start.6 = (f32[128,256]{1,0:T(8,128)S(1)}, f32[128,256]{1,0:T(8,128)S(1)}, u32[]{:S(2)}, u32[]{:S(2)}) collective-permute-start(f32[128,256]{1,0:T(8,128)S(1)} %constant_dynamic-slice_fusion.2), channel_id=1, source_target_pairs={{0,2},{2,0},{4,6},{6,4},{1,3},{3,1},{5,7},{7,5},{8,10},{10,8},{12,... | collective-permute-start | bytes 393224 | tf_op jit(solution)/shard_map/ppermute | solution.py:295
  55.3 13.3 %collective-permute-start.9 = (f32[128,256]{1,0:T(8,128)S(1)}, f32[128,256]{1,0:T(8,128)S(1)}, u32[]{:S(2)}, u32[]{:S(2)}) collective-permute-start(f32[128,256]{1,0:T(8,128)S(1)} %add_add_fusion), channel_id=1, source_target_pairs={{0,1},{1,0},{2,3},{3,2},{4,5},{5,4},{6,7},{7,6},{8,9},{9,8},{10,11... | collective-permute-start | bytes 393224 | tf_op jit(solution)/shard_map/ppermute | solution.py:295
  78.3 18.2 %collective-permute-start.12 = (bf16[256,1024]{1,0:T(8,128)(2,1)}, bf16[256,1024]{1,0:T(8,128)(2,1)}, u32[]{:S(2)}, u32[]{:S(2)}) collective-permute-start(bf16[256,1024]{1,0:T(8,128)(2,1)} %get-tuple-element.18), channel_id=1, source_target_pairs={{0,16},{8,24},{16,0},{24,8},{1,17},{9,25},{17,1},{25,9},{2,18},{10... | collective-permute-start | bytes 1572872 | tf_op jit(solution)/shard_map/ppermute | solution.py:295
  79.6 18.6 %collective-permute-start.10 = (bf16[256,1024]{1,0:T(8,128)(2,1)S(1)}, bf16[256,1024]{1,0:T(8,128)(2,1)}, u32[]{:S(2)}, u32[]{:S(2)}) collective-permute-start(bf16[256,1024]{1,0:T(8,128)(2,1)S(1)} %get-tuple-element.16), channel_id=1, source_target_pairs={{0,8},{8,0},{16,24},{24,16},{1,9},{9,1},{17,25},{25,17},{2,10},{10... | collective-permute-start | bytes 1572872 | tf_op jit(solution)/shard_map/ppermute | solution.py:295
  97.7 7.3 %collective-permute-start.13 = (bf16[256,512]{1,0:T(8,128)(2,1)S(1)}, bf16[256,512]{1,0:T(8,128)(2,1)S(1)}, u32[]{:S(2)}, u32[]{:S(2)}) collective-permute-start(bf16[256,512]{1,0:T(8,128)(2,1)S(1)} %dynamic-slice_convert_fusion), channel_id=1, source_target_pairs={{0,8},{8,0},{16,24},{24,16},{1,9},{9,1},{17,25},{25,17},{2,10},{10... | collective-permute-start | bytes 786440 | tf_op jit(solution)/shard_map/ppermute | solution.py:295
  99.4 7.0 %collective-permute-start.11 = (bf16[256,512]{1,0:T(8,128)(2,1)S(1)}, bf16[256,512]{1,0:T(8,128)(2,1)S(1)}, u32[]{:S(2)}, u32[]{:S(2)}) collective-permute-start(bf16[256,512]{1,0:T(8,128)(2,1)S(1)} %dynamic-slice_convert_fusion.1), channel_id=1, source_target_pairs={{0,16},{8,24},{16,0},{24,8},{1,17},{9,25},{17,1},{25,9},{2,18},{10... | collective-permute-start | bytes 786440 | tf_op jit(solution)/shard_map/ppermute | solution.py:295
  109.8 11.6 %collective-permute-start.15 = (bf16[256,256]{1,0:T(8,128)(2,1)S(1)}, bf16[256,256]{1,0:T(8,128)(2,1)S(1)}, u32[]{:S(2)}, u32[]{:S(2)}) collective-permute-start(bf16[256,256]{1,0:T(8,128)(2,1)S(1)} %pad_maximum_fusion.6), channel_id=1, source_target_pairs={{0,4},{2,6},{4,0},{6,2},{1,5},{3,7},{5,1},{7,3},{8,12},{10,14},{12... | collective-permute-start | bytes 393224 | tf_op jit(solution)/shard_map/ppermute | solution.py:295
  110.5 10.9 %collective-permute-start.14 = (bf16[256,256]{1,0:T(8,128)(2,1)S(1)}, bf16[256,256]{1,0:T(8,128)(2,1)S(1)}, u32[]{:S(2)}, u32[]{:S(2)}) collective-permute-start(bf16[256,256]{1,0:T(8,128)(2,1)S(1)} %pad_maximum_fusion.5), channel_id=1, source_target_pairs={{0,2},{2,0},{4,6},{6,4},{1,3},{3,1},{5,7},{7,5},{8,10},{10,8},{12,... | collective-permute-start | bytes 393224 | tf_op jit(solution)/shard_map/ppermute | solution.py:295
  121.5 5.9 %collective-permute-start.17 = (bf16[256,256]{1,0:T(8,128)(2,1)S(1)}, bf16[256,256]{1,0:T(8,128)(2,1)S(1)}, u32[]{:S(2)}, u32[]{:S(2)}) collective-permute-start(bf16[256,256]{1,0:T(8,128)(2,1)S(1)} %fusion.3), channel_id=1, source_target_pairs={{0,6},{2,4},{4,2},{6,0},{1,7},{3,5},{5,3},{7,1},{8,14},{10,12},{12... | collective-permute-start | bytes 393224 | tf_op jit(solution)/shard_map/ppermute | solution.py:295
  124.9 9.8 %collective-permute-start.18 = (bf16[256,256]{1,0:T(8,128)(2,1)S(1)}, bf16[256,256]{1,0:T(8,128)(2,1)S(1)}, u32[]{:S(2)}, u32[]{:S(2)}) collective-permute-start(bf16[256,256]{1,0:T(8,128)(2,1)S(1)} %fusion.3), channel_id=1, source_target_pairs={{0,4},{2,6},{4,0},{6,2},{1,5},{3,7},{5,1},{7,3},{8,12},{10,14},{12... | collective-permute-start | bytes 393224 | tf_op jit(solution)/shard_map/ppermute | solution.py:295
  124.9 9.8 %collective-permute-start.19 = (bf16[256,256]{1,0:T(8,128)(2,1)S(1)}, bf16[256,256]{1,0:T(8,128)(2,1)S(1)}, u32[]{:S(2)}, u32[]{:S(2)}) collective-permute-start(bf16[256,256]{1,0:T(8,128)(2,1)S(1)} %fusion.3), channel_id=1, source_target_pairs={{0,2},{2,0},{4,6},{6,4},{1,3},{3,1},{5,7},{7,5},{8,10},{10,8},{12,... | collective-permute-start | bytes 393224 | tf_op jit(solution)/shard_map/ppermute | solution.py:295
  135.0 8.8 %collective-permute-start.22 = (bf16[256,512]{1,0:T(8,128)(2,1)S(1)}, bf16[256,512]{1,0:T(8,128)(2,1)S(1)}, u32[]{:S(2)}, u32[]{:S(2)}) collective-permute-start(bf16[256,512]{1,0:T(8,128)(2,1)S(1)} %get-tuple-element.28), channel_id=1, source_target_pairs={{0,8},{8,0},{16,24},{24,16},{1,9},{9,1},{17,25},{25,17},{2,10},{10... | collective-permute-start | bytes 786440 | tf_op jit(solution)/shard_map/ppermute | solution.py:295
  136.2 11.7 %collective-permute-start.25 = (bf16[256,512]{1,0:T(8,128)(2,1)S(1)}, bf16[256,512]{1,0:T(8,128)(2,1)S(1)}, u32[]{:S(2)}, u32[]{:S(2)}) collective-permute-start(bf16[256,512]{1,0:T(8,128)(2,1)S(1)} %get-tuple-element.28), channel_id=1, source_target_pairs={{0,16},{8,24},{16,0},{24,8},{1,17},{9,25},{17,1},{25,9},{2,18},{10... | collective-permute-start | bytes 786440 | tf_op jit(solution)/shard_map/ppermute | solution.py:295
  136.5 11.4 %collective-permute-start.20 = (bf16[256,512]{1,0:T(8,128)(2,1)S(1)}, bf16[256,512]{1,0:T(8,128)(2,1)S(1)}, u32[]{:S(2)}, u32[]{:S(2)}) collective-permute-start(bf16[256,512]{1,0:T(8,128)(2,1)S(1)} %get-tuple-element.26), channel_id=1, source_target_pairs={{0,16},{8,24},{16,0},{24,8},{1,17},{9,25},{17,1},{25,9},{2,18},{10... | collective-permute-start | bytes 786440 | tf_op jit(solution)/shard_map/ppermute | solution.py:295
  137.9 10.0 %collective-permute-start.24 = (bf16[256,512]{1,0:T(8,128)(2,1)S(1)}, bf16[256,512]{1,0:T(8,128)(2,1)S(1)}, u32[]{:S(2)}, u32[]{:S(2)}) collective-permute-start(bf16[256,512]{1,0:T(8,128)(2,1)S(1)} %get-tuple-element.26), channel_id=1, source_target_pairs={{0,8},{8,0},{16,24},{24,16},{1,9},{9,1},{17,25},{25,17},{2,10},{10... | collective-permute-start | bytes 786440 | tf_op jit(solution)/shard_map/ppermute | solution.py:295
  148.0 11.0 %collective-permute-start.23 = (bf16[256,512]{1,0:T(8,128)(2,1)S(1)}, bf16[256,512]{1,0:T(8,128)(2,1)S(1)}, u32[]{:S(2)}, u32[]{:S(2)}) collective-permute-start(bf16[256,512]{1,0:T(8,128)(2,1)S(1)} %collective-permute-done.22), channel_id=1, source_target_pairs={{0,16},{8,24},{16,0},{24,8},{1,17},{9,25},{17,1},{25,9},{2,18},{10... | collective-permute-start | bytes 786440 | tf_op jit(solution)/shard_map/ppermute | solution.py:295
  148.3 10.9 %collective-permute-start.21 = (bf16[256,512]{1,0:T(8,128)(2,1)S(1)}, bf16[256,512]{1,0:T(8,128)(2,1)S(1)}, u32[]{:S(2)}, u32[]{:S(2)}) collective-permute-start(bf16[256,512]{1,0:T(8,128)(2,1)S(1)} %collective-permute-done.20), channel_id=1, source_target_pairs={{0,8},{8,0},{16,24},{24,16},{1,9},{9,1},{17,25},{25,17},{2,10},{10... | collective-permute-start | bytes 786440 | tf_op jit(solution)/shard_map/ppermute | solution.py:295
  159.3 8.9 %collective-permute-start.26 = (f32[256,1]{0,1:T(1,128)S(1)}, f32[256,1]{0,1:T(1,128)S(1)}, u32[]{:S(2)}, u32[]{:S(2)}) collective-permute-start(f32[256,1]{0,1:T(1,128)S(1)} %bitcast.48), channel_id=1, source_target_pairs={{0,1},{1,0},{2,3},{3,2},{4,5},{5,4},{6,7},{7,6},{8,9},{9,8},{10,11... | collective-permute-start | bytes 3080 | tf_op jit(solution)/shard_map/ppermute | solution.py:295
  (9 other events, 65.8 us)

commit v4 on v3

--- a/solution.py
+++ b/solution.py
@@ -73,17 +73,16 @@
     return high, (x - high.astype(F32)).astype(LOW)
 
 
-def apply_halves(upper, side_ref, inverse, high_ref, low_ref, out_refs):
+def apply_halves(upper, side_ref, inverse, mixed_ref, out_refs):
     inverse_high, inverse_low = split_low(inverse)
-    half = high_ref.shape[1] // 2
+    half = mixed_ref.shape[1] // 2
     size = half // 2
     width = tile_of(size)
     for turn, out_ref in enumerate(out_refs):
         side = side_ref[turn] if upper else 1 - side_ref[turn]
         for at in range(0, size, width):
             start = pl.multiple_of(side * size + (turn * half + at), LANES)
-            high = high_ref[:, pl.ds(start, width)]
-            low = low_ref[:, pl.ds(start, width)]
+            high, low = split_low(mixed_ref[:, pl.ds(start, width)])
             product = (
                 jnp.dot(inverse_high, low, preferred_element_type=F32)
                 + jnp.dot(inverse_low, high, preferred_element_type=F32)
@@ -91,40 +90,40 @@
             out_ref[:, at : at + width] = product.astype(out_ref.dtype)
 
 
-def sent_kernel(side_ref, gram_ref, high_ref, low_ref, inverse_ref, first_ref, second_ref, work_ref):
+def sent_kernel(side_ref, gram_ref, mixed_ref, inverse_ref, first_ref, second_ref, work_ref):
     inverse_factor_kernel(32, 16, gram_ref, inverse_ref, work_ref)
-    apply_halves(False, side_ref, inverse_ref[...], high_ref, low_ref, (first_ref, second_ref))
-
-
-def kept_kernel(side_ref, inverse_ref, high_ref, low_ref, first_ref, second_ref):
-    apply_halves(True, side_ref, inverse_ref[...], high_ref, low_ref, (first_ref, second_ref))
+    apply_halves(False, side_ref, inverse_ref[...], mixed_ref, (first_ref, second_ref))
+
+
+def kept_kernel(side_ref, inverse_ref, mixed_ref, first_ref, second_ref):
+    apply_halves(True, side_ref, inverse_ref[...], mixed_ref, (first_ref, second_ref))
 
 
 WHOLE = pl.BlockSpec(memory_space=pltpu.VMEM)
 SCALARS = pl.BlockSpec(memory_space=pltpu.SMEM)
 
 
-def inverse_and_sent(side, gram, high, low):
-    n, columns = high.shape
+def inverse_and_sent(side, gram, mixed):
+    n, columns = mixed.shape
     quarter = jax.ShapeDtypeStruct((n, columns // 4), LOW)
     return pl.pallas_call(
         sent_kernel,
-        in_specs=[SCALARS, WHOLE, WHOLE, WHOLE],
+        in_specs=[SCALARS, WHOLE, WHOLE],
         out_shape=(jax.ShapeDtypeStruct((n, n), F32), quarter, quarter),
         scratch_shapes=[pltpu.VMEM((n, 2 * n), F32)],
         compiler_params=pltpu.CompilerParams(vmem_limit_bytes=16 << 20),
-    )(side, gram, high, low)
-
-
-def kept_quarters(side, inverse, high, low):
-    n, columns = high.shape
+    )(side, gram, mixed)
+
+
+def kept_quarters(side, inverse, mixed):
+    n, columns = mixed.shape
     quarter = jax.ShapeDtypeStruct((n, columns // 4), F32)
     return pl.pallas_call(
         kept_kernel,
-        in_specs=[SCALARS, WHOLE, WHOLE, WHOLE],
+        in_specs=[SCALARS, WHOLE, WHOLE],
         out_shape=(quarter, quarter),
         compiler_params=pltpu.CompilerParams(vmem_limit_bytes=16 << 20),
-    )(side, inverse, high, low)
+    )(side, inverse, mixed)
 
 
 def tile_of(size):
@@ -145,7 +144,7 @@
 def left_product(moment, change, factor):
     rows, columns = moment.shape
     rank = factor.shape[1]
-    tile = min(rows, 256)
+    tile = min(rows, 512)
     return pl.pallas_call(
         left_kernel,
         grid=(rows // tile,),
@@ -167,10 +166,9 @@
 
 
 def mixed_product(left_low, moment, change):
-    mixed = lax.dot_general(
+    return lax.dot_general(
         left_low, moment, COLS_OVER, preferred_element_type=F32
     ) + lax.dot_general(left_low, change, COLS_OVER, preferred_element_type=F32)
-    return split_low(mixed)
 
 
 def total_kernel(moment_ref, change_ref, first_ref, second_ref):
@@ -215,14 +213,14 @@
 def feedback_columns(places, ortho_low, pieces, total, written):
     count, rank, width = pieces.shape
     rows, columns = total[0].shape[0], 2 * total[0].shape[1]
-    tile = tile_of(width)
+    tile = width
     steps = width // tile
 
     def column(j, place):
         return (0, 0, place[j // steps] * steps + j % steps)
 
     specs = [
-        pl.BlockSpec((rows, rank), lambda j, place: (0, 0)),
+        WHOLE,
         pl.BlockSpec((1, rank, tile), lambda j, place: (j // steps, 0, j % steps)),
         WHOLE,
         WHOLE,
@@ -247,43 +245,49 @@
     )(*operands)
 
 
-def step_kernel(scale, place_ref, ortho_ref, right_ref, norm_ref, step_ref, factor_ref):
-    factor = right_ref[0].astype(F32) / norm_ref[...]
+def step_kernel(scale, counts, place_ref, ortho_ref, *refs):
+    norm_ref, step_ref, factor_ref, work_ref = refs[len(counts) :]
+    j = pl.program_id(0)
+    first = 0
+    for count, right_ref in zip(counts, refs):
+        for at in range(count):
+
+            @pl.when(j == first + at)
+            def _():
+                work_ref[...] = right_ref[at].astype(F32) / norm_ref[...]
+
+        first += count
+    factor = work_ref[...]
     product = jnp.dot(ortho_ref[...], factor.astype(LOW), preferred_element_type=F32)
     step_ref[...] = (scale * product).astype(LOW)
     factor_ref[...] = factor.T
 
 
-def step_outputs(places, ortho_low, pieces, norms, scale):
-    count, rank, width = pieces.shape
+def step_outputs(places, ortho_low, rounds, norms, scale):
+    counts = [pieces.shape[0] for pieces in rounds]
+    _, rank, width = rounds[0].shape
     rows = ortho_low.shape[0]
-    tile = width
-    steps = width // tile
-    columns = count * width
-    return pl.pallas_call(
-        functools.partial(step_kernel, scale),
+    columns = sum(counts) * width
+    return pl.pallas_call(
+        functools.partial(step_kernel, scale, counts),
         grid_spec=pltpu.PrefetchScalarGridSpec(
             num_scalar_prefetch=1,
-            grid=(count * steps,),
-            in_specs=[
-                pl.BlockSpec((rows, rank), lambda j, place: (0, 0)),
-                pl.BlockSpec((1, rank, tile), lambda j, place: (j // steps, 0, j % steps)),
-                pl.BlockSpec((rank, 1), lambda j, place: (0, 0)),
+            grid=(sum(counts),),
+            in_specs=[pl.BlockSpec((rows, rank), lambda j, place: (0, 0))]
+            + [WHOLE] * len(counts)
+            + [pl.BlockSpec((rank, 1), lambda j, place: (0, 0))],
+            out_specs=[
+                pl.BlockSpec((rows, width), lambda j, place: (0, place[j])),
+                pl.BlockSpec((width, rank), lambda j, place: (place[j], 0)),
             ],
-            out_specs=[
-                pl.BlockSpec((rows, tile), lambda j, place: (0, place[j // steps] * steps + j % steps)),
-                pl.BlockSpec((tile, rank), lambda j, place: (place[j // steps] * steps + j % steps, 0)),
-            ],
+            scratch_shapes=[pltpu.VMEM((rank, width), F32)],
         ),
         out_shape=[
             jax.ShapeDtypeStruct((rows, columns), LOW),
             jax.ShapeDtypeStruct((columns, rank), F32),
         ],
         compiler_params=pltpu.CompilerParams(vmem_limit_bytes=16 << 20),
-        cost_estimate=pl.CostEstimate(
-            flops=2 * rows * rank * columns, bytes_accessed=2 * rows * columns, transcendentals=0
-        ),
-    )(places, ortho_low, pieces, norms)
+    )(places, ortho_low, *rounds, norms)
 
 
 def bits_of(axis):
@@ -351,13 +355,13 @@
     return [bits[turn % len(bits) :] + bits[: turn % len(bits)] for turn in range(2)]
 
 
-def scatter_right(gram, high, low):
+def scatter_right(gram, mixed):
     orders = orders_of()
     index = lax.axis_index("dp")
     side = jnp.stack([(index >> order[0]) & 1 for order in orders])
-    inverse, *sent = inverse_and_sent(side, gram, high, low)
+    inverse, *sent = inverse_and_sent(side, gram, mixed)
     come = [swap(x, "dp", 1 << order[0]) for x, order in zip(sent, orders)]
-    kept = kept_quarters(side, inverse, high, low)
+    kept = kept_quarters(side, inverse, mixed)
     parts = [a + b.astype(F32) for a, b in zip(kept, come)]
     for k in range(1, len(orders[0])):
         parts = [
@@ -425,8 +429,8 @@
     gram = sum_gram(
         lax.dot_general(left_low, left_low, COLS_OVER, preferred_element_type=F32)
     )
-    mixed_high, mixed_low = mixed_product(left_low, moment, change)
-    inverse, right = scatter_right(gram, mixed_high, mixed_low)
+    mixed = mixed_product(left_low, moment, change)
+    inverse, right = scatter_right(gram, mixed)
     ortho_low = jnp.dot(
         left_low.astype(F32), inverse.T, precision=lax.Precision.HIGH
     ).astype(LOW)
@@ -454,7 +458,7 @@
     norms = jnp.sqrt(square_sums / all_cols + 1e-06)
     scale = (all_rows / factor.shape[1]) ** 0.5
     step_direction, new_factor = step_outputs(
-        jnp.concatenate(all_places), ortho_low, jnp.concatenate(all_pieces), norms, scale
+        jnp.concatenate(all_places), ortho_low, all_pieces, norms, scale
     )
     return (new_momentum, step_direction, new_factor)
 

time: 181 us -> 174 us (0.961)
  waiting for transfers between devices: 44.9 us -> 40.5 us
  starting transfers between devices: 31.8 us -> 35.8 us
  Pallas kernels: 72.1 us -> 68.9 us
  matrix products: 20.5 us -> 17.8 us
  other arithmetic: 6.14 us -> 4.01 us
    ppermute x27, waiting for transfers between devices: 44.9 us -> 40.5 us  [swap(): return lax.ppermute(x, axis, [(i, i ^ mask) for i in range(size)])]
    ppermute x27, starting transfers between devices: 31.8 us -> 35.8 us  [swap(): return lax.ppermute(x, axis, [(i, i ^ mask) for i in range(size)])]
    dot_general x1, matrix products: 11.1 us -> 8.39 us  [mixed_product(): lax.dot_general(left_low, moment, COLS_OVER, preferred_element_type=F32)]
    add x2, other arithmetic: 2.38 us -> 0.36 us  [scatter_right(): parts = [a + b.astype(F32) for a, b in zip(kept, come)]]
    unnamed x19 -> x12, local copies, waits for them, and re-layouts: 3.33 us -> 4.47 us
  transfers between devices with their start and end apart: 27 -> 27, of which waited for: 13 -> 12; matrix products, arithmetic and copies ran while one was open for 13% -> 11% of each run, Pallas kernels for 19% -> 19%
where the time goes in v4:
time: 174 us; the launch traced here: 173 us
  Pallas kernels  68.9 us (40%)
  waiting for transfers between devices  40.5 us (23%)
  starting transfers between devices  35.8 us (21%)
  matrix products  17.8 us (10%)
  local copies, waits for them, and re-layouts  5.21 us (3%)
  other arithmetic  4.01 us (2%)
    ppermute x27, waiting for transfers between devices, swap(): return lax.ppermute(x, axis, [(i, i ^ mask) for i in range(size)])  40.5 us
    ppermute x27, starting transfers between devices, swap(): return lax.ppermute(x, axis, [(i, i ^ mask) for i in range(size)])  35.8 us
    pallas_call x3, Pallas kernels, feedback_columns(): pl.pallas_call(functools.partial(feedback_kernel, steps), grid_spec=pltpu...  19.7 us
    pallas_call x1, Pallas kernels, left_product(): pl.pallas_call(left_kernel, grid=(rows // tile,), in_specs=[pl.BlockSpec(...  15.7 us
    pallas_call x1, Pallas kernels, total_of(): pl.pallas_call(total_kernel, grid=(rows // tile,), in_specs=[block, block...  12.5 us
    pallas_call x1, Pallas kernels, step_outputs(): pl.pallas_call(functools.partial(step_kernel, scale, counts), grid_spec=p...  10.7 us
    pallas_call x1, Pallas kernels, inverse_and_sent(): pl.pallas_call(sent_kernel, in_specs=[SCALARS, WHOLE, WHOLE], out_shape=(...  8.86 us
    dot_general x1, matrix products, mixed_product(): lax.dot_general(left_low, moment, COLS_OVER, preferred_element_type=F32)  8.39 us
  transfers between devices with their start and end apart: 27, of which 12 were waited for; matrix products, arithmetic and copies ran while one was open for 11% of the time, Pallas kernels for 19%

profile of v4, /device:TPU:1, one launch (start us, length us, event | category | flops | bytes accessed | tf_op | source)
XLA Modules:
  0.0 173.4 jit_solution(5375154712908393394)
XLA Ops:
  0.6 15.7 %shard_map.58 = f32[2048,256]{1,0:T(8,128)S(1)} custom-call(bf16[2048,4096]{1,0:T(8,128)(2,1)} %bitcast.28, bf16[2048,4096]{1,0:T(8,128)(2,1)} %bitcast.26, f32[4096,256]{1,0:T(8,128)} %factor_ref.1), custom_call_target="tpu_custom_call" | custom-call | flops 8589934592 | bytes 33554432 | tf_op jit(solution)/shard_map/pallas_call | solution.py:148
  16.5 2.7 %collective-permute-done = f32[1024,256]{1,0:T(8,128)} collective-permute-done((f32[1024,256]{1,0:T(8,128)S(1)}, f32[1024,256]{1,0:T(8,128)}, u32[]{:S(2)}, u32[]{:S(2)}) %collective-permute-start) | collective-permute-done | bytes 1048608 | tf_op jit(solution)/shard_map/ppermute | solution.py:299
  20.6 2.4 %collective-permute-start.1 = (bf16[512,256]{1,0:T(8,128)(2,1)S(1)}, bf16[512,256]{1,0:T(8,128)(2,1)S(1)}, u32[]{:S(2)}, u32[]{:S(2)}) collective-permute-start(bf16[512,256]{1,0:T(8,128)(2,1)S(1)} %get-tuple-element.41), channel_id=1, source_target_pairs={{0,8},{8,0},{16,24},{24,16},{1,9},{9,1},{17,25},{25,17},{2,10},{10... | collective-permute-start | bytes 786440 | tf_op jit(solution)/shard_map/ppermute | solution.py:299
  24.3 5.1 %collective-permute-done.1 = bf16[512,256]{1,0:T(8,128)(2,1)S(1)} collective-permute-done((bf16[512,256]{1,0:T(8,128)(2,1)S(1)}, bf16[512,256]{1,0:T(8,128)(2,1)S(1)}, u32[]{:S(2)}, u32[]{:S(2)}) %collective-permute-start.1) | collective-permute-done | bytes 262176 | tf_op jit(solution)/shard_map/ppermute | solution.py:299
  32.0 4.7 %collective-permute-done.4 = bf16[512,256]{1,0:T(8,128)(2,1)S(1)} collective-permute-done((bf16[512,256]{1,0:T(8,128)(2,1)S(1)}, bf16[512,256]{1,0:T(8,128)(2,1)S(1)}, u32[]{:S(2)}, u32[]{:S(2)}) %collective-permute-start.4) | collective-permute-done | bytes 262176 | tf_op jit(solution)/shard_map/ppermute | solution.py:299
  37.3 2.5 %collective-permute-start.5 = (bf16[1024,256]{1,0:T(8,128)(2,1)S(1)}, bf16[1024,256]{1,0:T(8,128)(2,1)S(1)}, u32[]{:S(2)}, u32[]{:S(2)}) collective-permute-start(bf16[1024,256]{1,0:T(8,128)(2,1)S(1)} %fusion), channel_id=1, source_target_pairs={{0,1},{1,0},{2,3},{3,2},{4,5},{5,4},{6,7},{7,6},{8,9},{9,8},{10,11... | collective-permute-start | bytes 1572872 | tf_op jit(solution)/shard_map/ppermute | solution.py:299
  41.9 2.3 %collective-permute-start.7 = (f32[128,256]{1,0:T(8,128)S(1)}, f32[128,256]{1,0:T(8,128)S(1)}, u32[]{:S(2)}, u32[]{:S(2)}) collective-permute-start(f32[128,256]{1,0:T(8,128)S(1)} %constant_dynamic-slice_fusion.2), channel_id=1, source_target_pairs={{0,4},{2,6},{4,0},{6,2},{1,5},{3,7},{5,1},{7,3},{8,12},{10,14},{12... | collective-permute-start | bytes 393224 | tf_op jit(solution)/shard_map/ppermute | solution.py:299
  45.5 8.2 %fusion.4 = f32[256,4096]{1,0:T(8,128)S(1)} fusion(bf16[1,2048,4096]{2,1,0:T(8,128)(2,1)} %param.4, bf16[1024,256]{1,0:T(8,128)(2,1)S(1)} %collective-permute-done.5, bf16[1024,256]{1,0:T(8,128)(2,1)S(1)} %fusion, pred[]{:T(512)S(6)} %eq.10), kind=kOutput, calls=%fused_computation.62 | convolution fusion | flops 4299685888 | bytes 22020096 | tf_op jit(solution)/shard_map/dot_general | solution.py:171
  53.7 2.1 %collective-permute-start.9 = (f32[128,256]{1,0:T(8,128)S(1)}, f32[128,256]{1,0:T(8,128)S(1)}, u32[]{:S(2)}, u32[]{:S(2)}) collective-permute-start(f32[128,256]{1,0:T(8,128)S(1)} %add_add_fusion), channel_id=1, source_target_pairs={{0,1},{1,0},{2,3},{3,2},{4,5},{5,4},{6,7},{7,6},{8,9},{9,8},{10,11... | collective-permute-start | bytes 393224 | tf_op jit(solution)/shard_map/ppermute | solution.py:299
  55.8 8.4 %convolution_add_fusion.mixed_ref = f32[256,4096]{1,0:T(8,128)S(1)} fusion(f32[256,4096]{1,0:T(8,128)S(1)} %fusion.4, bf16[1,2048,4096]{2,1,0:T(8,128)(2,1)} %param.3, bf16[1024,256]{1,0:T(8,128)(2,1)S(1)} %collective-permute-done.5, bf16[1024,256]{1,0:T(8,128)(2,1)S(1)} %fusion, pred[]{:T(512)S(6)} %eq.10), kind=kOutput, calls=%fused_computation | convolution fusion | flops 4300734464 | bytes 26214400 | tf_op jit(solution)/shard_map/dot_general | solution.py:169
  64.3 8.9 %shard_map.59 = (f32[256,256]{1,0:T(8,128)S(1)}, bf16[256,1024]{1,0:T(8,128)(2,1)S(1)}, bf16[256,1024]{1,0:T(8,128)(2,1)S(1)}) custom-call(s32[2]{0:T(128)S(1)} %pad_add_fusion.1.side_ref, f32[256,256]{1,0:T(8,128)S(1)} %maximum_select_fusion.1.gram_ref, f32[256,4096]{1,0:T(8,128)S(1)} %convolution_add_fusion.mixed_ref), custom_call_target="tpu_custom_call" | custom-call | tf_op jit(solution)/shard_map/pallas_call | solution.py:109
  75.6 2.2 %copy-done.1 = f32[256,4096]{1,0:T(8,128)S(1)} copy-done((f32[256,4096]{1,0:T(8,128)S(1)}, f32[256,4096]{1,0:T(8,128)}, u32[]{:S(2)}) %copy-start.1) | copy-done | bytes 4194328
  79.4 7.4 %collective-permute-done.12 = bf16[256,1024]{1,0:T(8,128)(2,1)S(1)} collective-permute-done((bf16[256,1024]{1,0:T(8,128)(2,1)S(1)}, bf16[256,1024]{1,0:T(8,128)(2,1)S(1)}, u32[]{:S(2)}, u32[]{:S(2)}) %collective-permute-start.12) | collective-permute-done | bytes 524320 | tf_op jit(solution)/shard_map/ppermute | solution.py:299
  89.7 4.4 %collective-permute-done.13 = bf16[256,512]{1,0:T(8,128)(2,1)S(1)} collective-permute-done((bf16[256,512]{1,0:T(8,128)(2,1)S(1)}, bf16[256,512]{1,0:T(8,128)(2,1)S(1)}, u32[]{:S(2)}, u32[]{:S(2)}) %collective-permute-start.13) | collective-permute-done | bytes 262176 | tf_op jit(solution)/shard_map/ppermute | solution.py:299
  95.4 3.3 %collective-permute-start.16 = (bf16[256,256]{1,0:T(8,128)(2,1)S(1)}, bf16[256,256]{1,0:T(8,128)(2,1)S(1)}, u32[]{:S(2)}, u32[]{:S(2)}) collective-permute-start(bf16[256,256]{1,0:T(8,128)(2,1)S(1)} %pad_maximum_fusion.7), channel_id=1, source_target_pairs={{0,6},{2,4},{4,2},{6,0},{1,7},{3,5},{5,3},{7,1},{8,14},{10,12},{12... | collective-permute-start | bytes 393224 | tf_op jit(solution)/shard_map/ppermute | solution.py:299
  101.2 8.8 %collective-permute-done.15 = bf16[256,256]{1,0:T(8,128)(2,1)S(1)} collective-permute-done((bf16[256,256]{1,0:T(8,128)(2,1)S(1)}, bf16[256,256]{1,0:T(8,128)(2,1)S(1)}, u32[]{:S(2)}, u32[]{:S(2)}) %collective-permute-start.15) | collective-permute-done | bytes 131104 | tf_op jit(solution)/shard_map/ppermute | solution.py:299
  110.0 3.6 %collective-permute-start.17 = (bf16[256,256]{1,0:T(8,128)(2,1)S(1)}, bf16[256,256]{1,0:T(8,128)(2,1)S(1)}, u32[]{:S(2)}, u32[]{:S(2)}) collective-permute-start(bf16[256,256]{1,0:T(8,128)(2,1)S(1)} %fusion.3), channel_id=1, source_target_pairs={{0,6},{2,4},{4,2},{6,0},{1,7},{3,5},{5,3},{7,1},{8,14},{10,12},{12... | collective-permute-start | bytes 393224 | tf_op jit(solution)/shard_map/ppermute | solution.py:299
  114.2 12.5 %shard_map.61 = (f32[2048,2048]{1,0:T(8,128)S(1)}, f32[2048,2048]{1,0:T(8,128)S(1)}) custom-call(bf16[2048,4096]{1,0:T(8,128)(2,1)} %bitcast.29, bf16[2048,4096]{1,0:T(8,128)(2,1)} %bitcast.27), custom_call_target="tpu_custom_call" | custom-call | tf_op jit(solution)/shard_map/pallas_call | solution.py:186
  131.1 5.5 %shard_map.62.refs_0_ = f32[1,2048,4096]{2,1,0:T(8,128)} custom-call(s32[2]{0:T(128)S(1)} %pad_add_fusion.3.place_ref, bf16[2048,256]{1,0:T(8,128)(2,1)S(1)} %convolution_convert_fusion.ortho_ref, bf16[2,256,512]{2,1,0:T(8,128)(2,1)S(1)} %pad_maximum_fusion.2.right_ref.refs_0_, f32[2048,2048]{1,0:T(8,128)S(1)} %get-tuple-element.21.first_ref, ...), custom_call_target="tpu_custom_call" | custom-call | tf_op jit(solution)/shard_map/pallas_call | solution.py:234
  136.5 2.3 %collective-permute-done.20 = bf16[256,512]{1,0:T(8,128)(2,1)S(1)} collective-permute-done((bf16[256,512]{1,0:T(8,128)(2,1)S(1)}, bf16[256,512]{1,0:T(8,128)(2,1)S(1)}, u32[]{:S(2)}, u32[]{:S(2)}) %collective-permute-start.20) | collective-permute-done | bytes 262176 | tf_op jit(solution)/shard_map/ppermute | solution.py:299
  141.6 8.8 %shard_map.63.refs_0_ = f32[1,2048,4096]{2,1,0:T(8,128)} custom-call(s32[4]{0:T(128)S(1)} %pad_add_fusion.2.place_ref, bf16[2048,256]{1,0:T(8,128)(2,1)S(1)} %convolution_convert_fusion.ortho_ref, bf16[4,256,512]{2,1,0:T(8,128)(2,1)S(1)} %pad_maximum_fusion.right_ref.refs_1_, ...), custom_call_target="tpu_custom_call", output_to_operand_aliasing={{}: (5, {})} | custom-call | tf_op jit(solution)/shard_map/pallas_call | solution.py:234
  150.8 3.9 %collective-permute-start.26 = (f32[256,1]{0,1:T(1,128)S(1)}, f32[256,1]{0,1:T(1,128)S(1)}, u32[]{:S(2)}, u32[]{:S(2)}) collective-permute-start(f32[256,1]{0,1:T(1,128)S(1)} %bitcast.38), channel_id=1, source_target_pairs={{0,1},{1,0},{2,3},{3,2},{4,5},{5,4},{6,7},{7,6},{8,9},{9,8},{10,11... | collective-permute-start | bytes 3080 | tf_op jit(solution)/shard_map/ppermute | solution.py:299
  154.8 5.5 %shard_map.64 = f32[1,2048,4096]{2,1,0:T(8,128)} custom-call(s32[2]{0:T(128)S(1)} %pad_add_fusion.place_ref, bf16[2048,256]{1,0:T(8,128)(2,1)S(1)} %convolution_convert_fusion.ortho_ref, bf16[2,256,512]{2,1,0:T(8,128)(2,1)S(1)} %pad_maximum_fusion.1.right_ref.refs_2_, f32[2048,2048]{1,0:T(8,128)S(1)} %get-tuple-element.21.first_ref, ...), custom_call_target="tpu_custom_call", output_to_operand_aliasing={{}: (5, {})} | custom-call | tf_op jit(solution)/shard_map/pallas_call | solution.py:234
  162.7 10.7 %shard_map.65 = (bf16[2048,4096]{1,0:T(8,128)(2,1)}, f32[4096,256]{1,0:T(8,128)}) custom-call(s32[8]{0:T(128)S(1)} %concatenate.51.place_ref, bf16[2048,256]{1,0:T(8,128)(2,1)S(1)} %convolution_convert_fusion.ortho_ref, bf16[2,256,512]{2,1,0:T(8,128)(2,1)S(1)} %pad_maximum_fusion.2.right_ref.refs_0_, bf16[4,256,512]{2,1,0:T(8,128)(2,1)S(1)} %copy-done.3, ...), custom_call_target="tpu_custom_call" | custom-call | tf_op jit(solution)/shard_map/pallas_call | solution.py:271
  (101 shorter events, 30.7 us)
Async XLA Ops:
  20.6 8.8 %collective-permute-start.1 = (bf16[512,256]{1,0:T(8,128)(2,1)S(1)}, bf16[512,256]{1,0:T(8,128)(2,1)S(1)}, u32[]{:S(2)}, u32[]{:S(2)}) collective-permute-start(bf16[512,256]{1,0:T(8,128)(2,1)S(1)} %get-tuple-element.41), channel_id=1, source_target_pairs={{0,8},{8,0},{16,24},{24,16},{1,9},{9,1},{17,25},{25,17},{2,10},{10... | collective-permute-start | bytes 786440 | tf_op jit(solution)/shard_map/ppermute | solution.py:299
  23.0 7.2 %collective-permute-start.3 = (bf16[512,256]{1,0:T(8,128)(2,1)S(1)}, bf16[512,256]{1,0:T(8,128)(2,1)S(1)}, u32[]{:S(2)}, u32[]{:S(2)}) collective-permute-start(bf16[512,256]{1,0:T(8,128)(2,1)S(1)} %get-tuple-element.42), channel_id=1, source_target_pairs={{0,16},{8,24},{16,0},{24,8},{1,17},{9,25},{17,1},{25,9},{2,18},{10... | collective-permute-start | bytes 786440 | tf_op jit(solution)/shard_map/ppermute | solution.py:299
  30.3 6.3 %collective-permute-start.4 = (bf16[512,256]{1,0:T(8,128)(2,1)S(1)}, bf16[512,256]{1,0:T(8,128)(2,1)S(1)}, u32[]{:S(2)}, u32[]{:S(2)}) collective-permute-start(bf16[512,256]{1,0:T(8,128)(2,1)S(1)} %get-tuple-element.40), channel_id=1, source_target_pairs={{0,8},{8,0},{16,24},{24,16},{1,9},{9,1},{17,25},{25,17},{2,10},{10... | collective-permute-start | bytes 786440 | tf_op jit(solution)/shard_map/ppermute | solution.py:299
  30.8 6.3 %collective-permute-start.2 = (bf16[512,256]{1,0:T(8,128)(2,1)S(1)}, bf16[512,256]{1,0:T(8,128)(2,1)S(1)}, u32[]{:S(2)}, u32[]{:S(2)}) collective-permute-start(bf16[512,256]{1,0:T(8,128)(2,1)S(1)} %get-tuple-element.39), channel_id=1, source_target_pairs={{0,16},{8,24},{16,0},{24,8},{1,17},{9,25},{17,1},{25,9},{2,18},{10... | collective-permute-start | bytes 786440 | tf_op jit(solution)/shard_map/ppermute | solution.py:299
  41.9 11.8 %collective-permute-start.7 = (f32[128,256]{1,0:T(8,128)S(1)}, f32[128,256]{1,0:T(8,128)S(1)}, u32[]{:S(2)}, u32[]{:S(2)}) collective-permute-start(f32[128,256]{1,0:T(8,128)S(1)} %constant_dynamic-slice_fusion.2), channel_id=1, source_target_pairs={{0,4},{2,6},{4,0},{6,2},{1,5},{3,7},{5,1},{7,3},{8,12},{10,14},{12... | collective-permute-start | bytes 393224 | tf_op jit(solution)/shard_map/ppermute | solution.py:299
  44.2 9.5 %collective-permute-start.8 = (f32[128,256]{1,0:T(8,128)S(1)}, f32[128,256]{1,0:T(8,128)S(1)}, u32[]{:S(2)}, u32[]{:S(2)}) collective-permute-start(f32[128,256]{1,0:T(8,128)S(1)} %constant_dynamic-slice_fusion.2), channel_id=1, source_target_pairs={{0,6},{2,4},{4,2},{6,0},{1,7},{3,5},{5,3},{7,1},{8,14},{10,12},{12... | collective-permute-start | bytes 393224 | tf_op jit(solution)/shard_map/ppermute | solution.py:299
  45.2 8.4 %collective-permute-start.6 = (f32[128,256]{1,0:T(8,128)S(1)}, f32[128,256]{1,0:T(8,128)S(1)}, u32[]{:S(2)}, u32[]{:S(2)}) collective-permute-start(f32[128,256]{1,0:T(8,128)S(1)} %constant_dynamic-slice_fusion.2), channel_id=1, source_target_pairs={{0,2},{2,0},{4,6},{6,4},{1,3},{3,1},{5,7},{7,5},{8,10},{10,8},{12,... | collective-permute-start | bytes 393224 | tf_op jit(solution)/shard_map/ppermute | solution.py:299
  53.7 10.6 %collective-permute-start.9 = (f32[128,256]{1,0:T(8,128)S(1)}, f32[128,256]{1,0:T(8,128)S(1)}, u32[]{:S(2)}, u32[]{:S(2)}) collective-permute-start(f32[128,256]{1,0:T(8,128)S(1)} %add_add_fusion), channel_id=1, source_target_pairs={{0,1},{1,0},{2,3},{3,2},{4,5},{5,4},{6,7},{7,6},{8,9},{9,8},{10,11... | collective-permute-start | bytes 393224 | tf_op jit(solution)/shard_map/ppermute | solution.py:299
  73.2 13.6 %collective-permute-start.12 = (bf16[256,1024]{1,0:T(8,128)(2,1)S(1)}, bf16[256,1024]{1,0:T(8,128)(2,1)S(1)}, u32[]{:S(2)}, u32[]{:S(2)}) collective-permute-start(bf16[256,1024]{1,0:T(8,128)(2,1)S(1)} %get-tuple-element.18), channel_id=1, source_target_pairs={{0,16},{8,24},{16,0},{24,8},{1,17},{9,25},{17,1},{25,9},{2,18},{10... | collective-permute-start | bytes 1572872 | tf_op jit(solution)/shard_map/ppermute | solution.py:299
  74.4 13.8 %collective-permute-start.10 = (bf16[256,1024]{1,0:T(8,128)(2,1)S(1)}, bf16[256,1024]{1,0:T(8,128)(2,1)S(1)}, u32[]{:S(2)}, u32[]{:S(2)}) collective-permute-start(bf16[256,1024]{1,0:T(8,128)(2,1)S(1)} %get-tuple-element.16), channel_id=1, source_target_pairs={{0,8},{8,0},{16,24},{24,16},{1,9},{9,1},{17,25},{25,17},{2,10},{10... | collective-permute-start | bytes 1572872 | tf_op jit(solution)/shard_map/ppermute | solution.py:299
  87.0 7.1 %collective-permute-start.13 = (bf16[256,512]{1,0:T(8,128)(2,1)S(1)}, bf16[256,512]{1,0:T(8,128)(2,1)S(1)}, u32[]{:S(2)}, u32[]{:S(2)}) collective-permute-start(bf16[256,512]{1,0:T(8,128)(2,1)S(1)} %dynamic-slice_convert_fusion), channel_id=1, source_target_pairs={{0,8},{8,0},{16,24},{24,16},{1,9},{9,1},{17,25},{25,17},{2,10},{10... | collective-permute-start | bytes 786440 | tf_op jit(solution)/shard_map/ppermute | solution.py:299
  88.4 6.8 %collective-permute-start.11 = (bf16[256,512]{1,0:T(8,128)(2,1)S(1)}, bf16[256,512]{1,0:T(8,128)(2,1)S(1)}, u32[]{:S(2)}, u32[]{:S(2)}) collective-permute-start(bf16[256,512]{1,0:T(8,128)(2,1)S(1)} %dynamic-slice_convert_fusion.1), channel_id=1, source_target_pairs={{0,16},{8,24},{16,0},{24,8},{1,17},{9,25},{17,1},{25,9},{2,18},{10... | collective-permute-start | bytes 786440 | tf_op jit(solution)/shard_map/ppermute | solution.py:299
  98.6 11.3 %collective-permute-start.15 = (bf16[256,256]{1,0:T(8,128)(2,1)S(1)}, bf16[256,256]{1,0:T(8,128)(2,1)S(1)}, u32[]{:S(2)}, u32[]{:S(2)}) collective-permute-start(bf16[256,256]{1,0:T(8,128)(2,1)S(1)} %pad_maximum_fusion.6), channel_id=1, source_target_pairs={{0,4},{2,6},{4,0},{6,2},{1,5},{3,7},{5,1},{7,3},{8,12},{10,14},{12... | collective-permute-start | bytes 393224 | tf_op jit(solution)/shard_map/ppermute | solution.py:299
  99.3 10.7 %collective-permute-start.14 = (bf16[256,256]{1,0:T(8,128)(2,1)S(1)}, bf16[256,256]{1,0:T(8,128)(2,1)S(1)}, u32[]{:S(2)}, u32[]{:S(2)}) collective-permute-start(bf16[256,256]{1,0:T(8,128)(2,1)S(1)} %pad_maximum_fusion.5), channel_id=1, source_target_pairs={{0,2},{2,0},{4,6},{6,4},{1,3},{3,1},{5,7},{7,5},{8,10},{10,8},{12,... | collective-permute-start | bytes 393224 | tf_op jit(solution)/shard_map/ppermute | solution.py:299
  110.0 16.7 %collective-permute-start.17 = (bf16[256,256]{1,0:T(8,128)(2,1)S(1)}, bf16[256,256]{1,0:T(8,128)(2,1)S(1)}, u32[]{:S(2)}, u32[]{:S(2)}) collective-permute-start(bf16[256,256]{1,0:T(8,128)(2,1)S(1)} %fusion.3), channel_id=1, source_target_pairs={{0,6},{2,4},{4,2},{6,0},{1,7},{3,5},{5,3},{7,1},{8,14},{10,12},{12... | collective-permute-start | bytes 393224 | tf_op jit(solution)/shard_map/ppermute | solution.py:299
  113.6 13.1 %collective-permute-start.18 = (bf16[256,256]{1,0:T(8,128)(2,1)S(1)}, bf16[256,256]{1,0:T(8,128)(2,1)S(1)}, u32[]{:S(2)}, u32[]{:S(2)}) collective-permute-start(bf16[256,256]{1,0:T(8,128)(2,1)S(1)} %fusion.3), channel_id=1, source_target_pairs={{0,4},{2,6},{4,0},{6,2},{1,5},{3,7},{5,1},{7,3},{8,12},{10,14},{12... | collective-permute-start | bytes 393224 | tf_op jit(solution)/shard_map/ppermute | solution.py:299
  113.6 13.1 %collective-permute-start.19 = (bf16[256,256]{1,0:T(8,128)(2,1)S(1)}, bf16[256,256]{1,0:T(8,128)(2,1)S(1)}, u32[]{:S(2)}, u32[]{:S(2)}) collective-permute-start(bf16[256,256]{1,0:T(8,128)(2,1)S(1)} %fusion.3), channel_id=1, source_target_pairs={{0,2},{2,0},{4,6},{6,4},{1,3},{3,1},{5,7},{7,5},{8,10},{10,8},{12,... | collective-permute-start | bytes 393224 | tf_op jit(solution)/shard_map/ppermute | solution.py:299
  127.0 9.5 %collective-permute-start.22 = (bf16[256,512]{1,0:T(8,128)(2,1)S(1)}, bf16[256,512]{1,0:T(8,128)(2,1)S(1)}, u32[]{:S(2)}, u32[]{:S(2)}) collective-permute-start(bf16[256,512]{1,0:T(8,128)(2,1)S(1)} %get-tuple-element.28), channel_id=1, source_target_pairs={{0,8},{8,0},{16,24},{24,16},{1,9},{9,1},{17,25},{25,17},{2,10},{10... | collective-permute-start | bytes 786440 | tf_op jit(solution)/shard_map/ppermute | solution.py:299
  127.7 11.1 %collective-permute-start.25 = (bf16[256,512]{1,0:T(8,128)(2,1)S(1)}, bf16[256,512]{1,0:T(8,128)(2,1)S(1)}, u32[]{:S(2)}, u32[]{:S(2)}) collective-permute-start(bf16[256,512]{1,0:T(8,128)(2,1)S(1)} %get-tuple-element.28), channel_id=1, source_target_pairs={{0,16},{8,24},{16,0},{24,8},{1,17},{9,25},{17,1},{25,9},{2,18},{10... | collective-permute-start | bytes 786440 | tf_op jit(solution)/shard_map/ppermute | solution.py:299
  128.9 9.9 %collective-permute-start.20 = (bf16[256,512]{1,0:T(8,128)(2,1)S(1)}, bf16[256,512]{1,0:T(8,128)(2,1)S(1)}, u32[]{:S(2)}, u32[]{:S(2)}) collective-permute-start(bf16[256,512]{1,0:T(8,128)(2,1)S(1)} %get-tuple-element.26), channel_id=1, source_target_pairs={{0,16},{8,24},{16,0},{24,8},{1,17},{9,25},{17,1},{25,9},{2,18},{10... | collective-permute-start | bytes 786440 | tf_op jit(solution)/shard_map/ppermute | solution.py:299
  129.4 9.4 %collective-permute-start.24 = (bf16[256,512]{1,0:T(8,128)(2,1)S(1)}, bf16[256,512]{1,0:T(8,128)(2,1)S(1)}, u32[]{:S(2)}, u32[]{:S(2)}) collective-permute-start(bf16[256,512]{1,0:T(8,128)(2,1)S(1)} %get-tuple-element.26), channel_id=1, source_target_pairs={{0,8},{8,0},{16,24},{24,16},{1,9},{9,1},{17,25},{25,17},{2,10},{10... | collective-permute-start | bytes 786440 | tf_op jit(solution)/shard_map/ppermute | solution.py:299
  138.9 11.6 %collective-permute-start.23 = (bf16[256,512]{1,0:T(8,128)(2,1)S(1)}, bf16[256,512]{1,0:T(8,128)(2,1)S(1)}, u32[]{:S(2)}, u32[]{:S(2)}) collective-permute-start(bf16[256,512]{1,0:T(8,128)(2,1)S(1)} %collective-permute-done.22), channel_id=1, source_target_pairs={{0,16},{8,24},{16,0},{24,8},{1,17},{9,25},{17,1},{25,9},{2,18},{10... | collective-permute-start | bytes 786440 | tf_op jit(solution)/shard_map/ppermute | solution.py:299
  140.1 10.6 %collective-permute-start.21 = (bf16[256,512]{1,0:T(8,128)(2,1)S(1)}, bf16[256,512]{1,0:T(8,128)(2,1)S(1)}, u32[]{:S(2)}, u32[]{:S(2)}) collective-permute-start(bf16[256,512]{1,0:T(8,128)(2,1)S(1)} %collective-permute-done.20), channel_id=1, source_target_pairs={{0,8},{8,0},{16,24},{24,16},{1,9},{9,1},{17,25},{25,17},{2,10},{10... | collective-permute-start | bytes 786440 | tf_op jit(solution)/shard_map/ppermute | solution.py:299
  150.8 9.4 %collective-permute-start.26 = (f32[256,1]{0,1:T(1,128)S(1)}, f32[256,1]{0,1:T(1,128)S(1)}, u32[]{:S(2)}, u32[]{:S(2)}) collective-permute-start(f32[256,1]{0,1:T(1,128)S(1)} %bitcast.38), channel_id=1, source_target_pairs={{0,1},{1,0},{2,3},{3,2},{4,5},{5,4},{6,7},{7,6},{8,9},{9,8},{10,11... | collective-permute-start | bytes 3080 | tf_op jit(solution)/shard_map/ppermute | solution.py:299
  (9 other events, 43.0 us)

commit v5 on v4

v5 whole, which is shorter than its diff:
```python
import functools

import jax
import jax.numpy as jnp
from jax import lax
from jax.experimental import pallas as pl
from jax.experimental.pallas import tpu as pltpu
from jax.sharding import PartitionSpec as P

F32 = jnp.float32
LOW = jnp.bfloat16
LANES = 128
ROOM = 50 << 20
COLS_OVER = (((0,), (0,)), ((), ()))


def inverse_factor_kernel(panel, group, gram_ref, out_ref, work_ref):
    n = gram_ref.shape[0]
    work_ref[...] = jnp.zeros_like(work_ref)
    out_ref[...] = jnp.zeros_like(out_ref)
    rows = lax.broadcasted_iota(jnp.int32, (panel, LANES), 0)
    lanes = lax.broadcasted_iota(jnp.int32, (panel, LANES), 1)
    product = functools.partial(
        lax.dot_general,
        dimension_numbers=COLS_OVER,
        precision=lax.Precision.HIGHEST,
        preferred_element_type=F32,
    )
    for start in range(0, n, panel):
        base = start // LANES * LANES
        wide = base + LANES
        upper = gram_ref[start : start + panel, base:n]
        if start:
            before = work_ref[0:start, start : start + panel]
            upper = upper - product(before, work_ref[0:start, base:n])
            inverse = -product(before, work_ref[0:start, n : n + wide])
            inverse = [inverse[:, c : c + LANES] for c in range(0, wide, LANES)]
        else:
            inverse = [jnp.zeros((panel, LANES), F32)]
        inverse[-1] = inverse[-1] + (lanes == rows + (start - base)).astype(F32)
        upper = [upper[:, c : c + LANES] for c in range(0, n - base, LANES)]
        pivots = jnp.ones((panel, LANES), F32)
        for first in range(0, panel, group):
            lane = start - base + first
            columns = [
                jnp.broadcast_to(upper[0][:, lane + q : lane + q + 1], (panel, LANES))
                for q in range(group)
            ]
            factors = []
            for j in range(group):
                r = first + j
                pivot = columns[j][r : r + 1, :]
                pivots = jnp.where(rows == r, jnp.broadcast_to(pivot, rows.shape), pivots)
                factors.append(jnp.where(rows > r, columns[j] * (1.0 / pivot), 0.0))
                for q in range(j + 1, group):
                    columns[q] = columns[q] - factors[j] * columns[q][r : r + 1, :]
            for j in range(group):
                r = first + j
                upper = [x - factors[j] * x[r : r + 1, :] for x in upper]
                inverse = [x - factors[j] * x[r : r + 1, :] for x in inverse]
        scale = lax.rsqrt(pivots)
        for t, x in enumerate(upper):
            at = base + t * LANES
            work_ref[start : start + panel, at : at + LANES] = x * scale
        for t, x in enumerate(inverse):
            at = t * LANES
            work_ref[start : start + panel, n + at : n + at + LANES] = x * scale
            out_ref[start : start + panel, at : at + LANES] = x * scale


def split_low(x):
    high = x.astype(LOW)
    return high, (x - high.astype(F32)).astype(LOW)


def apply_inverse(inverse, mixed):
    inverse_high, inverse_low = split_low(inverse)
    high, low = split_low(mixed)
    return (
        jnp.dot(inverse_high, low, preferred_element_type=F32)
        + jnp.dot(inverse_low, high, preferred_element_type=F32)
    ) + jnp.dot(inverse_high, high, preferred_element_type=F32)


def sent_kernel(gram_ref, mixed_ref, inverse_ref, first_ref, second_ref, work_ref):
    inverse_factor_kernel(32, 16, gram_ref, inverse_ref, work_ref)
    inverse = inverse_ref[...]
    size = first_ref.shape[1]
    width = tile_of(size)
    for turn, out_ref in enumerate((first_ref, second_ref)):
        for at in range(0, size, width):
            mixed = mixed_ref[:, turn * size + at : turn * size + at + width]
            out_ref[:, at : at + width] = apply_inverse(inverse, mixed).astype(LOW)


def mixed_of(left_ref, moment_ref, change_ref):
    left = left_ref[...]
    return jnp.dot(left, moment_ref[...], preferred_element_type=F32) + jnp.dot(
        left, change_ref[...], preferred_element_type=F32
    )


def mixed_kernel(side_ref, left_ref, moment_ref, change_ref, out_ref):
    out_ref[...] = mixed_of(left_ref, moment_ref, change_ref)


def kept_kernel(side_ref, left_ref, moment_ref, change_ref, inverse_ref, out_ref):
    mixed = mixed_of(left_ref, moment_ref, change_ref)
    out_ref[...] = apply_inverse(inverse_ref[...], mixed)


WHOLE = pl.BlockSpec(memory_space=pltpu.VMEM)


def quarters_product(body, side, left_turned, moment, change, *operands):
    rank, rows = left_turned.shape
    columns = moment.shape[1]
    tile = min(columns // 4, 512)
    steps = columns // 4 // tile

    def place(j, side):
        return (0, (2 * (j // steps) + side[j // steps]) * steps + j % steps)

    block = pl.BlockSpec((rows, tile), place)
    return pl.pallas_call(
        body,
        grid_spec=pltpu.PrefetchScalarGridSpec(
            num_scalar_prefetch=1,
            grid=(2 * steps,),
            in_specs=[pl.BlockSpec((rank, rows), lambda j, side: (0, 0)), block, block]
            + [WHOLE] * len(operands),
            out_specs=pl.BlockSpec((rank, tile), lambda j, side: (0, j)),
        ),
        out_shape=jax.ShapeDtypeStruct((rank, columns // 2), F32),
        compiler_params=pltpu.CompilerParams(vmem_limit_bytes=ROOM),
    )(side, left_turned, moment, change, *operands)


def inverse_and_sent(gram, mixed):
    n, columns = mixed.shape
    quarter = jax.ShapeDtypeStruct((n, columns // 2), LOW)
    return pl.pallas_call(
        sent_kernel,
        out_shape=(jax.ShapeDtypeStruct((n, n), F32), quarter, quarter),
        scratch_shapes=[pltpu.VMEM((n, 2 * n), F32)],
        compiler_params=pltpu.CompilerParams(vmem_limit_bytes=16 << 20),
    )(gram, mixed)


def tile_of(size):
    return 256 if size % 256 == 0 else LANES


def left_kernel(moment_ref, change_ref, factor_ref, out_ref, low_ref):
    @pl.when(pl.program_id(0) == 0)
    def _():
        low_ref[...] = factor_ref[...].astype(LOW)

    factor = low_ref[...]
    out_ref[...] = jnp.dot(moment_ref[...], factor, preferred_element_type=F32) + jnp.dot(
        change_ref[...], factor, preferred_element_type=F32
    )


def left_product(moment, change, factor):
    rows, columns = moment.shape
    rank = factor.shape[1]
    tile = min(rows, 512)
    return pl.pallas_call(
        left_kernel,
        grid=(rows // tile,),
        in_specs=[
            pl.BlockSpec((tile, columns), lambda i: (i, 0)),
            pl.BlockSpec((tile, columns), lambda i: (i, 0)),
            pl.BlockSpec((columns, rank), lambda i: (0, 0), pipeline_mode=pl.Buffered(1)),
        ],
        out_specs=pl.BlockSpec((tile, rank), lambda i: (i, 0)),
        out_shape=jax.ShapeDtypeStruct((rows, rank), F32),
        scratch_shapes=[pltpu.VMEM((columns, rank), LOW)],
        compiler_params=pltpu.CompilerParams(vmem_limit_bytes=ROOM),
        cost_estimate=pl.CostEstimate(
            flops=4 * rows * columns * rank,
            bytes_accessed=4 * rows * columns,
            transcendentals=0,
        ),
    )(moment, change, factor)


def total_kernel(counts, place_ref, moment_ref, change_ref, *out_refs):
    j = pl.program_id(0)
    width = moment_ref.shape[1]
    first = 0
    for count, out_ref in zip(counts, out_refs):

        @pl.when((j >= first) & (j < first + count))
        def _():
            at = jnp.clip(j - first, 0, count - 1) * width
            out_ref[:, pl.ds(pl.multiple_of(at, width), width)] = moment_ref[...].astype(
                F32
            ) + change_ref[...].astype(F32)

        first += count


def totals_of(places, width, moment, change):
    rows = moment.shape[0]
    counts = [place.shape[0] for place in places]
    block = pl.BlockSpec((rows, width), lambda j, place: (0, place[j]))
    return pl.pallas_call(
        functools.partial(total_kernel, counts),
        grid_spec=pltpu.PrefetchScalarGridSpec(
            num_scalar_prefetch=1,
            grid=(sum(counts),),
            in_specs=[block, block],
            out_specs=[WHOLE] * len(counts),
        ),
        out_shape=[pltpu.VMEM((rows, count * width), F32) for count in counts],
        compiler_params=pltpu.CompilerParams(vmem_limit_bytes=14 << 20),
    )(jnp.concatenate(places), moment, change)


def first_kernel(place_ref, ortho_ref, right_ref, moment_ref, change_ref, out_ref):
    feedback = jnp.dot(ortho_ref[...], right_ref[0], preferred_element_type=F32)
    out_ref[0] = moment_ref[...].astype(F32) + change_ref[...].astype(F32) - 0.05 * feedback


def later_kernel(place_ref, ortho_ref, right_ref, total_ref, written_ref, out_ref):
    width = out_ref.shape[2]
    at = pl.multiple_of(pl.program_id(0) * width, width)
    feedback = jnp.dot(ortho_ref[...], right_ref[0], preferred_element_type=F32)
    out_ref[0] = total_ref[:, pl.ds(at, width)] - 0.05 * feedback


def feedback_columns(places, ortho_low, pieces, moment, change, total, written):
    count, rank, width = pieces.shape
    rows, columns = moment.shape
    specs = [WHOLE, pl.BlockSpec((1, rank, width), lambda j, place: (j, 0, 0))]
    if written is None:
        tile = tile_of(width)
        steps = width // tile
        specs[1] = pl.BlockSpec((1, rank, tile), lambda j, place: (j // steps, 0, j % steps))
        block = pl.BlockSpec(
            (rows, tile), lambda j, place: (0, place[j // steps] * steps + j % steps)
        )
        specs += [block, block]
        operands = [moment, change]
        aliases = {}
    else:
        tile, steps = width, 1
        specs += [WHOLE, pl.BlockSpec(memory_space=pl.ANY)]
        operands = [total, written]
        aliases = {4: 0}
    return pl.pallas_call(
        first_kernel if written is None else later_kernel,
        grid_spec=pltpu.PrefetchScalarGridSpec(
            num_scalar_prefetch=1,
            grid=(count * steps,),
            in_specs=specs,
            out_specs=pl.BlockSpec(
                (1, rows, tile), lambda j, place: (0, 0, place[j // steps] * steps + j % steps)
            ),
        ),
        out_shape=jax.ShapeDtypeStruct((1, rows, columns), F32),
        input_output_aliases=aliases,
        compiler_params=pltpu.CompilerParams(vmem_limit_bytes=12 << 20),
    )(places, ortho_low, pieces, *operands)


def step_kernel(scale, starts, place_ref, ortho_ref, *refs):
    norm_ref, step_ref, factor_ref, work_ref = refs[len(starts) :]
    j = pl.program_id(0)
    for start, right_ref in zip(starts, refs):

        @pl.when(j >= start)
        def _():
            work_ref[...] = right_ref[0].astype(F32) / norm_ref[...]

    factor = work_ref[...]
    product = jnp.dot(ortho_ref[...], factor.astype(LOW), preferred_element_type=F32)
    step_ref[...] = (scale * product).astype(LOW)
    factor_ref[...] = factor.T


def step_outputs(places, ortho_low, rounds, norms, scale):
    counts = [pieces.shape[0] for pieces in rounds]
    starts = [sum(counts[:r]) for r in range(len(counts))]
    _, rank, width = rounds[0].shape
    rows = ortho_low.shape[0]
    columns = sum(counts) * width

    def piece_block(start, count):
        return pl.BlockSpec(
            (1, rank, width), lambda j, place: (jnp.clip(j - start, 0, count - 1), 0, 0)
        )

    return pl.pallas_call(
        functools.partial(step_kernel, scale, starts),
        grid_spec=pltpu.PrefetchScalarGridSpec(
            num_scalar_prefetch=1,
            grid=(sum(counts),),
            in_specs=[pl.BlockSpec((rows, rank), lambda j, place: (0, 0))]
            + [piece_block(start, count) for start, count in zip(starts, counts)]
            + [pl.BlockSpec((rank, 1), lambda j, place: (0, 0))],
            out_specs=[
                pl.BlockSpec((rows, width), lambda j, place: (0, place[j])),
                pl.BlockSpec((width, rank), lambda j, place: (place[j], 0)),
            ],
            scratch_shapes=[pltpu.VMEM((rank, width), F32)],
        ),
        out_shape=[
            jax.ShapeDtypeStruct((rows, columns), LOW),
            jax.ShapeDtypeStruct((columns, rank), F32),
        ],
        compiler_params=pltpu.CompilerParams(vmem_limit_bytes=16 << 20),
    )(
        places,
        ortho_low,
        *(pltpu.with_memory_space_constraint(pieces, pltpu.HBM) for pieces in rounds),
        norms,
    )


def bits_of(axis):
    return range(lax.axis_size(axis).bit_length() - 1)


def swap(x, axis, mask):
    size = lax.axis_size(axis)
    return lax.ppermute(x, axis, [(i, i ^ mask) for i in range(size)])


def halve(x, axis, bit, dtype, dim):
    mine = (lax.axis_index(axis) >> bit) & 1
    size = x.shape[dim] // 2
    kept = lax.dynamic_slice_in_dim(x, mine * size, size, dim)
    sent = lax.dynamic_slice_in_dim(x, (1 - mine) * size, size, dim)
    return kept + swap(sent.astype(dtype), axis, 1 << bit).astype(F32)


def unhalve(x, axis, bit):
    mine = (lax.axis_index(axis) >> bit) & 1
    other = swap(x, axis, 1 << bit)
    return jnp.where(mine == 0, jnp.concatenate([x, other]), jnp.concatenate([other, x]))


def add_both(x, axis, bit):
    low = x.astype(LOW)
    return low.astype(F32) + swap(low, axis, 1 << bit).astype(F32)


def tree_sum(terms):
    while len(terms) > 1:
        terms = [terms[i] + terms[i + 1] for i in range(0, len(terms), 2)]
    return terms[0]


def sum_left(partial):
    for bit in bits_of("tensor"):
        partial = halve(partial, "tensor", bit, F32, 0)
    half = partial.shape[0] // 2
    parts = [partial[:half], partial[half:]]
    bits = list(bits_of("dp"))
    for k in range(len(bits)):
        parts = [
            add_both(part, "dp", bits[(k + turn) % len(bits)]) for turn, part in enumerate(parts)
        ]
    low = (jnp.concatenate(parts) / lax.axis_size("dp")).astype(LOW)
    for bit in reversed(bits_of("tensor")):
        low = unhalve(low, "tensor", bit)
    return low


def sum_gram(gram, mixed):
    shards = lax.axis_size("tensor")
    count = gram.shape[0] // shards
    part = lax.dynamic_slice_in_dim(gram, lax.axis_index("tensor") * count, count, 0)
    part = tree_sum([part] + [swap(part, "fsdp", k) for k in range(1, lax.axis_size("fsdp"))])
    part, mixed = lax.optimization_barrier((part, mixed))
    for bit in bits_of("tensor"):
        part = unhalve(part, "tensor", bit)
    return part, mixed


def orders_of():
    bits = list(bits_of("dp"))
    return [bits[turn % len(bits) :] + bits[: turn % len(bits)] for turn in range(2)]


def sides_of():
    index = lax.axis_index("dp")
    return jnp.stack([(index >> order[0]) & 1 for order in orders_of()])


def scatter_right(sent, keep):
    orders = orders_of()
    come = [swap(x, "dp", 1 << order[0]) for x, order in zip(sent, orders)]
    kept = keep()
    size = kept.shape[1] // 2
    parts = [a + b.astype(F32) for a, b in zip((kept[:, :size], kept[:, size:]), come)]
    for k in range(1, len(orders[0])):
        parts = [
            halve(part, "dp", order[k], LOW, 1) for part, order in zip(parts, orders)
        ]
    size = lax.axis_size("fsdp")
    index = lax.axis_index("fsdp")
    width = parts[0].shape[1] // size

    def share(at):
        return jnp.concatenate(
            [lax.dynamic_slice_in_dim(part, at * width, width, 1) for part in parts], axis=1
        )

    terms = [share(index)]
    for k in range(1, size):
        terms.append(swap(share(index ^ k).astype(LOW), "fsdp", k).astype(F32))
    return tree_sum(terms)


def gather_fsdp(low):
    size = lax.axis_size("fsdp")
    index = lax.axis_index("fsdp")
    width = low.shape[1] // 2
    blocks = [low] + [swap(low, "fsdp", k) for k in range(1, size)]
    for bit in bits_of("fsdp"):
        high = ((index >> bit) & 1) == 1
        blocks = [jnp.where(high, blocks[i ^ (1 << bit)], blocks[i]) for i in range(size)]
    return [
        jnp.concatenate([b[:, :width] for b in blocks], axis=1),
        jnp.concatenate([b[:, width:] for b in blocks], axis=1),
    ]


def masks_of():
    depth = len(orders_of()[0])
    return [
        [(turn, mask) for turn in range(2) for mask in range(1 << depth) if mask.bit_count() == r]
        for r in range(depth + 1)
    ]


def places_of(masks):
    index = lax.axis_index("dp")
    orders = orders_of()
    depth = len(orders[0])
    places = []
    for turn, mask in masks:
        place = jnp.int32(turn << depth)
        for k, b in enumerate(orders[turn]):
            place = place + ((((index ^ mask) >> b) & 1) << (depth - 1 - k))
        places.append(place)
    return jnp.stack(places)


def gather_rounds(pieces):
    known = {(turn, 0): piece for turn, piece in enumerate(pieces)}
    orders = orders_of()
    rounds = []
    for masks in masks_of():
        for turn, mask in masks:
            if mask:
                bit = next(b for b in orders[turn] if (mask >> b) & 1)
                known[turn, mask] = swap(known[turn, mask ^ (1 << bit)], "dp", 1 << bit)
        rounds.append({key: known[key] for key in masks})
    return rounds


def local(momentum, gradient, factor):
    replicas = lax.axis_size("dp")
    moment = momentum[0]
    change = gradient[0]
    all_rows = moment.shape[0] * lax.axis_size("fsdp")
    all_cols = moment.shape[1] * lax.axis_size("tensor")
    left_low = sum_left(left_product(moment, change, factor))
    left_turned = left_low.T
    sides = sides_of()
    mixed = quarters_product(mixed_kernel, 1 - sides, left_turned, moment, change)
    gram, mixed = sum_gram(
        jnp.dot(left_turned, left_low, preferred_element_type=F32), mixed
    )
    inverse, *sent = inverse_and_sent(gram, mixed)
    right = scatter_right(
        sent,
        lambda: quarters_product(kept_kernel, sides, left_turned, moment, change, inverse),
    )
    ortho_low = jnp.dot(
        left_low.astype(F32), inverse.T, precision=lax.Precision.HIGH
    ).astype(LOW)
    places = [places_of(masks) for masks in masks_of()]
    width = right.shape[1] // 2 * lax.axis_size("fsdp")
    moment, change, _ = lax.optimization_barrier((moment, change, inverse))
    moment, change = (
        pltpu.with_memory_space_constraint(x, pltpu.HBM) for x in (moment, change)
    )
    totals = totals_of(places[1:], width, moment, change)
    rounds = gather_rounds(gather_fsdp((right / replicas).astype(LOW)))
    new_momentum = None
    all_pieces = []
    sums = {}
    for r, new in enumerate(rounds):
        for key, piece in new.items():
            wide = piece.astype(F32)
            sums[key] = jnp.sum(wide * wide, axis=1, keepdims=True)
        pieces = jnp.stack(list(new.values()))
        new_momentum = feedback_columns(
            places[r],
            ortho_low,
            pieces,
            moment,
            change,
            totals[r - 1] if r else None,
            new_momentum,
        )
        all_pieces.append(pieces)
    square_sums = tree_sum([sums[key] for key in sorted(sums)])
    for bit in bits_of("tensor"):
        square_sums = square_sums + swap(square_sums, "tensor", 1 << bit)
    norms = jnp.sqrt(square_sums / all_cols + 1e-06)
    scale = (all_rows / factor.shape[1]) ** 0.5
    step_direction, new_factor = step_outputs(
        jnp.concatenate(places), ortho_low, all_pieces, norms, scale
    )
    return (new_momentum, step_direction, new_factor)


def solution(mesh):
    in_specs = (P("dp", "fsdp", "tensor"), P("dp", "fsdp", "tensor"), P("tensor", None))
    out_specs = (P("dp", "fsdp", "tensor"), P("fsdp", "tensor"), P("tensor", None))
    return jax.shard_map(local, mesh=mesh, in_specs=in_specs, out_specs=out_specs, check_vma=False)
```

time: 174 us -> 163 us (0.937)
  Pallas kernels: 68.9 us -> 86.7 us
  matrix products: 17.8 us -> 1.53 us
  waiting for transfers between devices: 40.5 us -> 32.3 us
  local copies, waits for them, and re-layouts: 5.21 us -> 1.57 us
  starting transfers between devices: 35.8 us -> 33.9 us
    pallas_call x7 -> x8, Pallas kernels: 53.3 us -> 71 us  [the longest x3 20.4 us: feedback_columns(): pl.pallas_call(first_kernel if written is None else later_kernel, grid_sp...]
    dot_general x3 -> x1, matrix products: 17.1 us -> 0.52 us  [local(): jnp.dot(left_turned, left_low, preferred_element_type=F32)]
    ppermute x27, waiting for transfers between devices: 40.5 us -> 32.3 us  [swap(): return lax.ppermute(x, axis, [(i, i ^ mask) for i in range(size)])]
    unnamed x12, local copies, waits for them, and re-layouts: 4.47 us -> 0.68 us
    ppermute x27, starting transfers between devices: 35.8 us -> 33.9 us  [swap(): return lax.ppermute(x, axis, [(i, i ^ mask) for i in range(size)])]
  transfers between devices with their start and end apart: 27 -> 27, of which waited for: 12 -> 13; matrix products, arithmetic and copies ran while one was open for 11% -> 2% of each run, Pallas kernels for 19% -> 31%
where the time goes in v5:
time: 163 us
  Pallas kernels  86.7 us (53%)
  starting transfers between devices  33.9 us (21%)
  waiting for transfers between devices  32.3 us (20%)
  other arithmetic  5.6 us (3%)
    ppermute x27, starting transfers between devices, swap(): return lax.ppermute(x, axis, [(i, i ^ mask) for i in range(size)])  33.9 us
    ppermute x27, waiting for transfers between devices, swap(): return lax.ppermute(x, axis, [(i, i ^ mask) for i in range(size)])  32.3 us
    pallas_call x3, Pallas kernels, feedback_columns(): pl.pallas_call(first_kernel if written is None else later_kernel, grid_sp...  20.4 us
    pallas_call x2, Pallas kernels, quarters_product(): pl.pallas_call(body, grid_spec=pltpu.PrefetchScalarGridSpec(num_scalar_pr...  19.6 us
    pallas_call x1, Pallas kernels, left_product(): pl.pallas_call(left_kernel, grid=(rows // tile,), in_specs=[pl.BlockSpec(...  15.7 us
    pallas_call x1, Pallas kernels, step_outputs(): pl.pallas_call(functools.partial(step_kernel, scale, starts), grid_spec=p...  12.5 us
    pallas_call x1, Pallas kernels, totals_of(): pl.pallas_call(functools.partial(total_kernel, counts), grid_spec=pltpu.P...  10.3 us
    pallas_call x1, Pallas kernels, inverse_and_sent(): pl.pallas_call(sent_kernel, out_shape=(jax.ShapeDtypeStruct((n, n), F32),...  8.37 us
  transfers between devices with their start and end apart: 27, of which 13 were waited for; matrix products, arithmetic and copies ran while one was open for 2% of the time, Pallas kernels for 31%

profile of v5, /device:TPU:1, one launch (start us, length us, event | category | flops | bytes accessed | tf_op | source)
XLA Modules:
  0.0 162.7 jit_solution(13339199754747287314)
XLA Ops:
  0.6 15.7 %shard_map.58 = f32[2048,256]{1,0:T(8,128)S(1)} custom-call(bf16[2048,4096]{1,0:T(8,128)(2,1)} %bitcast.24, bf16[2048,4096]{1,0:T(8,128)(2,1)} %bitcast.29, f32[4096,256]{1,0:T(8,128)} %factor_ref.1), custom_call_target="tpu_custom_call" | custom-call | flops 8589934592 | bytes 33554432 | tf_op jit(solution)/shard_map/pallas_call | solution.py:169
  17.2 2.4 %collective-permute-done = f32[1024,256]{0,1:T(8,128)} collective-permute-done((f32[1024,256]{0,1:T(8,128)S(1)}, f32[1024,256]{0,1:T(8,128)}, u32[]{:S(2)}, u32[]{:S(2)}) %collective-permute-start) | collective-permute-done | bytes 1048608 | tf_op jit(solution)/shard_map/ppermute | solution.py:329
  19.6 1.4 add_convert_fusion
  21.0 2.4 %collective-permute-start.1 = (bf16[512,256]{0,1:T(8,128)(2,1)S(1)}, bf16[512,256]{0,1:T(8,128)(2,1)S(1)}, u32[]{:S(2)}, u32[]{:S(2)}) collective-permute-start(bf16[512,256]{0,1:T(8,128)(2,1)S(1)} %get-tuple-element.47), channel_id=1, source_target_pairs={{0,8},{8,0},{16,24},{24,16},{1,9},{9,1},{17,25},{25,17},{2,10},{10... | collective-permute-start | bytes 786440 | tf_op jit(solution)/shard_map/ppermute | solution.py:329
  24.7 5.1 %collective-permute-done.1 = bf16[512,256]{0,1:T(8,128)(2,1)S(1)} collective-permute-done((bf16[512,256]{0,1:T(8,128)(2,1)S(1)}, bf16[512,256]{0,1:T(8,128)(2,1)S(1)}, u32[]{:S(2)}, u32[]{:S(2)}) %collective-permute-start.1) | collective-permute-done | bytes 262176 | tf_op jit(solution)/shard_map/ppermute | solution.py:329
  32.4 4.7 %collective-permute-done.4 = bf16[512,256]{0,1:T(8,128)(2,1)S(1)} collective-permute-done((bf16[512,256]{0,1:T(8,128)(2,1)S(1)}, bf16[512,256]{0,1:T(8,128)(2,1)S(1)}, u32[]{:S(2)}, u32[]{:S(2)}) %collective-permute-start.4) | collective-permute-done | bytes 262176 | tf_op jit(solution)/shard_map/ppermute | solution.py:329
  37.7 2.5 %collective-permute-start.5 = (bf16[1024,256]{0,1:T(8,128)(2,1)S(1)}, bf16[1024,256]{0,1:T(8,128)(2,1)S(1)}, u32[]{:S(2)}, u32[]{:S(2)}) collective-permute-start(bf16[1024,256]{0,1:T(8,128)(2,1)S(1)} %fusion), channel_id=1, source_target_pairs={{0,1},{1,0},{2,3},{3,2},{4,5},{5,4},{6,7},{7,6},{8,9},{9,8},{10,11... | collective-permute-start | bytes 1572872 | tf_op jit(solution)/shard_map/ppermute | solution.py:329
  40.3 1.5 collective-permute-done.5
  42.3 2.3 %collective-permute-start.7 = (f32[128,256]{1,0:T(8,128)S(1)}, f32[128,256]{1,0:T(8,128)S(1)}, u32[]{:S(2)}, u32[]{:S(2)}) collective-permute-start(f32[128,256]{1,0:T(8,128)S(1)} %constant_dynamic-slice_fusion.2), channel_id=1, source_target_pairs={{0,4},{2,6},{4,0},{6,2},{1,5},{3,7},{5,1},{7,3},{8,12},{10,14},{12... | collective-permute-start | bytes 393224 | tf_op jit(solution)/shard_map/ppermute | solution.py:329
  46.3 9.2 %shard_map.59.mixed_ref = f32[256,2048]{1,0:T(8,128)S(1)} custom-call(s32[2]{0:T(128)S(1)} %get-tuple-element.29.side_ref, bf16[256,2048]{1,0:T(8,128)(2,1)S(1)} %fusion.4.left_ref, bf16[2048,4096]{1,0:T(8,128)(2,1)} %bitcast.25, bf16[2048,4096]{1,0:T(8,128)(2,1)} %bitcast.30), custom_call_target="tpu_custom_call" | custom-call | tf_op jit(solution)/shard_map/pallas_call | solution.py:125
  57.6 8.4 %shard_map.60 = (f32[256,256]{1,0:T(8,128)S(1)}, bf16[256,1024]{1,0:T(8,128)(2,1)S(1)}, bf16[256,1024]{1,0:T(8,128)(2,1)S(1)}) custom-call(f32[256,256]{1,0:T(8,128)S(1)} %maximum_select_fusion.1.gram_ref, f32[256,2048]{1,0:T(8,128)S(1)} %shard_map.59.mixed_ref), custom_call_target="tpu_custom_call" | custom-call | tf_op jit(solution)/shard_map/pallas_call | solution.py:142
  68.4 10.4 %shard_map.61 = f32[256,2048]{1,0:T(8,128)S(1)} custom-call(s32[2]{0:T(128)S(1)} %get-tuple-element.30.side_ref, bf16[256,2048]{1,0:T(8,128)(2,1)S(1)} %fusion.4.left_ref, bf16[2048,4096]{1,0:T(8,128)(2,1)} %bitcast.26, bf16[2048,4096]{1,0:T(8,128)(2,1)} %bitcast.31, f32[256,256]{1,0:T(8,128)S(1)} %get-tuple-element.16.inverse_ref), custom_call_target="tpu_custom_call" | custom-call | tf_op jit(solution)/shard_map/pallas_call | solution.py:125
  80.1 1.5 slice_add_fusion.1
  83.5 4.5 %collective-permute-done.13 = bf16[256,512]{1,0:T(8,128)(2,1)S(1)} collective-permute-done((bf16[256,512]{1,0:T(8,128)(2,1)S(1)}, bf16[256,512]{1,0:T(8,128)(2,1)S(1)}, u32[]{:S(2)}, u32[]{:S(2)}) %collective-permute-start.13) | collective-permute-done | bytes 262176 | tf_op jit(solution)/shard_map/ppermute | solution.py:329
  88.5 2.9 %collective-permute-start.16 = (bf16[256,256]{1,0:T(8,128)(2,1)S(1)}, bf16[256,256]{1,0:T(8,128)(2,1)S(1)}, u32[]{:S(2)}, u32[]{:S(2)}) collective-permute-start(bf16[256,256]{1,0:T(8,128)(2,1)S(1)} %pad_maximum_fusion.7), channel_id=1, source_target_pairs={{0,6},{2,4},{4,2},{6,0},{1,7},{3,5},{5,3},{7,1},{8,14},{10,12},{12... | collective-permute-start | bytes 393224 | tf_op jit(solution)/shard_map/ppermute | solution.py:329
  92.5 1.8 %collective-permute-done.16 = bf16[256,256]{1,0:T(8,128)(2,1)S(1)} collective-permute-done((bf16[256,256]{1,0:T(8,128)(2,1)S(1)}, bf16[256,256]{1,0:T(8,128)(2,1)S(1)}, u32[]{:S(2)}, u32[]{:S(2)}) %collective-permute-start.16) | collective-permute-done | bytes 131104 | tf_op jit(solution)/shard_map/ppermute | solution.py:329
  94.2 8.7 %collective-permute-done.15 = bf16[256,256]{1,0:T(8,128)(2,1)S(1)} collective-permute-done((bf16[256,256]{1,0:T(8,128)(2,1)S(1)}, bf16[256,256]{1,0:T(8,128)(2,1)S(1)}, u32[]{:S(2)}, u32[]{:S(2)}) %collective-permute-start.15) | collective-permute-done | bytes 131104 | tf_op jit(solution)/shard_map/ppermute | solution.py:329
  103.0 3.4 %collective-permute-start.17 = (bf16[256,256]{1,0:T(8,128)(2,1)S(1)}, bf16[256,256]{1,0:T(8,128)(2,1)S(1)}, u32[]{:S(2)}, u32[]{:S(2)}) collective-permute-start(bf16[256,256]{1,0:T(8,128)(2,1)S(1)} %fusion.3), channel_id=1, source_target_pairs={{0,6},{2,4},{4,2},{6,0},{1,7},{3,5},{5,3},{7,1},{8,14},{10,12},{12... | collective-permute-start | bytes 393224 | tf_op jit(solution)/shard_map/ppermute | solution.py:329
  107.1 10.3 %shard_map.62 = (f32[2048,2048]{1,0:T(8,128)S(1)}, f32[2048,1024]{1,0:T(8,128)S(1)}) custom-call(s32[6]{0:T(128)S(1)} %concatenate.55.place_ref, bf16[2048,4096]{1,0:T(8,128)(2,1)} %bitcast.27, bf16[2048,4096]{1,0:T(8,128)(2,1)} %bitcast.32), custom_call_target="tpu_custom_call" | custom-call | tf_op jit(solution)/shard_map/pallas_call | solution.py:209
  122.0 8.3 %shard_map.63.written_ref = f32[1,2048,4096]{2,1,0:T(8,128)} custom-call(s32[2]{0:T(128)S(1)} %pad_add_fusion.3.place_ref, bf16[2048,256]{1,0:T(8,128)(2,1)S(1)} %convolution_convert_fusion.ortho_ref, bf16[2,256,512]{2,1,0:T(8,128)(2,1)S(1)} %pad_maximum_fusion.2.right_ref.refs_0_, bf16[2048,4096]{1,0:T(8,128)(2,1)} %bitcast.28, bf16[2048,4096]{1,0:T(8,128)(2,1)} %bitcast.33), custom_call_target="tpu_custom_call" | custom-call | tf_op jit(solution)/shard_map/pallas_call | solution.py:253
  133.3 7.4 %shard_map.64.written_ref = f32[1,2048,4096]{2,1,0:T(8,128)} custom-call(s32[4]{0:T(128)S(1)} %pad_add_fusion.2.place_ref, bf16[2048,256]{1,0:T(8,128)(2,1)S(1)} %convolution_convert_fusion.ortho_ref, bf16[4,256,512]{2,1,0:T(8,128)(2,1)S(1)} %pad_maximum_fusion.right_ref.refs_1_, ...), custom_call_target="tpu_custom_call", output_to_operand_aliasing={{}: (4, {})} | custom-call | tf_op jit(solution)/shard_map/pallas_call | solution.py:253
  141.2 4.1 %collective-permute-start.26 = (f32[256,1]{0,1:T(1,128)S(1)}, f32[256,1]{0,1:T(1,128)S(1)}, u32[]{:S(2)}, u32[]{:S(2)}) collective-permute-start(f32[256,1]{0,1:T(1,128)S(1)} %bitcast.42), channel_id=1, source_target_pairs={{0,1},{1,0},{2,3},{3,2},{4,5},{5,4},{6,7},{7,6},{8,9},{9,8},{10,11... | collective-permute-start | bytes 3080 | tf_op jit(solution)/shard_map/ppermute | solution.py:329
  145.4 4.7 %shard_map.65 = f32[1,2048,4096]{2,1,0:T(8,128)} custom-call(s32[2]{0:T(128)S(1)} %pad_add_fusion.place_ref, bf16[2048,256]{1,0:T(8,128)(2,1)S(1)} %convolution_convert_fusion.ortho_ref, bf16[2,256,512]{2,1,0:T(8,128)(2,1)S(1)} %pad_maximum_fusion.1.right_ref.refs_2_, f32[2048,1024]{1,0:T(8,128)S(1)} %get-tuple-element.21.total_ref, ...), custom_call_target="tpu_custom_call", output_to_operand_aliasing={{}: (4, {})} | custom-call | tf_op jit(solution)/shard_map/pallas_call | solution.py:253
  150.3 12.5 %shard_map.66 = (bf16[2048,4096]{1,0:T(8,128)(2,1)}, f32[4096,256]{1,0:T(8,128)}) custom-call(s32[8]{0:T(128)S(1)} %concatenate.56.place_ref, bf16[2048,256]{1,0:T(8,128)(2,1)S(1)} %convolution_convert_fusion.ortho_ref, bf16[2,256,512]{2,1,0:T(8,128)(2,1)} %copy-done.1, bf16[4,256,512]{2,1,0:T(8,128)(2,1)} %copy-done, bf16[2,256,512]{2,1,0:T(8,128)(2,1)} %copy-done.2, ...), custom_call_target="tpu_custom_call" | custom-call | tf_op jit(solution)/shard_map/pallas_call | solution.py:296
  (101 shorter events, 25.8 us)
Async XLA Ops:
  21.0 8.8 %collective-permute-start.1 = (bf16[512,256]{0,1:T(8,128)(2,1)S(1)}, bf16[512,256]{0,1:T(8,128)(2,1)S(1)}, u32[]{:S(2)}, u32[]{:S(2)}) collective-permute-start(bf16[512,256]{0,1:T(8,128)(2,1)S(1)} %get-tuple-element.47), channel_id=1, source_target_pairs={{0,8},{8,0},{16,24},{24,16},{1,9},{9,1},{17,25},{25,17},{2,10},{10... | collective-permute-start | bytes 786440 | tf_op jit(solution)/shard_map/ppermute | solution.py:329
  23.5 7.2 %collective-permute-start.3 = (bf16[512,256]{0,1:T(8,128)(2,1)S(1)}, bf16[512,256]{0,1:T(8,128)(2,1)S(1)}, u32[]{:S(2)}, u32[]{:S(2)}) collective-permute-start(bf16[512,256]{0,1:T(8,128)(2,1)S(1)} %get-tuple-element.48), channel_id=1, source_target_pairs={{0,16},{8,24},{16,0},{24,8},{1,17},{9,25},{17,1},{25,9},{2,18},{10... | collective-permute-start | bytes 786440 | tf_op jit(solution)/shard_map/ppermute | solution.py:329
  30.8 6.3 %collective-permute-start.4 = (bf16[512,256]{0,1:T(8,128)(2,1)S(1)}, bf16[512,256]{0,1:T(8,128)(2,1)S(1)}, u32[]{:S(2)}, u32[]{:S(2)}) collective-permute-start(bf16[512,256]{0,1:T(8,128)(2,1)S(1)} %get-tuple-element.46), channel_id=1, source_target_pairs={{0,8},{8,0},{16,24},{24,16},{1,9},{9,1},{17,25},{25,17},{2,10},{10... | collective-permute-start | bytes 786440 | tf_op jit(solution)/shard_map/ppermute | solution.py:329
  31.3 6.3 %collective-permute-start.2 = (bf16[512,256]{0,1:T(8,128)(2,1)S(1)}, bf16[512,256]{0,1:T(8,128)(2,1)S(1)}, u32[]{:S(2)}, u32[]{:S(2)}) collective-permute-start(bf16[512,256]{0,1:T(8,128)(2,1)S(1)} %get-tuple-element.45), channel_id=1, source_target_pairs={{0,16},{8,24},{16,0},{24,8},{1,17},{9,25},{17,1},{25,9},{2,18},{10... | collective-permute-start | bytes 786440 | tf_op jit(solution)/shard_map/ppermute | solution.py:329
  42.3 13.2 %collective-permute-start.7 = (f32[128,256]{1,0:T(8,128)S(1)}, f32[128,256]{1,0:T(8,128)S(1)}, u32[]{:S(2)}, u32[]{:S(2)}) collective-permute-start(f32[128,256]{1,0:T(8,128)S(1)} %constant_dynamic-slice_fusion.2), channel_id=1, source_target_pairs={{0,4},{2,6},{4,0},{6,2},{1,5},{3,7},{5,1},{7,3},{8,12},{10,14},{12... | collective-permute-start | bytes 393224 | tf_op jit(solution)/shard_map/ppermute | solution.py:329
  44.6 10.9 %collective-permute-start.8 = (f32[128,256]{1,0:T(8,128)S(1)}, f32[128,256]{1,0:T(8,128)S(1)}, u32[]{:S(2)}, u32[]{:S(2)}) collective-permute-start(f32[128,256]{1,0:T(8,128)S(1)} %constant_dynamic-slice_fusion.2), channel_id=1, source_target_pairs={{0,6},{2,4},{4,2},{6,0},{1,7},{3,5},{5,3},{7,1},{8,14},{10,12},{12... | collective-permute-start | bytes 393224 | tf_op jit(solution)/shard_map/ppermute | solution.py:329
  45.7 9.8 %collective-permute-start.6 = (f32[128,256]{1,0:T(8,128)S(1)}, f32[128,256]{1,0:T(8,128)S(1)}, u32[]{:S(2)}, u32[]{:S(2)}) collective-permute-start(f32[128,256]{1,0:T(8,128)S(1)} %constant_dynamic-slice_fusion.2), channel_id=1, source_target_pairs={{0,2},{2,0},{4,6},{6,4},{1,3},{3,1},{5,7},{7,5},{8,10},{10,8},{12,... | collective-permute-start | bytes 393224 | tf_op jit(solution)/shard_map/ppermute | solution.py:329
  66.0 13.3 %collective-permute-start.10 = (bf16[256,1024]{1,0:T(8,128)(2,1)S(1)}, bf16[256,1024]{1,0:T(8,128)(2,1)}, u32[]{:S(2)}, u32[]{:S(2)}) collective-permute-start(bf16[256,1024]{1,0:T(8,128)(2,1)S(1)} %get-tuple-element.17), channel_id=1, source_target_pairs={{0,8},{8,0},{16,24},{24,16},{1,9},{9,1},{17,25},{25,17},{2,10},{10... | collective-permute-start | bytes 1572872 | tf_op jit(solution)/shard_map/ppermute | solution.py:329
  67.2 12.9 %collective-permute-start.12 = (bf16[256,1024]{1,0:T(8,128)(2,1)S(1)}, bf16[256,1024]{1,0:T(8,128)(2,1)}, u32[]{:S(2)}, u32[]{:S(2)}) collective-permute-start(bf16[256,1024]{1,0:T(8,128)(2,1)S(1)} %get-tuple-element.18), channel_id=1, source_target_pairs={{0,16},{8,24},{16,0},{24,8},{1,17},{9,25},{17,1},{25,9},{2,18},{10... | collective-permute-start | bytes 1572872 | tf_op jit(solution)/shard_map/ppermute | solution.py:329
  81.7 6.4 %collective-permute-start.13 = (bf16[256,512]{1,0:T(8,128)(2,1)S(1)}, bf16[256,512]{1,0:T(8,128)(2,1)S(1)}, u32[]{:S(2)}, u32[]{:S(2)}) collective-permute-start(bf16[256,512]{1,0:T(8,128)(2,1)S(1)} %dynamic-slice_convert_fusion), channel_id=1, source_target_pairs={{0,8},{8,0},{16,24},{24,16},{1,9},{9,1},{17,25},{25,17},{2,10},{10... | collective-permute-start | bytes 786440 | tf_op jit(solution)/shard_map/ppermute | solution.py:329
  82.2 6.1 %collective-permute-start.11 = (bf16[256,512]{1,0:T(8,128)(2,1)S(1)}, bf16[256,512]{1,0:T(8,128)(2,1)S(1)}, u32[]{:S(2)}, u32[]{:S(2)}) collective-permute-start(bf16[256,512]{1,0:T(8,128)(2,1)S(1)} %dynamic-slice_convert_fusion.1), channel_id=1, source_target_pairs={{0,16},{8,24},{16,0},{24,8},{1,17},{9,25},{17,1},{25,9},{2,18},{10... | collective-permute-start | bytes 786440 | tf_op jit(solution)/shard_map/ppermute | solution.py:329
  88.5 5.8 %collective-permute-start.16 = (bf16[256,256]{1,0:T(8,128)(2,1)S(1)}, bf16[256,256]{1,0:T(8,128)(2,1)S(1)}, u32[]{:S(2)}, u32[]{:S(2)}) collective-permute-start(bf16[256,256]{1,0:T(8,128)(2,1)S(1)} %pad_maximum_fusion.7), channel_id=1, source_target_pairs={{0,6},{2,4},{4,2},{6,0},{1,7},{3,5},{5,3},{7,1},{8,14},{10,12},{12... | collective-permute-start | bytes 393224 | tf_op jit(solution)/shard_map/ppermute | solution.py:329
  91.4 11.6 %collective-permute-start.15 = (bf16[256,256]{1,0:T(8,128)(2,1)S(1)}, bf16[256,256]{1,0:T(8,128)(2,1)S(1)}, u32[]{:S(2)}, u32[]{:S(2)}) collective-permute-start(bf16[256,256]{1,0:T(8,128)(2,1)S(1)} %pad_maximum_fusion.6), channel_id=1, source_target_pairs={{0,4},{2,6},{4,0},{6,2},{1,5},{3,7},{5,1},{7,3},{8,12},{10,14},{12... | collective-permute-start | bytes 393224 | tf_op jit(solution)/shard_map/ppermute | solution.py:329
  92.0 10.9 %collective-permute-start.14 = (bf16[256,256]{1,0:T(8,128)(2,1)S(1)}, bf16[256,256]{1,0:T(8,128)(2,1)S(1)}, u32[]{:S(2)}, u32[]{:S(2)}) collective-permute-start(bf16[256,256]{1,0:T(8,128)(2,1)S(1)} %pad_maximum_fusion.5), channel_id=1, source_target_pairs={{0,2},{2,0},{4,6},{6,4},{1,3},{3,1},{5,7},{7,5},{8,10},{10,8},{12,... | collective-permute-start | bytes 393224 | tf_op jit(solution)/shard_map/ppermute | solution.py:329
  103.0 14.4 %collective-permute-start.17 = (bf16[256,256]{1,0:T(8,128)(2,1)S(1)}, bf16[256,256]{1,0:T(8,128)(2,1)S(1)}, u32[]{:S(2)}, u32[]{:S(2)}) collective-permute-start(bf16[256,256]{1,0:T(8,128)(2,1)S(1)} %fusion.3), channel_id=1, source_target_pairs={{0,6},{2,4},{4,2},{6,0},{1,7},{3,5},{5,3},{7,1},{8,14},{10,12},{12... | collective-permute-start | bytes 393224 | tf_op jit(solution)/shard_map/ppermute | solution.py:329
  106.4 11.0 %collective-permute-start.18 = (bf16[256,256]{1,0:T(8,128)(2,1)S(1)}, bf16[256,256]{1,0:T(8,128)(2,1)S(1)}, u32[]{:S(2)}, u32[]{:S(2)}) collective-permute-start(bf16[256,256]{1,0:T(8,128)(2,1)S(1)} %fusion.3), channel_id=1, source_target_pairs={{0,4},{2,6},{4,0},{6,2},{1,5},{3,7},{5,1},{7,3},{8,12},{10,14},{12... | collective-permute-start | bytes 393224 | tf_op jit(solution)/shard_map/ppermute | solution.py:329
  106.4 11.0 %collective-permute-start.19 = (bf16[256,256]{1,0:T(8,128)(2,1)S(1)}, bf16[256,256]{1,0:T(8,128)(2,1)S(1)}, u32[]{:S(2)}, u32[]{:S(2)}) collective-permute-start(bf16[256,256]{1,0:T(8,128)(2,1)S(1)} %fusion.3), channel_id=1, source_target_pairs={{0,2},{2,0},{4,6},{6,4},{1,3},{3,1},{5,7},{7,5},{8,10},{10,8},{12,... | collective-permute-start | bytes 393224 | tf_op jit(solution)/shard_map/ppermute | solution.py:329
  117.7 12.6 %collective-permute-start.22 = (bf16[256,512]{1,0:T(8,128)(2,1)S(1)}, bf16[256,512]{1,0:T(8,128)(2,1)S(1)}, u32[]{:S(2)}, u32[]{:S(2)}) collective-permute-start(bf16[256,512]{1,0:T(8,128)(2,1)S(1)} %get-tuple-element.28), channel_id=1, source_target_pairs={{0,8},{8,0},{16,24},{24,16},{1,9},{9,1},{17,25},{25,17},{2,10},{10... | collective-permute-start | bytes 786440 | tf_op jit(solution)/shard_map/ppermute | solution.py:329
  119.0 11.4 %collective-permute-start.25 = (bf16[256,512]{1,0:T(8,128)(2,1)S(1)}, bf16[256,512]{1,0:T(8,128)(2,1)S(1)}, u32[]{:S(2)}, u32[]{:S(2)}) collective-permute-start(bf16[256,512]{1,0:T(8,128)(2,1)S(1)} %get-tuple-element.28), channel_id=1, source_target_pairs={{0,16},{8,24},{16,0},{24,8},{1,17},{9,25},{17,1},{25,9},{2,18},{10... | collective-permute-start | bytes 786440 | tf_op jit(solution)/shard_map/ppermute | solution.py:329
  120.3 10.0 %collective-permute-start.20 = (bf16[256,512]{1,0:T(8,128)(2,1)S(1)}, bf16[256,512]{1,0:T(8,128)(2,1)S(1)}, u32[]{:S(2)}, u32[]{:S(2)}) collective-permute-start(bf16[256,512]{1,0:T(8,128)(2,1)S(1)} %get-tuple-element.26), channel_id=1, source_target_pairs={{0,16},{8,24},{16,0},{24,8},{1,17},{9,25},{17,1},{25,9},{2,18},{10... | collective-permute-start | bytes 786440 | tf_op jit(solution)/shard_map/ppermute | solution.py:329
  120.6 9.7 %collective-permute-start.24 = (bf16[256,512]{1,0:T(8,128)(2,1)S(1)}, bf16[256,512]{1,0:T(8,128)(2,1)S(1)}, u32[]{:S(2)}, u32[]{:S(2)}) collective-permute-start(bf16[256,512]{1,0:T(8,128)(2,1)S(1)} %get-tuple-element.26), channel_id=1, source_target_pairs={{0,8},{8,0},{16,24},{24,16},{1,9},{9,1},{17,25},{25,17},{2,10},{10... | collective-permute-start | bytes 786440 | tf_op jit(solution)/shard_map/ppermute | solution.py:329
  130.5 10.4 %collective-permute-start.23 = (bf16[256,512]{1,0:T(8,128)(2,1)S(1)}, bf16[256,512]{1,0:T(8,128)(2,1)S(1)}, u32[]{:S(2)}, u32[]{:S(2)}) collective-permute-start(bf16[256,512]{1,0:T(8,128)(2,1)S(1)} %collective-permute-done.22), channel_id=1, source_target_pairs={{0,16},{8,24},{16,0},{24,8},{1,17},{9,25},{17,1},{25,9},{2,18},{10... | collective-permute-start | bytes 786440 | tf_op jit(solution)/shard_map/ppermute | solution.py:329
  131.8 9.2 %collective-permute-start.21 = (bf16[256,512]{1,0:T(8,128)(2,1)S(1)}, bf16[256,512]{1,0:T(8,128)(2,1)S(1)}, u32[]{:S(2)}, u32[]{:S(2)}) collective-permute-start(bf16[256,512]{1,0:T(8,128)(2,1)S(1)} %collective-permute-done.20), channel_id=1, source_target_pairs={{0,8},{8,0},{16,24},{24,16},{1,9},{9,1},{17,25},{25,17},{2,10},{10... | collective-permute-start | bytes 786440 | tf_op jit(solution)/shard_map/ppermute | solution.py:329
  141.2 8.9 %collective-permute-start.26 = (f32[256,1]{0,1:T(1,128)S(1)}, f32[256,1]{0,1:T(1,128)S(1)}, u32[]{:S(2)}, u32[]{:S(2)}) collective-permute-start(f32[256,1]{0,1:T(1,128)S(1)} %bitcast.42), channel_id=1, source_target_pairs={{0,1},{1,0},{2,3},{3,2},{4,5},{5,4},{6,7},{7,6},{8,9},{9,8},{10,11... | collective-permute-start | bytes 3080 | tf_op jit(solution)/shard_map/ppermute | solution.py:329
  (8 other events, 39.8 us)

commit v6 on v5

--- a/solution.py
+++ b/solution.py
@@ -266,15 +266,17 @@
     )(places, ortho_low, pieces, *operands)
 
 
-def step_kernel(scale, starts, place_ref, ortho_ref, *refs):
-    norm_ref, step_ref, factor_ref, work_ref = refs[len(starts) :]
+def step_kernel(scale, counts, place_ref, ortho_ref, *refs):
+    norm_ref, step_ref, factor_ref, work_ref = refs[len(counts) :]
     j = pl.program_id(0)
-    for start, right_ref in zip(starts, refs):
-
-        @pl.when(j >= start)
+    start = 0
+    for count, right_ref in zip(counts, refs):
+
+        @pl.when((j >= start) & (j < start + count))
         def _():
             work_ref[...] = right_ref[0].astype(F32) / norm_ref[...]
 
+        start += count
     factor = work_ref[...]
     product = jnp.dot(ortho_ref[...], factor.astype(LOW), preferred_element_type=F32)
     step_ref[...] = (scale * product).astype(LOW)
@@ -294,11 +296,11 @@
         )
 
     return pl.pallas_call(
-        functools.partial(step_kernel, scale, starts),
+        functools.partial(step_kernel, scale, counts),
         grid_spec=pltpu.PrefetchScalarGridSpec(
             num_scalar_prefetch=1,
             grid=(sum(counts),),
-            in_specs=[pl.BlockSpec((rows, rank), lambda j, place: (0, 0))]
+            in_specs=[WHOLE]
             + [piece_block(start, count) for start, count in zip(starts, counts)]
             + [pl.BlockSpec((rank, 1), lambda j, place: (0, 0))],
             out_specs=[

time: 163 us -> 163 us (level)
  no operation moved by 1% of the time
where the time goes in v6:
time: 163 us; the launch traced here: 162 us
  Pallas kernels  86.2 us (53%)
  starting transfers between devices  33.9 us (21%)
  waiting for transfers between devices  32.3 us (20%)
  other arithmetic  5.6 us (3%)
    ppermute x27, starting transfers between devices, swap(): return lax.ppermute(x, axis, [(i, i ^ mask) for i in range(size)])  33.9 us
    ppermute x27, waiting for transfers between devices, swap(): return lax.ppermute(x, axis, [(i, i ^ mask) for i in range(size)])  32.3 us
    pallas_call x3, Pallas kernels, feedback_columns(): pl.pallas_call(first_kernel if written is None else later_kernel, grid_sp...  20.4 us
    pallas_call x2, Pallas kernels, quarters_product(): pl.pallas_call(body, grid_spec=pltpu.PrefetchScalarGridSpec(num_scalar_pr...  19.6 us
    pallas_call x1, Pallas kernels, left_product(): pl.pallas_call(left_kernel, grid=(rows // tile,), in_specs=[pl.BlockSpec(...  15.7 us
    pallas_call x1, Pallas kernels, step_outputs(): pl.pallas_call(functools.partial(step_kernel, scale, counts), grid_spec=p...  12 us
    pallas_call x1, Pallas kernels, totals_of(): pl.pallas_call(functools.partial(total_kernel, counts), grid_spec=pltpu.P...  10.3 us
    pallas_call x1, Pallas kernels, inverse_and_sent(): pl.pallas_call(sent_kernel, out_shape=(jax.ShapeDtypeStruct((n, n), F32),...  8.37 us
  transfers between devices with their start and end apart: 27, of which 13 were waited for; matrix products, arithmetic and copies ran while one was open for 2% of the time, Pallas kernels for 31%

profile of v6, /device:TPU:1, one launch (start us, length us, event | category | flops | bytes accessed | tf_op | source)
XLA Modules:
  0.0 162.3 jit_solution(7420641813187491247)
XLA Ops:
  0.6 15.7 %shard_map.58 = f32[2048,256]{1,0:T(8,128)S(1)} custom-call(bf16[2048,4096]{1,0:T(8,128)(2,1)} %bitcast.24, bf16[2048,4096]{1,0:T(8,128)(2,1)} %bitcast.29, f32[4096,256]{1,0:T(8,128)} %factor_ref.1), custom_call_target="tpu_custom_call" | custom-call | flops 8589934592 | bytes 33554432 | tf_op jit(solution)/shard_map/pallas_call | solution.py:169
  17.2 2.4 %collective-permute-done = f32[1024,256]{0,1:T(8,128)} collective-permute-done((f32[1024,256]{0,1:T(8,128)S(1)}, f32[1024,256]{0,1:T(8,128)}, u32[]{:S(2)}, u32[]{:S(2)}) %collective-permute-start) | collective-permute-done | bytes 1048608 | tf_op jit(solution)/shard_map/ppermute | solution.py:331
  19.6 1.4 add_convert_fusion
  21.0 2.4 %collective-permute-start.1 = (bf16[512,256]{0,1:T(8,128)(2,1)S(1)}, bf16[512,256]{0,1:T(8,128)(2,1)S(1)}, u32[]{:S(2)}, u32[]{:S(2)}) collective-permute-start(bf16[512,256]{0,1:T(8,128)(2,1)S(1)} %get-tuple-element.47), channel_id=1, source_target_pairs={{0,8},{8,0},{16,24},{24,16},{1,9},{9,1},{17,25},{25,17},{2,10},{10... | collective-permute-start | bytes 786440 | tf_op jit(solution)/shard_map/ppermute | solution.py:331
  24.7 5.1 %collective-permute-done.1 = bf16[512,256]{0,1:T(8,128)(2,1)S(1)} collective-permute-done((bf16[512,256]{0,1:T(8,128)(2,1)S(1)}, bf16[512,256]{0,1:T(8,128)(2,1)S(1)}, u32[]{:S(2)}, u32[]{:S(2)}) %collective-permute-start.1) | collective-permute-done | bytes 262176 | tf_op jit(solution)/shard_map/ppermute | solution.py:331
  32.4 4.7 %collective-permute-done.4 = bf16[512,256]{0,1:T(8,128)(2,1)S(1)} collective-permute-done((bf16[512,256]{0,1:T(8,128)(2,1)S(1)}, bf16[512,256]{0,1:T(8,128)(2,1)S(1)}, u32[]{:S(2)}, u32[]{:S(2)}) %collective-permute-start.4) | collective-permute-done | bytes 262176 | tf_op jit(solution)/shard_map/ppermute | solution.py:331
  37.7 2.5 %collective-permute-start.5 = (bf16[1024,256]{0,1:T(8,128)(2,1)S(1)}, bf16[1024,256]{0,1:T(8,128)(2,1)S(1)}, u32[]{:S(2)}, u32[]{:S(2)}) collective-permute-start(bf16[1024,256]{0,1:T(8,128)(2,1)S(1)} %fusion), channel_id=1, source_target_pairs={{0,1},{1,0},{2,3},{3,2},{4,5},{5,4},{6,7},{7,6},{8,9},{9,8},{10,11... | collective-permute-start | bytes 1572872 | tf_op jit(solution)/shard_map/ppermute | solution.py:331
  40.3 1.5 collective-permute-done.5
  42.3 2.3 %collective-permute-start.7 = (f32[128,256]{1,0:T(8,128)S(1)}, f32[128,256]{1,0:T(8,128)S(1)}, u32[]{:S(2)}, u32[]{:S(2)}) collective-permute-start(f32[128,256]{1,0:T(8,128)S(1)} %constant_dynamic-slice_fusion.2), channel_id=1, source_target_pairs={{0,4},{2,6},{4,0},{6,2},{1,5},{3,7},{5,1},{7,3},{8,12},{10,14},{12... | collective-permute-start | bytes 393224 | tf_op jit(solution)/shard_map/ppermute | solution.py:331
  46.3 9.2 %shard_map.59.mixed_ref = f32[256,2048]{1,0:T(8,128)S(1)} custom-call(s32[2]{0:T(128)S(1)} %get-tuple-element.29.side_ref, bf16[256,2048]{1,0:T(8,128)(2,1)S(1)} %fusion.4.left_ref, bf16[2048,4096]{1,0:T(8,128)(2,1)} %bitcast.25, bf16[2048,4096]{1,0:T(8,128)(2,1)} %bitcast.30), custom_call_target="tpu_custom_call" | custom-call | tf_op jit(solution)/shard_map/pallas_call | solution.py:125
  57.6 8.4 %shard_map.60 = (f32[256,256]{1,0:T(8,128)S(1)}, bf16[256,1024]{1,0:T(8,128)(2,1)S(1)}, bf16[256,1024]{1,0:T(8,128)(2,1)S(1)}) custom-call(f32[256,256]{1,0:T(8,128)S(1)} %maximum_select_fusion.1.gram_ref, f32[256,2048]{1,0:T(8,128)S(1)} %shard_map.59.mixed_ref), custom_call_target="tpu_custom_call" | custom-call | tf_op jit(solution)/shard_map/pallas_call | solution.py:142
  68.4 10.4 %shard_map.61 = f32[256,2048]{1,0:T(8,128)S(1)} custom-call(s32[2]{0:T(128)S(1)} %get-tuple-element.30.side_ref, bf16[256,2048]{1,0:T(8,128)(2,1)S(1)} %fusion.4.left_ref, bf16[2048,4096]{1,0:T(8,128)(2,1)} %bitcast.26, bf16[2048,4096]{1,0:T(8,128)(2,1)} %bitcast.31, f32[256,256]{1,0:T(8,128)S(1)} %get-tuple-element.16.inverse_ref), custom_call_target="tpu_custom_call" | custom-call | tf_op jit(solution)/shard_map/pallas_call | solution.py:125
  80.1 1.5 slice_add_fusion.1
  83.5 4.5 %collective-permute-done.13 = bf16[256,512]{1,0:T(8,128)(2,1)S(1)} collective-permute-done((bf16[256,512]{1,0:T(8,128)(2,1)S(1)}, bf16[256,512]{1,0:T(8,128)(2,1)S(1)}, u32[]{:S(2)}, u32[]{:S(2)}) %collective-permute-start.13) | collective-permute-done | bytes 262176 | tf_op jit(solution)/shard_map/ppermute | solution.py:331
  88.5 2.9 %collective-permute-start.16 = (bf16[256,256]{1,0:T(8,128)(2,1)S(1)}, bf16[256,256]{1,0:T(8,128)(2,1)S(1)}, u32[]{:S(2)}, u32[]{:S(2)}) collective-permute-start(bf16[256,256]{1,0:T(8,128)(2,1)S(1)} %pad_maximum_fusion.7), channel_id=1, source_target_pairs={{0,6},{2,4},{4,2},{6,0},{1,7},{3,5},{5,3},{7,1},{8,14},{10,12},{12... | collective-permute-start | bytes 393224 | tf_op jit(solution)/shard_map/ppermute | solution.py:331
  92.5 1.8 %collective-permute-done.16 = bf16[256,256]{1,0:T(8,128)(2,1)S(1)} collective-permute-done((bf16[256,256]{1,0:T(8,128)(2,1)S(1)}, bf16[256,256]{1,0:T(8,128)(2,1)S(1)}, u32[]{:S(2)}, u32[]{:S(2)}) %collective-permute-start.16) | collective-permute-done | bytes 131104 | tf_op jit(solution)/shard_map/ppermute | solution.py:331
  94.2 8.7 %collective-permute-done.15 = bf16[256,256]{1,0:T(8,128)(2,1)S(1)} collective-permute-done((bf16[256,256]{1,0:T(8,128)(2,1)S(1)}, bf16[256,256]{1,0:T(8,128)(2,1)S(1)}, u32[]{:S(2)}, u32[]{:S(2)}) %collective-permute-start.15) | collective-permute-done | bytes 131104 | tf_op jit(solution)/shard_map/ppermute | solution.py:331
  103.0 3.4 %collective-permute-start.17 = (bf16[256,256]{1,0:T(8,128)(2,1)S(1)}, bf16[256,256]{1,0:T(8,128)(2,1)S(1)}, u32[]{:S(2)}, u32[]{:S(2)}) collective-permute-start(bf16[256,256]{1,0:T(8,128)(2,1)S(1)} %fusion.3), channel_id=1, source_target_pairs={{0,6},{2,4},{4,2},{6,0},{1,7},{3,5},{5,3},{7,1},{8,14},{10,12},{12... | collective-permute-start | bytes 393224 | tf_op jit(solution)/shard_map/ppermute | solution.py:331
  107.1 10.3 %shard_map.62 = (f32[2048,2048]{1,0:T(8,128)S(1)}, f32[2048,1024]{1,0:T(8,128)S(1)}) custom-call(s32[6]{0:T(128)S(1)} %concatenate.55.place_ref, bf16[2048,4096]{1,0:T(8,128)(2,1)} %bitcast.27, bf16[2048,4096]{1,0:T(8,128)(2,1)} %bitcast.32), custom_call_target="tpu_custom_call" | custom-call | tf_op jit(solution)/shard_map/pallas_call | solution.py:209
  122.0 8.3 %shard_map.63.written_ref = f32[1,2048,4096]{2,1,0:T(8,128)} custom-call(s32[2]{0:T(128)S(1)} %pad_add_fusion.3.place_ref, bf16[2048,256]{1,0:T(8,128)(2,1)S(1)} %convolution_convert_fusion.ortho_ref, bf16[2,256,512]{2,1,0:T(8,128)(2,1)S(1)} %pad_maximum_fusion.2.right_ref.refs_0_, bf16[2048,4096]{1,0:T(8,128)(2,1)} %bitcast.28, bf16[2048,4096]{1,0:T(8,128)(2,1)} %bitcast.33), custom_call_target="tpu_custom_call" | custom-call | tf_op jit(solution)/shard_map/pallas_call | solution.py:253
  133.3 7.4 %shard_map.64.written_ref = f32[1,2048,4096]{2,1,0:T(8,128)} custom-call(s32[4]{0:T(128)S(1)} %pad_add_fusion.2.place_ref, bf16[2048,256]{1,0:T(8,128)(2,1)S(1)} %convolution_convert_fusion.ortho_ref, bf16[4,256,512]{2,1,0:T(8,128)(2,1)S(1)} %pad_maximum_fusion.right_ref.refs_1_, ...), custom_call_target="tpu_custom_call", output_to_operand_aliasing={{}: (4, {})} | custom-call | tf_op jit(solution)/shard_map/pallas_call | solution.py:253
  141.2 4.1 %collective-permute-start.26 = (f32[256,1]{0,1:T(1,128)S(1)}, f32[256,1]{0,1:T(1,128)S(1)}, u32[]{:S(2)}, u32[]{:S(2)}) collective-permute-start(f32[256,1]{0,1:T(1,128)S(1)} %bitcast.42), channel_id=1, source_target_pairs={{0,1},{1,0},{2,3},{3,2},{4,5},{5,4},{6,7},{7,6},{8,9},{9,8},{10,11... | collective-permute-start | bytes 3080 | tf_op jit(solution)/shard_map/ppermute | solution.py:331
  145.4 4.7 %shard_map.65 = f32[1,2048,4096]{2,1,0:T(8,128)} custom-call(s32[2]{0:T(128)S(1)} %pad_add_fusion.place_ref, bf16[2048,256]{1,0:T(8,128)(2,1)S(1)} %convolution_convert_fusion.ortho_ref, bf16[2,256,512]{2,1,0:T(8,128)(2,1)S(1)} %pad_maximum_fusion.1.right_ref.refs_2_, f32[2048,1024]{1,0:T(8,128)S(1)} %get-tuple-element.21.total_ref, ...), custom_call_target="tpu_custom_call", output_to_operand_aliasing={{}: (4, {})} | custom-call | tf_op jit(solution)/shard_map/pallas_call | solution.py:253
  150.3 12.0 %shard_map.66 = (bf16[2048,4096]{1,0:T(8,128)(2,1)}, f32[4096,256]{1,0:T(8,128)}) custom-call(s32[8]{0:T(128)S(1)} %concatenate.56.place_ref, bf16[2048,256]{1,0:T(8,128)(2,1)S(1)} %convolution_convert_fusion.ortho_ref, bf16[2,256,512]{2,1,0:T(8,128)(2,1)} %copy-done.1, bf16[4,256,512]{2,1,0:T(8,128)(2,1)} %copy-done, bf16[2,256,512]{2,1,0:T(8,128)(2,1)} %copy-done.2, ...), custom_call_target="tpu_custom_call" | custom-call | tf_op jit(solution)/shard_map/pallas_call | solution.py:298
  (101 shorter events, 25.8 us)
Async XLA Ops:
  21.0 8.8 %collective-permute-start.1 = (bf16[512,256]{0,1:T(8,128)(2,1)S(1)}, bf16[512,256]{0,1:T(8,128)(2,1)S(1)}, u32[]{:S(2)}, u32[]{:S(2)}) collective-permute-start(bf16[512,256]{0,1:T(8,128)(2,1)S(1)} %get-tuple-element.47), channel_id=1, source_target_pairs={{0,8},{8,0},{16,24},{24,16},{1,9},{9,1},{17,25},{25,17},{2,10},{10... | collective-permute-start | bytes 786440 | tf_op jit(solution)/shard_map/ppermute | solution.py:331
  23.5 7.2 %collective-permute-start.3 = (bf16[512,256]{0,1:T(8,128)(2,1)S(1)}, bf16[512,256]{0,1:T(8,128)(2,1)S(1)}, u32[]{:S(2)}, u32[]{:S(2)}) collective-permute-start(bf16[512,256]{0,1:T(8,128)(2,1)S(1)} %get-tuple-element.48), channel_id=1, source_target_pairs={{0,16},{8,24},{16,0},{24,8},{1,17},{9,25},{17,1},{25,9},{2,18},{10... | collective-permute-start | bytes 786440 | tf_op jit(solution)/shard_map/ppermute | solution.py:331
  30.8 6.3 %collective-permute-start.4 = (bf16[512,256]{0,1:T(8,128)(2,1)S(1)}, bf16[512,256]{0,1:T(8,128)(2,1)S(1)}, u32[]{:S(2)}, u32[]{:S(2)}) collective-permute-start(bf16[512,256]{0,1:T(8,128)(2,1)S(1)} %get-tuple-element.46), channel_id=1, source_target_pairs={{0,8},{8,0},{16,24},{24,16},{1,9},{9,1},{17,25},{25,17},{2,10},{10... | collective-permute-start | bytes 786440 | tf_op jit(solution)/shard_map/ppermute | solution.py:331
  31.3 6.3 %collective-permute-start.2 = (bf16[512,256]{0,1:T(8,128)(2,1)S(1)}, bf16[512,256]{0,1:T(8,128)(2,1)S(1)}, u32[]{:S(2)}, u32[]{:S(2)}) collective-permute-start(bf16[512,256]{0,1:T(8,128)(2,1)S(1)} %get-tuple-element.45), channel_id=1, source_target_pairs={{0,16},{8,24},{16,0},{24,8},{1,17},{9,25},{17,1},{25,9},{2,18},{10... | collective-permute-start | bytes 786440 | tf_op jit(solution)/shard_map/ppermute | solution.py:331
  42.3 13.2 %collective-permute-start.7 = (f32[128,256]{1,0:T(8,128)S(1)}, f32[128,256]{1,0:T(8,128)S(1)}, u32[]{:S(2)}, u32[]{:S(2)}) collective-permute-start(f32[128,256]{1,0:T(8,128)S(1)} %constant_dynamic-slice_fusion.2), channel_id=1, source_target_pairs={{0,4},{2,6},{4,0},{6,2},{1,5},{3,7},{5,1},{7,3},{8,12},{10,14},{12... | collective-permute-start | bytes 393224 | tf_op jit(solution)/shard_map/ppermute | solution.py:331
  44.6 10.9 %collective-permute-start.8 = (f32[128,256]{1,0:T(8,128)S(1)}, f32[128,256]{1,0:T(8,128)S(1)}, u32[]{:S(2)}, u32[]{:S(2)}) collective-permute-start(f32[128,256]{1,0:T(8,128)S(1)} %constant_dynamic-slice_fusion.2), channel_id=1, source_target_pairs={{0,6},{2,4},{4,2},{6,0},{1,7},{3,5},{5,3},{7,1},{8,14},{10,12},{12... | collective-permute-start | bytes 393224 | tf_op jit(solution)/shard_map/ppermute | solution.py:331
  45.7 9.8 %collective-permute-start.6 = (f32[128,256]{1,0:T(8,128)S(1)}, f32[128,256]{1,0:T(8,128)S(1)}, u32[]{:S(2)}, u32[]{:S(2)}) collective-permute-start(f32[128,256]{1,0:T(8,128)S(1)} %constant_dynamic-slice_fusion.2), channel_id=1, source_target_pairs={{0,2},{2,0},{4,6},{6,4},{1,3},{3,1},{5,7},{7,5},{8,10},{10,8},{12,... | collective-permute-start | bytes 393224 | tf_op jit(solution)/shard_map/ppermute | solution.py:331
  66.0 13.3 %collective-permute-start.10 = (bf16[256,1024]{1,0:T(8,128)(2,1)S(1)}, bf16[256,1024]{1,0:T(8,128)(2,1)}, u32[]{:S(2)}, u32[]{:S(2)}) collective-permute-start(bf16[256,1024]{1,0:T(8,128)(2,1)S(1)} %get-tuple-element.17), channel_id=1, source_target_pairs={{0,8},{8,0},{16,24},{24,16},{1,9},{9,1},{17,25},{25,17},{2,10},{10... | collective-permute-start | bytes 1572872 | tf_op jit(solution)/shard_map/ppermute | solution.py:331
  67.2 12.9 %collective-permute-start.12 = (bf16[256,1024]{1,0:T(8,128)(2,1)S(1)}, bf16[256,1024]{1,0:T(8,128)(2,1)}, u32[]{:S(2)}, u32[]{:S(2)}) collective-permute-start(bf16[256,1024]{1,0:T(8,128)(2,1)S(1)} %get-tuple-element.18), channel_id=1, source_target_pairs={{0,16},{8,24},{16,0},{24,8},{1,17},{9,25},{17,1},{25,9},{2,18},{10... | collective-permute-start | bytes 1572872 | tf_op jit(solution)/shard_map/ppermute | solution.py:331
  81.7 6.4 %collective-permute-start.13 = (bf16[256,512]{1,0:T(8,128)(2,1)S(1)}, bf16[256,512]{1,0:T(8,128)(2,1)S(1)}, u32[]{:S(2)}, u32[]{:S(2)}) collective-permute-start(bf16[256,512]{1,0:T(8,128)(2,1)S(1)} %dynamic-slice_convert_fusion), channel_id=1, source_target_pairs={{0,8},{8,0},{16,24},{24,16},{1,9},{9,1},{17,25},{25,17},{2,10},{10... | collective-permute-start | bytes 786440 | tf_op jit(solution)/shard_map/ppermute | solution.py:331
  82.2 6.1 %collective-permute-start.11 = (bf16[256,512]{1,0:T(8,128)(2,1)S(1)}, bf16[256,512]{1,0:T(8,128)(2,1)S(1)}, u32[]{:S(2)}, u32[]{:S(2)}) collective-permute-start(bf16[256,512]{1,0:T(8,128)(2,1)S(1)} %dynamic-slice_convert_fusion.1), channel_id=1, source_target_pairs={{0,16},{8,24},{16,0},{24,8},{1,17},{9,25},{17,1},{25,9},{2,18},{10... | collective-permute-start | bytes 786440 | tf_op jit(solution)/shard_map/ppermute | solution.py:331
  88.5 5.8 %collective-permute-start.16 = (bf16[256,256]{1,0:T(8,128)(2,1)S(1)}, bf16[256,256]{1,0:T(8,128)(2,1)S(1)}, u32[]{:S(2)}, u32[]{:S(2)}) collective-permute-start(bf16[256,256]{1,0:T(8,128)(2,1)S(1)} %pad_maximum_fusion.7), channel_id=1, source_target_pairs={{0,6},{2,4},{4,2},{6,0},{1,7},{3,5},{5,3},{7,1},{8,14},{10,12},{12... | collective-permute-start | bytes 393224 | tf_op jit(solution)/shard_map/ppermute | solution.py:331
  91.4 11.6 %collective-permute-start.15 = (bf16[256,256]{1,0:T(8,128)(2,1)S(1)}, bf16[256,256]{1,0:T(8,128)(2,1)S(1)}, u32[]{:S(2)}, u32[]{:S(2)}) collective-permute-start(bf16[256,256]{1,0:T(8,128)(2,1)S(1)} %pad_maximum_fusion.6), channel_id=1, source_target_pairs={{0,4},{2,6},{4,0},{6,2},{1,5},{3,7},{5,1},{7,3},{8,12},{10,14},{12... | collective-permute-start | bytes 393224 | tf_op jit(solution)/shard_map/ppermute | solution.py:331
  92.0 10.9 %collective-permute-start.14 = (bf16[256,256]{1,0:T(8,128)(2,1)S(1)}, bf16[256,256]{1,0:T(8,128)(2,1)S(1)}, u32[]{:S(2)}, u32[]{:S(2)}) collective-permute-start(bf16[256,256]{1,0:T(8,128)(2,1)S(1)} %pad_maximum_fusion.5), channel_id=1, source_target_pairs={{0,2},{2,0},{4,6},{6,4},{1,3},{3,1},{5,7},{7,5},{8,10},{10,8},{12,... | collective-permute-start | bytes 393224 | tf_op jit(solution)/shard_map/ppermute | solution.py:331
  103.0 14.4 %collective-permute-start.17 = (bf16[256,256]{1,0:T(8,128)(2,1)S(1)}, bf16[256,256]{1,0:T(8,128)(2,1)S(1)}, u32[]{:S(2)}, u32[]{:S(2)}) collective-permute-start(bf16[256,256]{1,0:T(8,128)(2,1)S(1)} %fusion.3), channel_id=1, source_target_pairs={{0,6},{2,4},{4,2},{6,0},{1,7},{3,5},{5,3},{7,1},{8,14},{10,12},{12... | collective-permute-start | bytes 393224 | tf_op jit(solution)/shard_map/ppermute | solution.py:331
  106.4 11.0 %collective-permute-start.18 = (bf16[256,256]{1,0:T(8,128)(2,1)S(1)}, bf16[256,256]{1,0:T(8,128)(2,1)S(1)}, u32[]{:S(2)}, u32[]{:S(2)}) collective-permute-start(bf16[256,256]{1,0:T(8,128)(2,1)S(1)} %fusion.3), channel_id=1, source_target_pairs={{0,4},{2,6},{4,0},{6,2},{1,5},{3,7},{5,1},{7,3},{8,12},{10,14},{12... | collective-permute-start | bytes 393224 | tf_op jit(solution)/shard_map/ppermute | solution.py:331
  106.4 11.0 %collective-permute-start.19 = (bf16[256,256]{1,0:T(8,128)(2,1)S(1)}, bf16[256,256]{1,0:T(8,128)(2,1)S(1)}, u32[]{:S(2)}, u32[]{:S(2)}) collective-permute-start(bf16[256,256]{1,0:T(8,128)(2,1)S(1)} %fusion.3), channel_id=1, source_target_pairs={{0,2},{2,0},{4,6},{6,4},{1,3},{3,1},{5,7},{7,5},{8,10},{10,8},{12,... | collective-permute-start | bytes 393224 | tf_op jit(solution)/shard_map/ppermute | solution.py:331
  117.7 12.6 %collective-permute-start.22 = (bf16[256,512]{1,0:T(8,128)(2,1)S(1)}, bf16[256,512]{1,0:T(8,128)(2,1)S(1)}, u32[]{:S(2)}, u32[]{:S(2)}) collective-permute-start(bf16[256,512]{1,0:T(8,128)(2,1)S(1)} %get-tuple-element.28), channel_id=1, source_target_pairs={{0,8},{8,0},{16,24},{24,16},{1,9},{9,1},{17,25},{25,17},{2,10},{10... | collective-permute-start | bytes 786440 | tf_op jit(solution)/shard_map/ppermute | solution.py:331
  119.0 11.4 %collective-permute-start.25 = (bf16[256,512]{1,0:T(8,128)(2,1)S(1)}, bf16[256,512]{1,0:T(8,128)(2,1)S(1)}, u32[]{:S(2)}, u32[]{:S(2)}) collective-permute-start(bf16[256,512]{1,0:T(8,128)(2,1)S(1)} %get-tuple-element.28), channel_id=1, source_target_pairs={{0,16},{8,24},{16,0},{24,8},{1,17},{9,25},{17,1},{25,9},{2,18},{10... | collective-permute-start | bytes 786440 | tf_op jit(solution)/shard_map/ppermute | solution.py:331
  120.3 10.0 %collective-permute-start.20 = (bf16[256,512]{1,0:T(8,128)(2,1)S(1)}, bf16[256,512]{1,0:T(8,128)(2,1)S(1)}, u32[]{:S(2)}, u32[]{:S(2)}) collective-permute-start(bf16[256,512]{1,0:T(8,128)(2,1)S(1)} %get-tuple-element.26), channel_id=1, source_target_pairs={{0,16},{8,24},{16,0},{24,8},{1,17},{9,25},{17,1},{25,9},{2,18},{10... | collective-permute-start | bytes 786440 | tf_op jit(solution)/shard_map/ppermute | solution.py:331
  120.6 9.7 %collective-permute-start.24 = (bf16[256,512]{1,0:T(8,128)(2,1)S(1)}, bf16[256,512]{1,0:T(8,128)(2,1)S(1)}, u32[]{:S(2)}, u32[]{:S(2)}) collective-permute-start(bf16[256,512]{1,0:T(8,128)(2,1)S(1)} %get-tuple-element.26), channel_id=1, source_target_pairs={{0,8},{8,0},{16,24},{24,16},{1,9},{9,1},{17,25},{25,17},{2,10},{10... | collective-permute-start | bytes 786440 | tf_op jit(solution)/shard_map/ppermute | solution.py:331
  130.5 10.4 %collective-permute-start.23 = (bf16[256,512]{1,0:T(8,128)(2,1)S(1)}, bf16[256,512]{1,0:T(8,128)(2,1)S(1)}, u32[]{:S(2)}, u32[]{:S(2)}) collective-permute-start(bf16[256,512]{1,0:T(8,128)(2,1)S(1)} %collective-permute-done.22), channel_id=1, source_target_pairs={{0,16},{8,24},{16,0},{24,8},{1,17},{9,25},{17,1},{25,9},{2,18},{10... | collective-permute-start | bytes 786440 | tf_op jit(solution)/shard_map/ppermute | solution.py:331
  131.8 9.2 %collective-permute-start.21 = (bf16[256,512]{1,0:T(8,128)(2,1)S(1)}, bf16[256,512]{1,0:T(8,128)(2,1)S(1)}, u32[]{:S(2)}, u32[]{:S(2)}) collective-permute-start(bf16[256,512]{1,0:T(8,128)(2,1)S(1)} %collective-permute-done.20), channel_id=1, source_target_pairs={{0,8},{8,0},{16,24},{24,16},{1,9},{9,1},{17,25},{25,17},{2,10},{10... | collective-permute-start | bytes 786440 | tf_op jit(solution)/shard_map/ppermute | solution.py:331
  141.2 8.9 %collective-permute-start.26 = (f32[256,1]{0,1:T(1,128)S(1)}, f32[256,1]{0,1:T(1,128)S(1)}, u32[]{:S(2)}, u32[]{:S(2)}) collective-permute-start(f32[256,1]{0,1:T(1,128)S(1)} %bitcast.42), channel_id=1, source_target_pairs={{0,1},{1,0},{2,3},{3,2},{4,5},{5,4},{6,7},{7,6},{8,9},{9,8},{10,11... | collective-permute-start | bytes 3080 | tf_op jit(solution)/shard_map/ppermute | solution.py:331
  (8 other events, 39.8 us)

commit v7 on v6

--- a/solution.py
+++ b/solution.py
@@ -20,12 +20,15 @@
     out_ref[...] = jnp.zeros_like(out_ref)
     rows = lax.broadcasted_iota(jnp.int32, (panel, LANES), 0)
     lanes = lax.broadcasted_iota(jnp.int32, (panel, LANES), 1)
-    product = functools.partial(
-        lax.dot_general,
-        dimension_numbers=COLS_OVER,
-        precision=lax.Precision.HIGHEST,
-        preferred_element_type=F32,
-    )
+    dot = functools.partial(
+        lax.dot_general, dimension_numbers=COLS_OVER, preferred_element_type=F32
+    )
+
+    def product(x, y):
+        x_high, x_low = split_low(x)
+        y_high, y_low = split_low(y)
+        return (dot(x_high, y_low) + dot(x_low, y_high)) + dot(x_high, y_high)
+
     for start in range(0, n, panel):
         base = start // LANES * LANES
         wide = base + LANES

time: 163 us -> 162 us (level)
  no operation moved by 1% of the time
where the time goes in v7:
time: 162 us
  Pallas kernels  85.7 us (53%)
  starting transfers between devices  33.9 us (21%)
  waiting for transfers between devices  32.3 us (20%)
  other arithmetic  5.6 us (3%)
    ppermute x27, starting transfers between devices, swap(): return lax.ppermute(x, axis, [(i, i ^ mask) for i in range(size)])  33.9 us
    ppermute x27, waiting for transfers between devices, swap(): return lax.ppermute(x, axis, [(i, i ^ mask) for i in range(size)])  32.3 us
    pallas_call x3, Pallas kernels, feedback_columns(): pl.pallas_call(first_kernel if written is None else later_kernel, grid_sp...  20.4 us
    pallas_call x2, Pallas kernels, quarters_product(): pl.pallas_call(body, grid_spec=pltpu.PrefetchScalarGridSpec(num_scalar_pr...  19.6 us
    pallas_call x1, Pallas kernels, left_product(): pl.pallas_call(left_kernel, grid=(rows // tile,), in_specs=[pl.BlockSpec(...  15.7 us
    pallas_call x1, Pallas kernels, step_outputs(): pl.pallas_call(functools.partial(step_kernel, scale, counts), grid_spec=p...  12 us
    pallas_call x1, Pallas kernels, totals_of(): pl.pallas_call(functools.partial(total_kernel, counts), grid_spec=pltpu.P...  10.3 us
    pallas_call x1, Pallas kernels, inverse_and_sent(): pl.pallas_call(sent_kernel, out_shape=(jax.ShapeDtypeStruct((n, n), F32),...  7.83 us
  transfers between devices with their start and end apart: 27, of which 13 were waited for; matrix products, arithmetic and copies ran while one was open for 2% of the time, Pallas kernels for 31%

profile of v7, /device:TPU:1, one launch (start us, length us, event | category | flops | bytes accessed | tf_op | source)
XLA Modules:
  0.0 161.7 jit_solution(16589105161722396226)
XLA Ops:
  0.6 15.7 %shard_map.58 = f32[2048,256]{1,0:T(8,128)S(1)} custom-call(bf16[2048,4096]{1,0:T(8,128)(2,1)} %bitcast.24, bf16[2048,4096]{1,0:T(8,128)(2,1)} %bitcast.29, f32[4096,256]{1,0:T(8,128)} %factor_ref.1), custom_call_target="tpu_custom_call" | custom-call | flops 8589934592 | bytes 33554432 | tf_op jit(solution)/shard_map/pallas_call | solution.py:172
  17.2 2.4 %collective-permute-done = f32[1024,256]{0,1:T(8,128)} collective-permute-done((f32[1024,256]{0,1:T(8,128)S(1)}, f32[1024,256]{0,1:T(8,128)}, u32[]{:S(2)}, u32[]{:S(2)}) %collective-permute-start) | collective-permute-done | bytes 1048608 | tf_op jit(solution)/shard_map/ppermute | solution.py:334
  19.6 1.4 add_convert_fusion
  21.0 2.4 %collective-permute-start.1 = (bf16[512,256]{0,1:T(8,128)(2,1)S(1)}, bf16[512,256]{0,1:T(8,128)(2,1)S(1)}, u32[]{:S(2)}, u32[]{:S(2)}) collective-permute-start(bf16[512,256]{0,1:T(8,128)(2,1)S(1)} %get-tuple-element.47), channel_id=1, source_target_pairs={{0,8},{8,0},{16,24},{24,16},{1,9},{9,1},{17,25},{25,17},{2,10},{10... | collective-permute-start | bytes 786440 | tf_op jit(solution)/shard_map/ppermute | solution.py:334
  24.7 5.1 %collective-permute-done.1 = bf16[512,256]{0,1:T(8,128)(2,1)S(1)} collective-permute-done((bf16[512,256]{0,1:T(8,128)(2,1)S(1)}, bf16[512,256]{0,1:T(8,128)(2,1)S(1)}, u32[]{:S(2)}, u32[]{:S(2)}) %collective-permute-start.1) | collective-permute-done | bytes 262176 | tf_op jit(solution)/shard_map/ppermute | solution.py:334
  32.4 4.7 %collective-permute-done.4 = bf16[512,256]{0,1:T(8,128)(2,1)S(1)} collective-permute-done((bf16[512,256]{0,1:T(8,128)(2,1)S(1)}, bf16[512,256]{0,1:T(8,128)(2,1)S(1)}, u32[]{:S(2)}, u32[]{:S(2)}) %collective-permute-start.4) | collective-permute-done | bytes 262176 | tf_op jit(solution)/shard_map/ppermute | solution.py:334
  37.7 2.5 %collective-permute-start.5 = (bf16[1024,256]{0,1:T(8,128)(2,1)S(1)}, bf16[1024,256]{0,1:T(8,128)(2,1)S(1)}, u32[]{:S(2)}, u32[]{:S(2)}) collective-permute-start(bf16[1024,256]{0,1:T(8,128)(2,1)S(1)} %fusion), channel_id=1, source_target_pairs={{0,1},{1,0},{2,3},{3,2},{4,5},{5,4},{6,7},{7,6},{8,9},{9,8},{10,11... | collective-permute-start | bytes 1572872 | tf_op jit(solution)/shard_map/ppermute | solution.py:334
  40.3 1.5 collective-permute-done.5
  42.3 2.3 %collective-permute-start.7 = (f32[128,256]{1,0:T(8,128)S(1)}, f32[128,256]{1,0:T(8,128)S(1)}, u32[]{:S(2)}, u32[]{:S(2)}) collective-permute-start(f32[128,256]{1,0:T(8,128)S(1)} %constant_dynamic-slice_fusion.2), channel_id=1, source_target_pairs={{0,4},{2,6},{4,0},{6,2},{1,5},{3,7},{5,1},{7,3},{8,12},{10,14},{12... | collective-permute-start | bytes 393224 | tf_op jit(solution)/shard_map/ppermute | solution.py:334
  46.3 9.2 %shard_map.59.mixed_ref = f32[256,2048]{1,0:T(8,128)S(1)} custom-call(s32[2]{0:T(128)S(1)} %get-tuple-element.29.side_ref, bf16[256,2048]{1,0:T(8,128)(2,1)S(1)} %fusion.4.left_ref, bf16[2048,4096]{1,0:T(8,128)(2,1)} %bitcast.25, bf16[2048,4096]{1,0:T(8,128)(2,1)} %bitcast.30), custom_call_target="tpu_custom_call" | custom-call | tf_op jit(solution)/shard_map/pallas_call | solution.py:128
  57.6 7.8 %shard_map.60 = (f32[256,256]{1,0:T(8,128)S(1)}, bf16[256,1024]{1,0:T(8,128)(2,1)S(1)}, bf16[256,1024]{1,0:T(8,128)(2,1)S(1)}) custom-call(f32[256,256]{1,0:T(8,128)S(1)} %maximum_select_fusion.1.gram_ref, f32[256,2048]{1,0:T(8,128)S(1)} %shard_map.59.mixed_ref), custom_call_target="tpu_custom_call" | custom-call | tf_op jit(solution)/shard_map/pallas_call | solution.py:145
  67.9 10.4 %shard_map.61 = f32[256,2048]{1,0:T(8,128)S(1)} custom-call(s32[2]{0:T(128)S(1)} %get-tuple-element.30.side_ref, bf16[256,2048]{1,0:T(8,128)(2,1)S(1)} %fusion.4.left_ref, bf16[2048,4096]{1,0:T(8,128)(2,1)} %bitcast.26, bf16[2048,4096]{1,0:T(8,128)(2,1)} %bitcast.31, f32[256,256]{1,0:T(8,128)S(1)} %get-tuple-element.16.inverse_ref), custom_call_target="tpu_custom_call" | custom-call | tf_op jit(solution)/shard_map/pallas_call | solution.py:128
  79.6 1.5 slice_add_fusion.1
  83.0 4.5 %collective-permute-done.13 = bf16[256,512]{1,0:T(8,128)(2,1)S(1)} collective-permute-done((bf16[256,512]{1,0:T(8,128)(2,1)S(1)}, bf16[256,512]{1,0:T(8,128)(2,1)S(1)}, u32[]{:S(2)}, u32[]{:S(2)}) %collective-permute-start.13) | collective-permute-done | bytes 262176 | tf_op jit(solution)/shard_map/ppermute | solution.py:334
  87.9 2.9 %collective-permute-start.16 = (bf16[256,256]{1,0:T(8,128)(2,1)S(1)}, bf16[256,256]{1,0:T(8,128)(2,1)S(1)}, u32[]{:S(2)}, u32[]{:S(2)}) collective-permute-start(bf16[256,256]{1,0:T(8,128)(2,1)S(1)} %pad_maximum_fusion.7), channel_id=1, source_target_pairs={{0,6},{2,4},{4,2},{6,0},{1,7},{3,5},{5,3},{7,1},{8,14},{10,12},{12... | collective-permute-start | bytes 393224 | tf_op jit(solution)/shard_map/ppermute | solution.py:334
  91.9 1.8 %collective-permute-done.16 = bf16[256,256]{1,0:T(8,128)(2,1)S(1)} collective-permute-done((bf16[256,256]{1,0:T(8,128)(2,1)S(1)}, bf16[256,256]{1,0:T(8,128)(2,1)S(1)}, u32[]{:S(2)}, u32[]{:S(2)}) %collective-permute-start.16) | collective-permute-done | bytes 131104 | tf_op jit(solution)/shard_map/ppermute | solution.py:334
  93.7 8.7 %collective-permute-done.15 = bf16[256,256]{1,0:T(8,128)(2,1)S(1)} collective-permute-done((bf16[256,256]{1,0:T(8,128)(2,1)S(1)}, bf16[256,256]{1,0:T(8,128)(2,1)S(1)}, u32[]{:S(2)}, u32[]{:S(2)}) %collective-permute-start.15) | collective-permute-done | bytes 131104 | tf_op jit(solution)/shard_map/ppermute | solution.py:334
  102.5 3.4 %collective-permute-start.17 = (bf16[256,256]{1,0:T(8,128)(2,1)S(1)}, bf16[256,256]{1,0:T(8,128)(2,1)S(1)}, u32[]{:S(2)}, u32[]{:S(2)}) collective-permute-start(bf16[256,256]{1,0:T(8,128)(2,1)S(1)} %fusion.3), channel_id=1, source_target_pairs={{0,6},{2,4},{4,2},{6,0},{1,7},{3,5},{5,3},{7,1},{8,14},{10,12},{12... | collective-permute-start | bytes 393224 | tf_op jit(solution)/shard_map/ppermute | solution.py:334
  106.6 10.3 %shard_map.62 = (f32[2048,2048]{1,0:T(8,128)S(1)}, f32[2048,1024]{1,0:T(8,128)S(1)}) custom-call(s32[6]{0:T(128)S(1)} %concatenate.55.place_ref, bf16[2048,4096]{1,0:T(8,128)(2,1)} %bitcast.27, bf16[2048,4096]{1,0:T(8,128)(2,1)} %bitcast.32), custom_call_target="tpu_custom_call" | custom-call | tf_op jit(solution)/shard_map/pallas_call | solution.py:212
  121.5 8.3 %shard_map.63.written_ref = f32[1,2048,4096]{2,1,0:T(8,128)} custom-call(s32[2]{0:T(128)S(1)} %pad_add_fusion.3.place_ref, bf16[2048,256]{1,0:T(8,128)(2,1)S(1)} %convolution_convert_fusion.ortho_ref, bf16[2,256,512]{2,1,0:T(8,128)(2,1)S(1)} %pad_maximum_fusion.2.right_ref.refs_0_, bf16[2048,4096]{1,0:T(8,128)(2,1)} %bitcast.28, bf16[2048,4096]{1,0:T(8,128)(2,1)} %bitcast.33), custom_call_target="tpu_custom_call" | custom-call | tf_op jit(solution)/shard_map/pallas_call | solution.py:256
  132.8 7.4 %shard_map.64.written_ref = f32[1,2048,4096]{2,1,0:T(8,128)} custom-call(s32[4]{0:T(128)S(1)} %pad_add_fusion.2.place_ref, bf16[2048,256]{1,0:T(8,128)(2,1)S(1)} %convolution_convert_fusion.ortho_ref, bf16[4,256,512]{2,1,0:T(8,128)(2,1)S(1)} %pad_maximum_fusion.right_ref.refs_1_, ...), custom_call_target="tpu_custom_call", output_to_operand_aliasing={{}: (4, {})} | custom-call | tf_op jit(solution)/shard_map/pallas_call | solution.py:256
  140.7 4.1 %collective-permute-start.26 = (f32[256,1]{0,1:T(1,128)S(1)}, f32[256,1]{0,1:T(1,128)S(1)}, u32[]{:S(2)}, u32[]{:S(2)}) collective-permute-start(f32[256,1]{0,1:T(1,128)S(1)} %bitcast.42), channel_id=1, source_target_pairs={{0,1},{1,0},{2,3},{3,2},{4,5},{5,4},{6,7},{7,6},{8,9},{9,8},{10,11... | collective-permute-start | bytes 3080 | tf_op jit(solution)/shard_map/ppermute | solution.py:334
  144.8 4.7 %shard_map.65 = f32[1,2048,4096]{2,1,0:T(8,128)} custom-call(s32[2]{0:T(128)S(1)} %pad_add_fusion.place_ref, bf16[2048,256]{1,0:T(8,128)(2,1)S(1)} %convolution_convert_fusion.ortho_ref, bf16[2,256,512]{2,1,0:T(8,128)(2,1)S(1)} %pad_maximum_fusion.1.right_ref.refs_2_, f32[2048,1024]{1,0:T(8,128)S(1)} %get-tuple-element.21.total_ref, ...), custom_call_target="tpu_custom_call", output_to_operand_aliasing={{}: (4, {})} | custom-call | tf_op jit(solution)/shard_map/pallas_call | solution.py:256
  149.7 12.0 %shard_map.66 = (bf16[2048,4096]{1,0:T(8,128)(2,1)}, f32[4096,256]{1,0:T(8,128)}) custom-call(s32[8]{0:T(128)S(1)} %concatenate.56.place_ref, bf16[2048,256]{1,0:T(8,128)(2,1)S(1)} %convolution_convert_fusion.ortho_ref, bf16[2,256,512]{2,1,0:T(8,128)(2,1)} %copy-done.1, bf16[4,256,512]{2,1,0:T(8,128)(2,1)} %copy-done, bf16[2,256,512]{2,1,0:T(8,128)(2,1)} %copy-done.2, ...), custom_call_target="tpu_custom_call" | custom-call | tf_op jit(solution)/shard_map/pallas_call | solution.py:301
  (101 shorter events, 25.8 us)
Async XLA Ops:
  21.0 8.8 %collective-permute-start.1 = (bf16[512,256]{0,1:T(8,128)(2,1)S(1)}, bf16[512,256]{0,1:T(8,128)(2,1)S(1)}, u32[]{:S(2)}, u32[]{:S(2)}) collective-permute-start(bf16[512,256]{0,1:T(8,128)(2,1)S(1)} %get-tuple-element.47), channel_id=1, source_target_pairs={{0,8},{8,0},{16,24},{24,16},{1,9},{9,1},{17,25},{25,17},{2,10},{10... | collective-permute-start | bytes 786440 | tf_op jit(solution)/shard_map/ppermute | solution.py:334
  23.5 7.2 %collective-permute-start.3 = (bf16[512,256]{0,1:T(8,128)(2,1)S(1)}, bf16[512,256]{0,1:T(8,128)(2,1)S(1)}, u32[]{:S(2)}, u32[]{:S(2)}) collective-permute-start(bf16[512,256]{0,1:T(8,128)(2,1)S(1)} %get-tuple-element.48), channel_id=1, source_target_pairs={{0,16},{8,24},{16,0},{24,8},{1,17},{9,25},{17,1},{25,9},{2,18},{10... | collective-permute-start | bytes 786440 | tf_op jit(solution)/shard_map/ppermute | solution.py:334
  30.8 6.3 %collective-permute-start.4 = (bf16[512,256]{0,1:T(8,128)(2,1)S(1)}, bf16[512,256]{0,1:T(8,128)(2,1)S(1)}, u32[]{:S(2)}, u32[]{:S(2)}) collective-permute-start(bf16[512,256]{0,1:T(8,128)(2,1)S(1)} %get-tuple-element.46), channel_id=1, source_target_pairs={{0,8},{8,0},{16,24},{24,16},{1,9},{9,1},{17,25},{25,17},{2,10},{10... | collective-permute-start | bytes 786440 | tf_op jit(solution)/shard_map/ppermute | solution.py:334
  31.3 6.3 %collective-permute-start.2 = (bf16[512,256]{0,1:T(8,128)(2,1)S(1)}, bf16[512,256]{0,1:T(8,128)(2,1)S(1)}, u32[]{:S(2)}, u32[]{:S(2)}) collective-permute-start(bf16[512,256]{0,1:T(8,128)(2,1)S(1)} %get-tuple-element.45), channel_id=1, source_target_pairs={{0,16},{8,24},{16,0},{24,8},{1,17},{9,25},{17,1},{25,9},{2,18},{10... | collective-permute-start | bytes 786440 | tf_op jit(solution)/shard_map/ppermute | solution.py:334
  42.3 13.2 %collective-permute-start.7 = (f32[128,256]{1,0:T(8,128)S(1)}, f32[128,256]{1,0:T(8,128)S(1)}, u32[]{:S(2)}, u32[]{:S(2)}) collective-permute-start(f32[128,256]{1,0:T(8,128)S(1)} %constant_dynamic-slice_fusion.2), channel_id=1, source_target_pairs={{0,4},{2,6},{4,0},{6,2},{1,5},{3,7},{5,1},{7,3},{8,12},{10,14},{12... | collective-permute-start | bytes 393224 | tf_op jit(solution)/shard_map/ppermute | solution.py:334
  44.6 10.9 %collective-permute-start.8 = (f32[128,256]{1,0:T(8,128)S(1)}, f32[128,256]{1,0:T(8,128)S(1)}, u32[]{:S(2)}, u32[]{:S(2)}) collective-permute-start(f32[128,256]{1,0:T(8,128)S(1)} %constant_dynamic-slice_fusion.2), channel_id=1, source_target_pairs={{0,6},{2,4},{4,2},{6,0},{1,7},{3,5},{5,3},{7,1},{8,14},{10,12},{12... | collective-permute-start | bytes 393224 | tf_op jit(solution)/shard_map/ppermute | solution.py:334
  45.7 9.8 %collective-permute-start.6 = (f32[128,256]{1,0:T(8,128)S(1)}, f32[128,256]{1,0:T(8,128)S(1)}, u32[]{:S(2)}, u32[]{:S(2)}) collective-permute-start(f32[128,256]{1,0:T(8,128)S(1)} %constant_dynamic-slice_fusion.2), channel_id=1, source_target_pairs={{0,2},{2,0},{4,6},{6,4},{1,3},{3,1},{5,7},{7,5},{8,10},{10,8},{12,... | collective-permute-start | bytes 393224 | tf_op jit(solution)/shard_map/ppermute | solution.py:334
  65.4 13.3 %collective-permute-start.10 = (bf16[256,1024]{1,0:T(8,128)(2,1)S(1)}, bf16[256,1024]{1,0:T(8,128)(2,1)}, u32[]{:S(2)}, u32[]{:S(2)}) collective-permute-start(bf16[256,1024]{1,0:T(8,128)(2,1)S(1)} %get-tuple-element.17), channel_id=1, source_target_pairs={{0,8},{8,0},{16,24},{24,16},{1,9},{9,1},{17,25},{25,17},{2,10},{10... | collective-permute-start | bytes 1572872 | tf_op jit(solution)/shard_map/ppermute | solution.py:334
  66.6 12.9 %collective-permute-start.12 = (bf16[256,1024]{1,0:T(8,128)(2,1)S(1)}, bf16[256,1024]{1,0:T(8,128)(2,1)}, u32[]{:S(2)}, u32[]{:S(2)}) collective-permute-start(bf16[256,1024]{1,0:T(8,128)(2,1)S(1)} %get-tuple-element.18), channel_id=1, source_target_pairs={{0,16},{8,24},{16,0},{24,8},{1,17},{9,25},{17,1},{25,9},{2,18},{10... | collective-permute-start | bytes 1572872 | tf_op jit(solution)/shard_map/ppermute | solution.py:334
  81.2 6.4 %collective-permute-start.13 = (bf16[256,512]{1,0:T(8,128)(2,1)S(1)}, bf16[256,512]{1,0:T(8,128)(2,1)S(1)}, u32[]{:S(2)}, u32[]{:S(2)}) collective-permute-start(bf16[256,512]{1,0:T(8,128)(2,1)S(1)} %dynamic-slice_convert_fusion), channel_id=1, source_target_pairs={{0,8},{8,0},{16,24},{24,16},{1,9},{9,1},{17,25},{25,17},{2,10},{10... | collective-permute-start | bytes 786440 | tf_op jit(solution)/shard_map/ppermute | solution.py:334
  81.7 6.1 %collective-permute-start.11 = (bf16[256,512]{1,0:T(8,128)(2,1)S(1)}, bf16[256,512]{1,0:T(8,128)(2,1)S(1)}, u32[]{:S(2)}, u32[]{:S(2)}) collective-permute-start(bf16[256,512]{1,0:T(8,128)(2,1)S(1)} %dynamic-slice_convert_fusion.1), channel_id=1, source_target_pairs={{0,16},{8,24},{16,0},{24,8},{1,17},{9,25},{17,1},{25,9},{2,18},{10... | collective-permute-start | bytes 786440 | tf_op jit(solution)/shard_map/ppermute | solution.py:334
  87.9 5.8 %collective-permute-start.16 = (bf16[256,256]{1,0:T(8,128)(2,1)S(1)}, bf16[256,256]{1,0:T(8,128)(2,1)S(1)}, u32[]{:S(2)}, u32[]{:S(2)}) collective-permute-start(bf16[256,256]{1,0:T(8,128)(2,1)S(1)} %pad_maximum_fusion.7), channel_id=1, source_target_pairs={{0,6},{2,4},{4,2},{6,0},{1,7},{3,5},{5,3},{7,1},{8,14},{10,12},{12... | collective-permute-start | bytes 393224 | tf_op jit(solution)/shard_map/ppermute | solution.py:334
  90.8 11.6 %collective-permute-start.15 = (bf16[256,256]{1,0:T(8,128)(2,1)S(1)}, bf16[256,256]{1,0:T(8,128)(2,1)S(1)}, u32[]{:S(2)}, u32[]{:S(2)}) collective-permute-start(bf16[256,256]{1,0:T(8,128)(2,1)S(1)} %pad_maximum_fusion.6), channel_id=1, source_target_pairs={{0,4},{2,6},{4,0},{6,2},{1,5},{3,7},{5,1},{7,3},{8,12},{10,14},{12... | collective-permute-start | bytes 393224 | tf_op jit(solution)/shard_map/ppermute | solution.py:334
  91.5 10.9 %collective-permute-start.14 = (bf16[256,256]{1,0:T(8,128)(2,1)S(1)}, bf16[256,256]{1,0:T(8,128)(2,1)S(1)}, u32[]{:S(2)}, u32[]{:S(2)}) collective-permute-start(bf16[256,256]{1,0:T(8,128)(2,1)S(1)} %pad_maximum_fusion.5), channel_id=1, source_target_pairs={{0,2},{2,0},{4,6},{6,4},{1,3},{3,1},{5,7},{7,5},{8,10},{10,8},{12,... | collective-permute-start | bytes 393224 | tf_op jit(solution)/shard_map/ppermute | solution.py:334
  102.5 14.4 %collective-permute-start.17 = (bf16[256,256]{1,0:T(8,128)(2,1)S(1)}, bf16[256,256]{1,0:T(8,128)(2,1)S(1)}, u32[]{:S(2)}, u32[]{:S(2)}) collective-permute-start(bf16[256,256]{1,0:T(8,128)(2,1)S(1)} %fusion.3), channel_id=1, source_target_pairs={{0,6},{2,4},{4,2},{6,0},{1,7},{3,5},{5,3},{7,1},{8,14},{10,12},{12... | collective-permute-start | bytes 393224 | tf_op jit(solution)/shard_map/ppermute | solution.py:334
  105.9 11.0 %collective-permute-start.18 = (bf16[256,256]{1,0:T(8,128)(2,1)S(1)}, bf16[256,256]{1,0:T(8,128)(2,1)S(1)}, u32[]{:S(2)}, u32[]{:S(2)}) collective-permute-start(bf16[256,256]{1,0:T(8,128)(2,1)S(1)} %fusion.3), channel_id=1, source_target_pairs={{0,4},{2,6},{4,0},{6,2},{1,5},{3,7},{5,1},{7,3},{8,12},{10,14},{12... | collective-permute-start | bytes 393224 | tf_op jit(solution)/shard_map/ppermute | solution.py:334
  105.9 11.0 %collective-permute-start.19 = (bf16[256,256]{1,0:T(8,128)(2,1)S(1)}, bf16[256,256]{1,0:T(8,128)(2,1)S(1)}, u32[]{:S(2)}, u32[]{:S(2)}) collective-permute-start(bf16[256,256]{1,0:T(8,128)(2,1)S(1)} %fusion.3), channel_id=1, source_target_pairs={{0,2},{2,0},{4,6},{6,4},{1,3},{3,1},{5,7},{7,5},{8,10},{10,8},{12,... | collective-permute-start | bytes 393224 | tf_op jit(solution)/shard_map/ppermute | solution.py:334
  117.2 12.6 %collective-permute-start.22 = (bf16[256,512]{1,0:T(8,128)(2,1)S(1)}, bf16[256,512]{1,0:T(8,128)(2,1)S(1)}, u32[]{:S(2)}, u32[]{:S(2)}) collective-permute-start(bf16[256,512]{1,0:T(8,128)(2,1)S(1)} %get-tuple-element.28), channel_id=1, source_target_pairs={{0,8},{8,0},{16,24},{24,16},{1,9},{9,1},{17,25},{25,17},{2,10},{10... | collective-permute-start | bytes 786440 | tf_op jit(solution)/shard_map/ppermute | solution.py:334
  118.4 11.4 %collective-permute-start.25 = (bf16[256,512]{1,0:T(8,128)(2,1)S(1)}, bf16[256,512]{1,0:T(8,128)(2,1)S(1)}, u32[]{:S(2)}, u32[]{:S(2)}) collective-permute-start(bf16[256,512]{1,0:T(8,128)(2,1)S(1)} %get-tuple-element.28), channel_id=1, source_target_pairs={{0,16},{8,24},{16,0},{24,8},{1,17},{9,25},{17,1},{25,9},{2,18},{10... | collective-permute-start | bytes 786440 | tf_op jit(solution)/shard_map/ppermute | solution.py:334
  119.8 10.0 %collective-permute-start.20 = (bf16[256,512]{1,0:T(8,128)(2,1)S(1)}, bf16[256,512]{1,0:T(8,128)(2,1)S(1)}, u32[]{:S(2)}, u32[]{:S(2)}) collective-permute-start(bf16[256,512]{1,0:T(8,128)(2,1)S(1)} %get-tuple-element.26), channel_id=1, source_target_pairs={{0,16},{8,24},{16,0},{24,8},{1,17},{9,25},{17,1},{25,9},{2,18},{10... | collective-permute-start | bytes 786440 | tf_op jit(solution)/shard_map/ppermute | solution.py:334
  120.1 9.7 %collective-permute-start.24 = (bf16[256,512]{1,0:T(8,128)(2,1)S(1)}, bf16[256,512]{1,0:T(8,128)(2,1)S(1)}, u32[]{:S(2)}, u32[]{:S(2)}) collective-permute-start(bf16[256,512]{1,0:T(8,128)(2,1)S(1)} %get-tuple-element.26), channel_id=1, source_target_pairs={{0,8},{8,0},{16,24},{24,16},{1,9},{9,1},{17,25},{25,17},{2,10},{10... | collective-permute-start | bytes 786440 | tf_op jit(solution)/shard_map/ppermute | solution.py:334
  130.0 10.4 %collective-permute-start.23 = (bf16[256,512]{1,0:T(8,128)(2,1)S(1)}, bf16[256,512]{1,0:T(8,128)(2,1)S(1)}, u32[]{:S(2)}, u32[]{:S(2)}) collective-permute-start(bf16[256,512]{1,0:T(8,128)(2,1)S(1)} %collective-permute-done.22), channel_id=1, source_target_pairs={{0,16},{8,24},{16,0},{24,8},{1,17},{9,25},{17,1},{25,9},{2,18},{10... | collective-permute-start | bytes 786440 | tf_op jit(solution)/shard_map/ppermute | solution.py:334
  131.2 9.2 %collective-permute-start.21 = (bf16[256,512]{1,0:T(8,128)(2,1)S(1)}, bf16[256,512]{1,0:T(8,128)(2,1)S(1)}, u32[]{:S(2)}, u32[]{:S(2)}) collective-permute-start(bf16[256,512]{1,0:T(8,128)(2,1)S(1)} %collective-permute-done.20), channel_id=1, source_target_pairs={{0,8},{8,0},{16,24},{24,16},{1,9},{9,1},{17,25},{25,17},{2,10},{10... | collective-permute-start | bytes 786440 | tf_op jit(solution)/shard_map/ppermute | solution.py:334
  140.7 8.9 %collective-permute-start.26 = (f32[256,1]{0,1:T(1,128)S(1)}, f32[256,1]{0,1:T(1,128)S(1)}, u32[]{:S(2)}, u32[]{:S(2)}) collective-permute-start(f32[256,1]{0,1:T(1,128)S(1)} %bitcast.42), channel_id=1, source_target_pairs={{0,1},{1,0},{2,3},{3,2},{4,5},{5,4},{6,7},{7,6},{8,9},{9,8},{10,11... | collective-permute-start | bytes 3080 | tf_op jit(solution)/shard_map/ppermute | solution.py:334
  (8 other events, 39.8 us)
